TPU v7x, 32 devices: a whole 2x2x4 slice. The times are simulated.
32 devices in a mesh: ctx: 16 (over z, x, core), head: 2 (over y).
Axes of the slice: x: 2, y: 2, z: 4, core: 2. Of those that a mesh axis runs over, the one named last changes fastest.
Arguments:
- queries: bfloat16 [4096, 4096], P(('ctx', 'head')), may hold values from -6 to 6
- key_rows: bfloat16 [4096, 4096], P(('ctx', 'head')), may hold values from -6 to 6
- value_rows: bfloat16 [4096, 4096], P(('ctx', 'head')), may hold values from -6 to 6
- grad_out: bfloat16 [4096, 4096], P(('ctx', 'head')), may hold values from -6 to 6
Outputs:
- grad_query: bfloat16 [4096, 4096], P(('ctx', 'head'))
- grad_key: bfloat16 [4096, 4096], P(('ctx', 'head'))
- grad_value: bfloat16 [4096, 4096], P(('ctx', 'head'))
All inputs are finite; a program needn't handle non-finite values.
Results may differ from a plain program's by a relative error of at most 0.0021.
Values may be sent and summed in bfloat16 or wider, within the bound.
No kernel may reach another device: no remote copies, remote signals or barrier semaphores. Data moves between devices by JAX's collectives and lax.ppermute only.
A program may use at most 128 MiB of HBM per device.

v0:
```python
import jax
import jax.numpy as jnp
from jax import lax
from jax.sharding import PartitionSpec as P

HEAD_DIM = 128
GROUP = 128


def entering(part, axis, combine, identity, reverse):
    count = lax.axis_size(axis)
    place = lax.axis_index(axis)
    ahead = count - 1 - place if reverse else place
    gathered = lax.all_gather(part, axis)
    state = jnp.zeros_like(part) + jnp.asarray(identity, part.dtype)

    def one(turn, state):
        source = count - 1 - turn if reverse else turn
        return combine(state, lax.dynamic_index_in_dim(gathered, source, 0, False))

    return lax.fori_loop(0, ahead, one, state)


def add_states(earlier, later):
    return jax.tree.map(jnp.add, earlier, later)


def per_device(queries, key_rows, value_rows, grad_out):
    q_all, k_all, v_all, d_all = (
        lax.all_to_all(queries, "head", split_axis=1, concat_axis=0, tiled=True),
        lax.all_to_all(key_rows, "head", split_axis=1, concat_axis=0, tiled=True),
        lax.all_to_all(value_rows, "head", split_axis=1, concat_axis=0, tiled=True),
        lax.all_to_all(grad_out, "head", split_axis=1, concat_axis=0, tiled=True),
    )
    rows_here = q_all.shape[0]
    heads_here = q_all.shape[1] // HEAD_DIM
    scale = (HEAD_DIM * rows_here * lax.axis_size("ctx")) ** (-0.5)
    highest = lax.Precision.HIGHEST
    block = GROUP
    nblocks = rows_here // block
    shape_four = (nblocks, block, heads_here, HEAD_DIM)
    q_four = q_all.reshape(shape_four)
    k_four = k_all.reshape(shape_four)
    v_four = v_all.reshape(shape_four)
    d_four = d_all.reshape(shape_four)
    kv_blocks = jnp.einsum("ntha,nthb->nhab", v_four, k_four, preferred_element_type=jnp.float32)
    g_blocks = jnp.einsum("ntha,nthb->nhab", d_four, q_four, preferred_element_type=jnp.float32)
    kv_local = jnp.sum(kv_blocks, axis=0)
    g_local = jnp.sum(g_blocks, axis=0)
    zeros_state = jnp.zeros_like(kv_local)
    kv_before = entering(kv_local, "ctx", add_states, zeros_state, False)
    g_after = entering(g_local, "ctx", add_states, zeros_state, True)
    row_ids = lax.broadcasted_iota(jnp.int32, (nblocks, nblocks), 0)
    col_ids = lax.broadcasted_iota(jnp.int32, (nblocks, nblocks), 1)
    strict_lower = (col_ids < row_ids).astype(jnp.float32)
    strict_upper = (col_ids > row_ids).astype(jnp.float32)
    kv_in = kv_before[None] + jnp.einsum(
        "mn,nhab->mhab", strict_lower, kv_blocks, precision=highest
    )
    g_in = g_after[None] + jnp.einsum("mn,nhab->mhab", strict_upper, g_blocks, precision=highest)
    later = lax.broadcasted_iota(jnp.int32, (block, block), 0)
    earlier = lax.broadcasted_iota(jnp.int32, (block, block), 1)
    causal = (later >= earlier).astype(jnp.float32)
    scores = (
        jnp.einsum("nthd,nshd->nhts", q_four, k_four, preferred_element_type=jnp.float32)
        * (scale * causal)
    ).astype(jnp.bfloat16)
    dscores = (
        jnp.einsum("nthd,nshd->nhts", d_four, v_four, preferred_element_type=jnp.float32) * causal
    ).astype(jnp.bfloat16)
    k_float = k_four.astype(jnp.float32)
    v_float = v_four.astype(jnp.float32)
    d_float = d_four.astype(jnp.float32)
    grad_q = scale * (
        jnp.einsum("nhts,nshd->nthd", dscores, k_four, preferred_element_type=jnp.float32)
        + jnp.einsum("ntha,nhab->nthb", d_float, kv_in, precision=highest)
    )
    grad_k = scale * (
        jnp.einsum("nhts,nthd->nshd", dscores, q_four, preferred_element_type=jnp.float32)
        + jnp.einsum("ntha,nhab->nthb", v_float, g_in, precision=highest)
    )
    grad_v = jnp.einsum(
        "nhts,nthd->nshd", scores, d_four, preferred_element_type=jnp.float32
    ) + scale * jnp.einsum("nthb,nhab->ntha", k_float, g_in, precision=highest)
    flat_shape = (rows_here, heads_here * HEAD_DIM)
    grad_q = grad_q.reshape(flat_shape).astype(jnp.bfloat16)
    grad_k = grad_k.reshape(flat_shape).astype(jnp.bfloat16)
    grad_v = grad_v.reshape(flat_shape).astype(jnp.bfloat16)
    result_q, result_k, result_v = (
        lax.all_to_all(grad_q, "head", split_axis=0, concat_axis=1, tiled=True),
        lax.all_to_all(grad_k, "head", split_axis=0, concat_axis=1, tiled=True),
        lax.all_to_all(grad_v, "head", split_axis=0, concat_axis=1, tiled=True),
    )
    return (result_q, result_k, result_v)


def solution(mesh):
    placed = (
        P(("ctx", "head"), None),
        P(("ctx", "head"), None),
        P(("ctx", "head"), None),
        P(("ctx", "head"), None),
    )
    return jax.shard_map(
        per_device,
        mesh=mesh,
        in_specs=placed,
        out_specs=(P(("ctx", "head"), None), P(("ctx", "head"), None), P(("ctx", "head"), None)),
        check_vma=False,
    )
```

profile of v0, /device:TPU:0, one launch (start us, length us, event | category | flops | bytes accessed | tf_op | source)
XLA Modules:
  0.0 376.4 jit_solution(10768845672230715887)
XLA Ops:
  7.2 2.4 copy.41
  9.5 4.2 %all-to-all-start.1 = ((bf16[128,2,2048]{0,2,1:T(8,128)(2,1)}), bf16[128,2,2048]{0,2,1:T(8,128)(2,1)S(1)}, u32[]{:S(2)}, u32[]{:S(2)}) async-start(bf16[128,2,2048]{0,2,1:T(8,128)(2,1)} %bitcast.5), calls=%async_computation.1 | async-start | bytes 2097152 | tf_op jit(solution)/shard_map/all_to_all | solution.py:32
  14.4 13.8 %all-to-all-done.1 = bf16[128,2,2048]{0,2,1:T(8,128)(2,1)S(1)} async-done(((bf16[128,2,2048]{0,2,1:T(8,128)(2,1)}), bf16[128,2,2048]{0,2,1:T(8,128)(2,1)S(1)}, u32[]{:S(2)}, u32[]{:S(2)}) %all-to-all-start.1) | async-done | bytes 1048608 | tf_op jit(solution)/shard_map/all_to_all | solution.py:32
  28.2 15.8 %all_to_all.112 = bf16[128,2,2048]{0,2,1:T(8,128)(2,1)S(1)} all-to-all(bf16[128,2,2048]{0,2,1:T(8,128)(2,1)S(1)} %bitcast.104), channel_id=1, replica_groups=mesh['ctx'=16,'head'=2] {'head'}, dimensions={1} | all-to-all | bytes 2097152 | tf_op jit(solution)/shard_map/all_to_all | solution.py:31
  44.0 3.3 fusion.32
  48.6 3.6 all-to-all-start
  52.2 2.3 copy.74
  54.5 10.0 %all-to-all-done = bf16[128,2,2048]{0,2,1:T(8,128)(2,1)S(1)} async-done(((bf16[128,2,2048]{0,2,1:T(8,128)(2,1)}), bf16[128,2,2048]{0,2,1:T(8,128)(2,1)S(1)}, u32[]{:S(2)}, u32[]{:S(2)}) %all-to-all-start) | async-done | bytes 1048608 | tf_op jit(solution)/shard_map/all_to_all | solution.py:33
  64.5 15.1 %all_to_all.113 = bf16[128,2,2048]{0,2,1:T(8,128)(2,1)S(1)} all-to-all(bf16[128,2,2048]{0,2,1:T(8,128)(2,1)} %bitcast.105), channel_id=1, replica_groups=mesh['ctx'=16,'head'=2] {'head'}, dimensions={1} | all-to-all | bytes 2097152 | tf_op jit(solution)/shard_map/all_to_all | solution.py:30
  79.7 3.2 fusion.33
  82.9 1.5 multiply_convert_fusion.1
  84.4 90.1 %all-gather.5.cloned.1.call-done = f32[256,128,128]{2,1,0:T(8,128)} async-done(((f32[16,128,128]{2,1,0:T(8,128)}), f32[256,128,128]{2,1,0:T(8,128)}) %all-gather.5.cloned.1.call-update) | async-done | bytes 16777232 | tf_op jit(solution)/shard_map/all_gather | solution.py:14
  174.6 6.9 %fusion.15 = f32[2,16,128,128]{3,0,2,1:T(2,128)S(1)} fusion(f32[2,16,128,128]{3,2,1,0:T(8,128)} %get-tuple-element.101, f32[16,128,128]{2,1,0:T(8,128)S(1)} %get-tuple-element.82), kind=kOutput, calls=%fused_computation.22 | convolution fusion | flops 13107204 | bytes 5242880 | tf_op jit(solution)/shard_map/mn,nhab->mhab/dot_general | solution.py:57
  181.5 1.9 fusion.5
  183.4 1.8 fusion.4
  185.2 4.4 %all-to-all-start.3 = ((bf16[2,128,2048]{1,2,0:T(8,128)(2,1)}), bf16[2,128,2048]{1,2,0:T(8,128)(2,1)}, u32[]{:S(2)}, u32[]{:S(2)}) async-start(bf16[2,128,2048]{1,2,0:T(8,128)(2,1)} %bitcast.19), calls=%async_computation.3 | async-start | bytes 2097152 | tf_op jit(solution)/shard_map/all_to_all | solution.py:90
  189.7 112.1 %all-gather.7.cloned.1.call-done = f32[256,128,128]{2,1,0:T(8,128)} async-done(((f32[16,128,128]{2,1,0:T(8,128)}), f32[256,128,128]{2,1,0:T(8,128)}) %all-gather.7.cloned.1.call-update) | async-done | bytes 16777232 | tf_op jit(solution)/shard_map/all_gather | solution.py:14
  301.9 22.9 %while.23 = (s32[]{:T(128)}, f32[16,128,128]{2,1,0:T(8,128)S(1)}, s32[]{:T(128)}, f32[16,16,128,128]{3,2,1,0:T(8,128)}, s32[]{:T(128)}, /*index=5*/s32[]{:T(128)}, s32[]{:T(128)}, s32[]{:T(128)}) while((s32[]{:T(128)}, f32[16,128,128]{2,1,0:T(8,128)S(1)}, s32[]{:T(128)}, f32[16,16,128,128]{3,2,1,0:T(8,128)}, s32[]{:T(128)}, ...), condition=%wide.region_5.6_spmd, body=%wide.region_4.5_spmd.sunk | while | flops 262150 | bytes 3145871 | solution.py:21
  302.1 1.5 bitcast_add_fusion.8
  303.6 1.5 bitcast_add_fusion.8
  305.1 1.5 bitcast_add_fusion.8
  312.6 1.5 bitcast_add_fusion.8
  324.7 7.0 %fusion.18 = f32[2,16,128,128]{3,0,2,1:T(2,128)S(1)} fusion(f32[2,16,128,128]{3,2,1,0:T(8,128)} %get-tuple-element.103, f32[16,128,128]{2,1,0:T(8,128)S(1)} %get-tuple-element.83), kind=kOutput, calls=%fused_computation.23 | convolution fusion | flops 13107204 | bytes 5242880 | tf_op jit(solution)/shard_map/mn,nhab->mhab/dot_general | solution.py:60
  331.8 1.8 fusion.11
  335.5 4.4 %all-to-all-start.5 = ((bf16[2,128,2048]{1,2,0:T(8,128)(2,1)}), bf16[2,128,2048]{1,2,0:T(8,128)(2,1)}, u32[]{:S(2)}, u32[]{:S(2)}) async-start(bf16[2,128,2048]{1,2,0:T(8,128)(2,1)} %bitcast.100), calls=%async_computation.5 | async-start | bytes 2097152 | tf_op jit(solution)/shard_map/all_to_all | solution.py:91
  340.0 4.0 %fusion.13 = f32[2,16,128,128]{3,2,1,0:T(8,128)} fusion(bf16[2,128,16,128]{1,3,2,0:T(8,128)(2,1)S(1)} %bitcast.88, f32[2,16,128,128]{3,0,2,1:T(2,128)} %copy-done), kind=kOutput, calls=%fused_computation.20 | convolution fusion | flops 805306368 | bytes 5242880 | tf_op jit(solution)/shard_map/nthb,nhab->ntha/dot_general | solution.py:84
  343.9 3.4 fusion
  347.3 5.5 %all-to-all-done.5 = bf16[2,128,2048]{1,2,0:T(8,128)(2,1)} async-done(((bf16[2,128,2048]{1,2,0:T(8,128)(2,1)}), bf16[2,128,2048]{1,2,0:T(8,128)(2,1)}, u32[]{:S(2)}, u32[]{:S(2)}) %all-to-all-start.5) | async-done | bytes 1048608 | tf_op jit(solution)/shard_map/all_to_all | solution.py:91
  352.8 3.6 all-to-all-start.6
  356.4 2.3 copy.73
  358.7 2.3 copy.75
  360.9 7.3 %all-to-all-done.6 = bf16[2,128,2048]{1,2,0:T(8,128)(2,1)S(1)} async-done(((bf16[2,128,2048]{1,2,0:T(8,128)(2,1)}), bf16[2,128,2048]{1,2,0:T(8,128)(2,1)S(1)}, u32[]{:S(2)}, u32[]{:S(2)}) %all-to-all-start.6) | async-done | bytes 1048608 | tf_op jit(solution)/shard_map/all_to_all | solution.py:92
  (43 shorter events, 21.9 us)
Async XLA Ops:
  7.2 6.6 %copy-start.7 = (bf16[128,4096]{1,0:T(8,128)(2,1)S(1)}, bf16[128,4096]{1,0:T(8,128)(2,1)}, u32[]{:S(2)}) copy-start(bf16[128,4096]{1,0:T(8,128)(2,1)} %param.9) | copy-start | bytes 3145732
  9.5 18.7 %all-to-all-start.1 = ((bf16[128,2,2048]{0,2,1:T(8,128)(2,1)}), bf16[128,2,2048]{0,2,1:T(8,128)(2,1)S(1)}, u32[]{:S(2)}, u32[]{:S(2)}) async-start(bf16[128,2,2048]{0,2,1:T(8,128)(2,1)} %bitcast.5), calls=%async_computation.1 | async-start | bytes 2097152 | tf_op jit(solution)/shard_map/all_to_all | solution.py:32
  13.8 160.7 %all-gather.5.cloned.1.call-start = ((), (), s32[]{:S(2)}) async-start(), calls=%async_computation.7 | async-start | bytes 17825792 | tf_op jit(solution)/shard_map/all_gather | solution.py:14
  28.2 54.7 %copy-start.1 = (bf16[128,2,2048]{0,2,1:T(8,128)(2,1)}, bf16[128,2,2048]{0,2,1:T(8,128)(2,1)S(1)}, u32[]{:S(2)}) copy-start(bf16[128,2,2048]{0,2,1:T(8,128)(2,1)S(1)} %all-to-all-done.1) | copy-start | bytes 3145732
  44.0 3.3 copy-start.8
  48.6 16.0 %all-to-all-start = ((bf16[128,2,2048]{0,2,1:T(8,128)(2,1)}), bf16[128,2,2048]{0,2,1:T(8,128)(2,1)S(1)}, u32[]{:S(2)}, u32[]{:S(2)}) async-start(bf16[128,2,2048]{0,2,1:T(8,128)(2,1)} %bitcast.103), calls=%async_computation | async-start | bytes 2097152 | tf_op jit(solution)/shard_map/all_to_all | solution.py:33
  52.2 249.6 %all-gather.7.cloned.1.call-start = ((), (), s32[]{:S(2)}) async-start(), calls=%async_computation.8 | async-start | bytes 17825792 | tf_op jit(solution)/shard_map/all_gather | solution.py:14
  79.7 3.2 copy-start.3
  181.5 1.9 copy-start.5
  185.2 150.3 %all-to-all-start.3 = ((bf16[2,128,2048]{1,2,0:T(8,128)(2,1)}), bf16[2,128,2048]{1,2,0:T(8,128)(2,1)}, u32[]{:S(2)}, u32[]{:S(2)}) async-start(bf16[2,128,2048]{1,2,0:T(8,128)(2,1)} %bitcast.19), calls=%async_computation.3 | async-start | bytes 2097152 | tf_op jit(solution)/shard_map/all_to_all | solution.py:90
  324.7 7.0 %copy-start.2 = (bf16[128,2,2048]{0,2,1:T(8,128)(2,1)S(1)}, bf16[128,2,2048]{0,2,1:T(8,128)(2,1)}, u32[]{:S(2)}) copy-start(bf16[128,2,2048]{0,2,1:T(8,128)(2,1)} %copy-done.1) | copy-start | bytes 3145732
  331.7 1.8 copy-start
  331.7 2.0 copy-start.4
  331.7 2.3 copy-start.6
  335.5 17.3 %all-to-all-start.5 = ((bf16[2,128,2048]{1,2,0:T(8,128)(2,1)}), bf16[2,128,2048]{1,2,0:T(8,128)(2,1)}, u32[]{:S(2)}, u32[]{:S(2)}) async-start(bf16[2,128,2048]{1,2,0:T(8,128)(2,1)} %bitcast.100), calls=%async_computation.5 | async-start | bytes 2097152 | tf_op jit(solution)/shard_map/all_to_all | solution.py:91
  352.8 15.4 %all-to-all-start.6 = ((bf16[2,128,2048]{1,2,0:T(8,128)(2,1)}), bf16[2,128,2048]{1,2,0:T(8,128)(2,1)S(1)}, u32[]{:S(2)}, u32[]{:S(2)}) async-start(bf16[2,128,2048]{1,2,0:T(8,128)(2,1)} %bitcast.101), calls=%async_computation.6 | async-start | bytes 2097152 | tf_op jit(solution)/shard_map/all_to_all | solution.py:92
Sparse Core Ops, SparseCore 0:
  47.4 127.0 all-gather.4
  176.7 125.0 all-gather.6
where the time goes:
time: 378 us; the launch traced here: 376 us
  waiting for transfers between devices  239 us (63%)
  matrix products  36.2 us (10%)
  blocking collectives  30.9 us (8%)
  other arithmetic  22.3 us (6%)
  starting transfers between devices  20.3 us (5%)
  between operations  14.2 us (4%)
  local copies, waits for them, and re-layouts  13.1 us (3%)
    all_gather x2, waiting for transfers between devices, entering(): gathered = lax.all_gather(part, axis)  202 us
    add x15, other arithmetic, add_states(): return jax.tree.map(jnp.add, earlier, later)  22.3 us
    all_to_all x1, blocking collectives, per_device(): lax.all_to_all(key_rows, 'head', split_axis=1, concat_axis=0, tiled=True)  15.8 us
    all_to_all x1, blocking collectives, per_device(): lax.all_to_all(queries, 'head', split_axis=1, concat_axis=0, tiled=True)  15.1 us
    all_to_all x1, waiting for transfers between devices, per_device(): lax.all_to_all(value_rows, 'head', split_axis=1, concat_axis=0, tiled=True)  13.8 us
    all_to_all x1, waiting for transfers between devices, per_device(): lax.all_to_all(grad_out, 'head', split_axis=1, concat_axis=0, tiled=True)  10 us
  transfers between devices with their start and end apart: 7, of which 6 were waited for; matrix products, arithmetic and copies ran while one was open for 17% of the time, Pallas kernels for 0%

commit v1 on v0

v1 whole, which is shorter than its diff:
```python
import functools

import jax
import jax.numpy as jnp
from jax import lax
from jax.experimental import pallas as pl
from jax.experimental.pallas import tpu as pltpu
from jax.sharding import PartitionSpec as P

HEAD_DIM = 128
GROUP = 128
AXES = ("ctx", "head")
F32 = jnp.float32
BF16 = jnp.bfloat16
HALF = jnp.float16
TAIL = 16
TOP = 15.0


def dot(a, b, dims):
    return lax.dot_general(a, b, (dims, ((), ())), preferred_element_type=F32)


def state_kernel(order, q0, k0, v0, d0, q1, k1, v1, d1, mine, sent, most):
    step = pl.program_id(0)

    @pl.when(step == 0)
    def _():
        most[...] = jnp.zeros_like(most)

    for refs, out in (((q0, k0, v0, d0), mine), ((q1, k1, v1, d1), sent)):
        q, k, v, d = refs
        for head in range(q.shape[1] // HEAD_DIM):
            cols = slice(head * HEAD_DIM, (head + 1) * HEAD_DIM)
            for kind, (left, right) in enumerate(((v, k), (d, q))):
                state = dot(left[:, cols], right[:, cols], ((0,), (0,)))
                out[0, kind, cols, :] = state
                peak = jnp.max(jnp.abs(state).reshape(HEAD_DIM // 8, 8, HEAD_DIM), axis=0)
                rows = slice(kind * 8, kind * 8 + 8)
                most[rows, :] = jnp.maximum(most[rows, :], peak)

    @pl.when(step == pl.num_programs(0) - 1)
    def _():
        for kind in range(2):
            rows = slice(kind * 8, kind * 8 + 8)
            most[rows, :] = jnp.full((8, HEAD_DIM), jnp.max(most[rows, :]), F32)


def states(order, arrays, width):
    rows = arrays[0].shape[0]
    specs = [pl.BlockSpec((rows, width), lambda i, o: (0, o[i]))] * 4
    specs += [pl.BlockSpec((rows, width), lambda i, o: (0, o[i + 4]))] * 4
    block = pl.BlockSpec((1, 2, width, HEAD_DIM), lambda i, o: (i, 0, 0, 0))
    shape = jax.ShapeDtypeStruct((4, 2, width, HEAD_DIM), F32)
    return pl.pallas_call(
        state_kernel,
        grid_spec=pltpu.PrefetchScalarGridSpec(
            num_scalar_prefetch=1,
            grid=(4,),
            in_specs=specs,
            out_specs=(block, block, pl.BlockSpec((16, HEAD_DIM), lambda i, o: (0, 0))),
        ),
        out_shape=(shape, shape, jax.ShapeDtypeStruct((16, HEAD_DIM), F32)),
        cost_estimate=pl.CostEstimate(
            flops=32 * rows * width * HEAD_DIM, bytes_accessed=24 * rows * width * 8, transcendentals=0
        ),
        name="group_states",
    )(order, *arrays, *arrays)


def gradient_kernel(scale, order, q, k, v, d, state, *rest):
    gq, gk, gv = rest[-3:]
    rows = q.shape[0]
    later = lax.broadcasted_iota(jnp.int32, (rows, rows), 0)
    earlier = lax.broadcasted_iota(jnp.int32, (rows, rows), 1)
    causal = later >= earlier
    nn, nt, tn = ((1,), (0,)), ((1,), (1,)), ((0,), (0,))
    for head in range(q.shape[1] // HEAD_DIM):
        cols = slice(head * HEAD_DIM, (head + 1) * HEAD_DIM)
        qh, kh, vh, dh = q[:, cols], k[:, cols], v[:, cols], d[:, cols]
        scores = jnp.where(causal, dot(qh, kh, nt) * scale, 0.0).astype(BF16)
        dscores = jnp.where(causal, dot(dh, vh, nt), 0.0).astype(BF16)
        kv, g = state[0, 0, cols, :], state[0, 1, cols, :]
        kv_hi, g_hi = kv.astype(BF16), g.astype(BF16)
        kv_lo = (kv - kv_hi.astype(F32)).astype(BF16)
        g_lo = (g - g_hi.astype(F32)).astype(BF16)
        out_q = dot(dscores, kh, nn) + (dot(dh, kv_hi, nn) + dot(dh, kv_lo, nn))
        out_k = dot(dscores, qh, tn) + (dot(vh, g_hi, nn) + dot(vh, g_lo, nn))
        out_v = dot(scores, dh, tn) + scale * (dot(kh, g_hi, nt) + dot(kh, g_lo, nt))
        gq[:, cols] = (out_q * scale).astype(BF16)
        gk[:, cols] = (out_k * scale).astype(BF16)
        gv[:, cols] = out_v.astype(BF16)


def gradients(order, arrays, state, scale, width, before):
    rows, columns = arrays[0].shape
    block = pl.BlockSpec((rows, width), lambda i, o: (0, o[i]))
    shape = jax.ShapeDtypeStruct((rows, columns), BF16)
    extra = () if before is None else tuple(before)
    return pl.pallas_call(
        functools.partial(gradient_kernel, scale),
        grid_spec=pltpu.PrefetchScalarGridSpec(
            num_scalar_prefetch=1,
            grid=(4,),
            in_specs=[block] * 4
            + [pl.BlockSpec((1, 2, width, HEAD_DIM), lambda i, o: (i, 0, 0, 0))]
            + [pl.BlockSpec(memory_space=pl.ANY)] * len(extra),
            out_specs=(block,) * 3,
        ),
        out_shape=(shape,) * 3,
        input_output_aliases={6 + i: i for i in range(len(extra))},
        cost_estimate=pl.CostEstimate(
            flops=88 * rows * width * HEAD_DIM, bytes_accessed=88 * rows * width, transcendentals=0
        ),
        name="group_gradients",
    )(order, *arrays, state, *extra)


def exponents(bound):
    return jnp.clip(jnp.ceil(jnp.log2(jnp.maximum(bound, 1e-30))) + 1.0, -100.0, 60.0)


def per_kind(rows):
    return rows.reshape(2, 8, HEAD_DIM)[:, :1, :]


def encode(parts, exps):
    factor = jnp.exp2(TOP - exps)
    factor = per_kind(factor)
    flat = [(part * factor[: part.shape[0]]).reshape(-1, HEAD_DIM) for part in parts]
    return jnp.concatenate(flat + [exps], axis=0).astype(HALF)


def exponents_of(message):
    return message[-TAIL:].astype(F32)


def decode(rows, exps, kinds):
    factor = per_kind(jnp.exp2(exps - TOP))
    return rows.reshape(kinds, -1, HEAD_DIM).astype(F32) * factor[:kinds]


def whole_groups(queries, key_rows, value_rows, grad_out):
    arrays = (queries, key_rows, value_rows, grad_out)
    rows = queries.shape[0]
    heads = queries.shape[1] // HEAD_DIM
    n_ctx, n_head = lax.axis_size("ctx"), lax.axis_size("head")
    devices = n_ctx * n_head
    place = lax.axis_index("ctx") * n_head + lax.axis_index("head")
    scale = (HEAD_DIM * rows * devices) ** (-0.5)
    outer = (devices // 8).bit_length() - 1
    per = heads // 8

    def move(x, mask):
        return lax.ppermute(x, AXES, [(p, p ^ mask) for p in range(devices)])

    bit = [((place >> b) & 1).astype(F32) for b in range(3 + outer)]

    def weight(b):
        return jnp.stack([bit[b], 1.0 - bit[b]]).reshape(2, 1, 1)

    masks = [4 * (r >> 1) + (r & 1) for r in range(4)]
    handled = place % 8
    order_heads = jnp.stack([(handled ^ m) * per for m in masks] + [(handled ^ m ^ 2) * per for m in masks])

    chunks = [(0, per // 2), (per // 2, per // 2)]
    done = None
    work = []
    for first, count in chunks:
        width = count * HEAD_DIM
        order = ((order_heads + first) // count).astype(jnp.int32)
        with jax.named_scope("states"):
            mine, sent, most = states(order, arrays, width)
        with jax.named_scope("core_exchange"):
            peer = move(sent, 2)
            peer_most = move(most, 2)
            exps = exponents(jnp.maximum(most, peer_most))
        with jax.named_scope("up"):
            got = [None] * 4
            for r in (1, 2, 3):
                got[r] = move(encode([mine[r], peer[r]], exps), masks[r])
            blocks = {(0, 0): mine[0], (1, 0): peer[0]}
            bound = 2.0 * jnp.exp2(exps)
            for r in (1, 2, 3):
                e = exponents_of(got[r])
                bound = bound + 2.0 * jnp.exp2(e)
                halves = got[r][:-TAIL].reshape(2, 2, width, HEAD_DIM)
                for c in (0, 1):
                    blocks[c, r] = decode(halves[c], e, 2)
            total = functools.reduce(jnp.add, blocks.values())
        with jax.named_scope("outer"):
            entering = jnp.zeros_like(total)
            running, running_bound = total, bound
            entering_bound = jnp.zeros_like(bound)
            for b in range(outer):
                mask = ((2 << b) - 1) << 3
                w = weight(3 + b)
                w_rows = jnp.repeat(w.reshape(2, 1), 8, axis=0)
                e = exponents(running_bound)
                if b < outer - 1:
                    reply = move(encode([running], e), mask)
                    e = exponents_of(reply)
                    other = decode(reply[:-TAIL], e, 2)
                    entering = entering + w * other
                    running = running + other
                    running_bound = running_bound + jnp.exp2(e)
                else:
                    up = bit[3 + b] > 0.5
                    payload = jnp.where(up, running[1], running[0])
                    e = jnp.tile(jnp.where(up, e[8:], e[:8]), (2, 1))
                    reply = move(encode([payload[None]], e), mask)
                    e = exponents_of(reply)
                    other = decode(reply[:-TAIL], e, 1)
                    entering = entering + w * other
                entering_bound = entering_bound + jnp.exp2(e)
        with jax.named_scope("down"):
            before = {}
            level = blocks
            wy, wc, wx = weight(0), weight(1), weight(2)
            pair = {(c, x): blocks[c, 2 * x] + blocks[c, 2 * x + 1] for c in (0, 1) for x in (0, 1)}
            quad = {x: pair[0, x] + pair[1, x] for x in (0, 1)}
            for c in (0, 1):
                for x in (0, 1):
                    for y in (0, 1):
                        near = blocks[c, 2 * x + 1 - y] * (wy if y == 0 else 1.0 - wy)
                        mid = pair[1 - c, x] * (wc if c == 0 else 1.0 - wc)
                        far = quad[1 - x] * (wx if x == 0 else 1.0 - wx)
                        before[c, 2 * x + y] = entering + near + mid + far
            e = exponents(entering_bound + bound)
            back = [None] * 4
            for r in (1, 2, 3):
                back[r] = move(encode([before[0, r], before[1, r]], e), masks[r])
            own_exps = e
        with jax.named_scope("core_return"):
            each = 2 * width
            parts = [encode([before[1, 0]], own_exps)]
            for r in (1, 2, 3):
                parts += [back[r][each : 2 * each], back[r][-TAIL:]]
            forward = move(jnp.concatenate(parts, axis=0), 2)
        with jax.named_scope("gradients"):
            near = [before[0, 0]]
            for r in (1, 2, 3):
                near.append(decode(back[r][:each], exponents_of(back[r]), 2))
            done = gradients(order[:4], arrays, jnp.stack(near), scale, width, done)
            pieces = forward.reshape(4, each + TAIL, HEAD_DIM)
            far = [decode(pieces[r, :each], exponents_of(pieces[r]), 2) for r in range(4)]
            done = gradients(order[4:], arrays, jnp.stack(far), scale, width, done)
    return tuple(done)


def entering(part, axis, reverse):
    count = lax.axis_size(axis)
    place = lax.axis_index(axis)
    ahead = count - 1 - place if reverse else place
    gathered = lax.all_gather(part, axis)

    def one(turn, state):
        source = count - 1 - turn if reverse else turn
        return state + lax.dynamic_index_in_dim(gathered, source, 0, False)

    return lax.fori_loop(0, ahead, one, jnp.zeros_like(part))


def split_groups(queries, key_rows, value_rows, grad_out):
    q_all, k_all, v_all, d_all = (
        lax.all_to_all(a, "head", split_axis=1, concat_axis=0, tiled=True)
        for a in (queries, key_rows, value_rows, grad_out)
    )
    rows_here = q_all.shape[0]
    heads_here = q_all.shape[1] // HEAD_DIM
    scale = (HEAD_DIM * rows_here * lax.axis_size("ctx")) ** (-0.5)
    highest = lax.Precision.HIGHEST
    block = GROUP
    nblocks = rows_here // block
    shape_four = (nblocks, block, heads_here, HEAD_DIM)
    q_four = q_all.reshape(shape_four)
    k_four = k_all.reshape(shape_four)
    v_four = v_all.reshape(shape_four)
    d_four = d_all.reshape(shape_four)
    kv_blocks = jnp.einsum("ntha,nthb->nhab", v_four, k_four, preferred_element_type=F32)
    g_blocks = jnp.einsum("ntha,nthb->nhab", d_four, q_four, preferred_element_type=F32)
    kv_before = entering(jnp.sum(kv_blocks, axis=0), "ctx", False)
    g_after = entering(jnp.sum(g_blocks, axis=0), "ctx", True)
    row_ids = lax.broadcasted_iota(jnp.int32, (nblocks, nblocks), 0)
    col_ids = lax.broadcasted_iota(jnp.int32, (nblocks, nblocks), 1)
    strict_lower = (col_ids < row_ids).astype(F32)
    strict_upper = (col_ids > row_ids).astype(F32)
    kv_in = kv_before[None] + jnp.einsum("mn,nhab->mhab", strict_lower, kv_blocks, precision=highest)
    g_in = g_after[None] + jnp.einsum("mn,nhab->mhab", strict_upper, g_blocks, precision=highest)
    later = lax.broadcasted_iota(jnp.int32, (block, block), 0)
    earlier = lax.broadcasted_iota(jnp.int32, (block, block), 1)
    causal = (later >= earlier).astype(F32)
    scores = (
        jnp.einsum("nthd,nshd->nhts", q_four, k_four, preferred_element_type=F32) * (scale * causal)
    ).astype(BF16)
    dscores = (jnp.einsum("nthd,nshd->nhts", d_four, v_four, preferred_element_type=F32) * causal).astype(BF16)
    k_float, v_float, d_float = (a.astype(F32) for a in (k_four, v_four, d_four))
    grad_q = scale * (
        jnp.einsum("nhts,nshd->nthd", dscores, k_four, preferred_element_type=F32)
        + jnp.einsum("ntha,nhab->nthb", d_float, kv_in, precision=highest)
    )
    grad_k = scale * (
        jnp.einsum("nhts,nthd->nshd", dscores, q_four, preferred_element_type=F32)
        + jnp.einsum("ntha,nhab->nthb", v_float, g_in, precision=highest)
    )
    grad_v = jnp.einsum(
        "nhts,nthd->nshd", scores, d_four, preferred_element_type=F32
    ) + scale * jnp.einsum("nthb,nhab->ntha", k_float, g_in, precision=highest)
    flat_shape = (rows_here, heads_here * HEAD_DIM)
    return tuple(
        lax.all_to_all(
            a.reshape(flat_shape).astype(BF16), "head", split_axis=0, concat_axis=1, tiled=True
        )
        for a in (grad_q, grad_k, grad_v)
    )


def per_device(*arrays):
    rows, columns = arrays[0].shape
    devices = lax.axis_size("ctx") * lax.axis_size("head")
    whole = rows == GROUP and lax.axis_size("head") == 2 and devices >= 16 and devices & (devices - 1) == 0
    if whole and columns % (16 * HEAD_DIM) == 0:
        return whole_groups(*arrays)
    return split_groups(*arrays)


def solution(mesh):
    placed = P(AXES, None)
    return jax.shard_map(
        per_device, mesh=mesh, in_specs=(placed,) * 4, out_specs=(placed,) * 3, check_vma=False
    )
```

time: 378 us -> 118 us (0.31)
  waiting for transfers between devices: 239 us -> 22.8 us
  matrix products: 36.2 us -> 0 us
  Pallas kernels: 0 us -> 33 us
  blocking collectives: 30.9 us -> 0 us
  between operations: 14.2 us -> 1.65 us
  starting transfers between devices: 20.3 us -> 31.5 us
  other arithmetic: 22.3 us -> 15.5 us
    all_gather x2 -> x0, waiting for transfers between devices: 202 us -> none  [entering(): gathered = lax.all_gather(part, axis)]
    all_to_all x5 -> x0, waiting for transfers between devices: 36.6 us -> none  [the longest x1 13.8 us: per_device(): lax.all_to_all(value_rows, 'head', split_axis=1, concat_axis=0, tiled=True)]
    dot_general x11 -> x0, matrix products: 36.2 us -> none  [the longest x1 6.98 us: per_device(): jnp.einsum('mn,nhab->mhab', strict_upper, g_blocks, precision=highest)]
    pallas_call x0 -> x6, Pallas kernels: none -> 33 us  [the longest x4 22.8 us: gradients(): pl.pallas_call(functools.partial(gradient_kernel, scale), grid_spec=pltpu...]
    ppermute x0 -> x22, starting transfers between devices: none -> 31.5 us  [move(): return lax.ppermute(x, AXES, [(p, p ^ mask) for p in range(devices)])]
    all_to_all x2 -> x0, blocking collectives: 30.9 us -> none  [the longest x1 15.8 us: per_device(): lax.all_to_all(key_rows, 'head', split_axis=1, concat_axis=0, tiled=True)]
    ppermute x0 -> x22, waiting for transfers between devices: none -> 22.8 us  [move(): return lax.ppermute(x, AXES, [(p, p ^ mask) for p in range(devices)])]
    all_to_all x5 -> x0, starting transfers between devices: 20.2 us -> none  [the longest x1 4.43 us: per_device(): lax.all_to_all(grad_q, 'head', split_axis=0, concat_axis=1, tiled=True)]
  transfers between devices with their start and end apart: 7 -> 22, of which waited for: 6 -> 10; matrix products, arithmetic and copies ran while one was open for 17% -> 17% of each run, Pallas kernels for 0% -> 9%
where the time goes in v1:
time: 118 us; the launch traced here: 117 us
  Pallas kernels  33 us (28%)
  starting transfers between devices  31.5 us (27%)
  waiting for transfers between devices  22.8 us (19%)
  other arithmetic  15.5 us (13%)
  local copies, waits for them, and re-layouts  12.8 us (11%)
  between operations  1.65 us (1%)
    ppermute x22, starting transfers between devices, move(): return lax.ppermute(x, AXES, [(p, p ^ mask) for p in range(devices)])  31.5 us
    ppermute x22, waiting for transfers between devices, move(): return lax.ppermute(x, AXES, [(p, p ^ mask) for p in range(devices)])  22.8 us
    pallas_call x4, Pallas kernels, gradients(): pl.pallas_call(functools.partial(gradient_kernel, scale), grid_spec=pltpu...  22.8 us
    pallas_call x2, Pallas kernels, states(): pl.pallas_call(state_kernel, grid_spec=pltpu.PrefetchScalarGridSpec(num_s...  10.2 us
    unnamed x45, local copies, waits for them, and re-layouts  5.35 us
    another operation x16, other arithmetic  4.87 us
    slice x32, local copies, waits for them, and re-layouts, per_kind(): return rows.reshape(2, 8, HEAD_DIM)[:, :1, :]  2.75 us
  transfers between devices with their start and end apart: 22, of which 10 were waited for; matrix products, arithmetic and copies ran while one was open for 17% of the time, Pallas kernels for 9%

profile of v1, /device:TPU:0, one launch (start us, length us, event | category | flops | bytes accessed | tf_op | source)
XLA Modules:
  0.0 117.2 jit_solution(8574572592004358716)
XLA Ops:
  1.3 5.1 %group_states.3 = (f32[4,2,256,128]{3,2,1,0:T(8,128)}, f32[4,2,256,128]{3,2,1,0:T(8,128)}, f32[16,128]{1,0:T(8,128)}) custom-call(s32[8]{0:T(128)} %get-tuple-element.155.order, bf16[128,4096]{1,0:T(8,128)(2,1)} %q.7, bf16[128,4096]{1,0:T(8,128)(2,1)} %k.7, bf16[128,4096]{1,0:T(8,128)(2,1)} %v.7, bf16[128,4096]{1,0:T(8,128)(2,1)} %d.7, bf16[128,4096]{1,0:T(8,128)(2,1)} %q.7, ...), custom_call_target="tpu_custom_call" | custom-call | flops 134217728 | bytes 6291456 | tf_op jit(solution)/shard_map/states/group_states/pallas_call | solution.py:55
  7.0 5.2 %group_states.2 = (f32[4,2,256,128]{3,2,1,0:T(8,128)}, f32[4,2,256,128]{3,2,1,0:T(8,128)}, f32[16,128]{1,0:T(8,128)}) custom-call(s32[8]{0:T(128)} %get-tuple-element.156.order, bf16[128,4096]{1,0:T(8,128)(2,1)} %q.7, bf16[128,4096]{1,0:T(8,128)(2,1)} %k.7, bf16[128,4096]{1,0:T(8,128)(2,1)} %v.7, bf16[128,4096]{1,0:T(8,128)(2,1)} %d.7, bf16[128,4096]{1,0:T(8,128)(2,1)} %q.7, ...), custom_call_target="tpu_custom_call" | custom-call | flops 134217728 | bytes 6291456 | tf_op jit(solution)/shard_map/states/group_states/pallas_call | solution.py:55
  15.5 1.3 %fusion.170 = (f32[1,2,256,128]{3,2,1,0:T(8,128)S(1)}, f32[1,2,256,128]{3,2,1,0:T(8,128)S(1)}, f32[1,2,256,128]{3,2,1,0:T(8,128)S(1)}, f32[1,2,256,128]{3,2,1,0:T(8,128)S(1)}) fusion(f32[4,2,256,128]{3,2,1,0:T(8,128)} %get-tuple-element.18), kind=kLoop, calls=%fused_computation.368 | loop fusion | bytes 2097152 | tf_op jit(solution)/shard_map/up/slice | solution.py:181
  19.7 3.0 %collective-permute-start.13 = (f16[1040,128]{1,0:T(8,128)(2,1)S(1)}, f16[1040,128]{1,0:T(8,128)(2,1)S(1)}, u32[]{:S(2)}, u32[]{:S(2)}) collective-permute-start(f16[1040,128]{1,0:T(8,128)(2,1)S(1)} %get-tuple-element.132), channel_id=1, source_target_pairs={{0,1},{1,0},{2,3},{3,2},{4,5},{5,4},{6,7},{7,6},{8,9},{9,8},{10,11... | collective-permute-start | bytes 798728 | tf_op jit(solution)/shard_map/up/ppermute | solution.py:155
  22.7 1.5 %collective-permute-start.14 = (f16[1040,128]{1,0:T(8,128)(2,1)S(1)}, f16[1040,128]{1,0:T(8,128)(2,1)S(1)}, u32[]{:S(2)}, u32[]{:S(2)}) collective-permute-start(f16[1040,128]{1,0:T(8,128)(2,1)S(1)} %get-tuple-element.133), channel_id=1, source_target_pairs={{0,4},{1,5},{2,6},{3,7},{4,0},{5,1},{6,2},{7,3},{8,12},{9,13},{10,... | collective-permute-start | bytes 798728 | tf_op jit(solution)/shard_map/up/ppermute | solution.py:155
  24.8 2.0 %collective-permute-start.2 = (f16[1040,128]{1,0:T(8,128)(2,1)S(1)}, f16[1040,128]{1,0:T(8,128)(2,1)S(1)}, u32[]{:S(2)}, u32[]{:S(2)}) collective-permute-start(f16[1040,128]{1,0:T(8,128)(2,1)S(1)} %get-tuple-element.138), channel_id=1, source_target_pairs={{0,1},{1,0},{2,3},{3,2},{4,5},{5,4},{6,7},{7,6},{8,9},{9,8},{10,11... | collective-permute-start | bytes 798728 | tf_op jit(solution)/shard_map/up/ppermute | solution.py:155
  26.8 1.5 %collective-permute-start.3 = (f16[1040,128]{1,0:T(8,128)(2,1)S(1)}, f16[1040,128]{1,0:T(8,128)(2,1)S(1)}, u32[]{:S(2)}, u32[]{:S(2)}) collective-permute-start(f16[1040,128]{1,0:T(8,128)(2,1)S(1)} %get-tuple-element.139), channel_id=1, source_target_pairs={{0,4},{1,5},{2,6},{3,7},{4,0},{5,1},{6,2},{7,3},{8,12},{9,13},{10,... | collective-permute-start | bytes 798728 | tf_op jit(solution)/shard_map/up/ppermute | solution.py:155
  28.3 1.8 %collective-permute-done.13 = f16[1040,128]{1,0:T(8,128)(2,1)S(1)} collective-permute-done((f16[1040,128]{1,0:T(8,128)(2,1)S(1)}, f16[1040,128]{1,0:T(8,128)(2,1)S(1)}, u32[]{:S(2)}, u32[]{:S(2)}) %collective-permute-start.13) | collective-permute-done | bytes 266272 | tf_op jit(solution)/shard_map/up/ppermute | solution.py:155
  30.1 3.7 %collective-permute-start.4 = (f16[1040,128]{1,0:T(8,128)(2,1)S(1)}, f16[1040,128]{1,0:T(8,128)(2,1)S(1)}, u32[]{:S(2)}, u32[]{:S(2)}) collective-permute-start(f16[1040,128]{1,0:T(8,128)(2,1)S(1)} %get-tuple-element.140), channel_id=1, source_target_pairs={{0,5},{1,4},{2,7},{3,6},{4,1},{5,0},{6,3},{7,2},{8,13},{9,12},{10,... | collective-permute-start | bytes 798728 | tf_op jit(solution)/shard_map/up/ppermute | solution.py:155
  33.8 3.5 %collective-permute-done.15 = f16[1040,128]{1,0:T(8,128)(2,1)S(1)} collective-permute-done((f16[1040,128]{1,0:T(8,128)(2,1)S(1)}, f16[1040,128]{1,0:T(8,128)(2,1)S(1)}, u32[]{:S(2)}, u32[]{:S(2)}) %collective-permute-start.15) | collective-permute-done | bytes 266272 | tf_op jit(solution)/shard_map/up/ppermute | solution.py:155
  37.6 2.1 %collective-permute-start.16 = (f16[528,128]{1,0:T(8,128)(2,1)S(1)}, f16[528,128]{1,0:T(8,128)(2,1)S(1)}, u32[]{:S(2)}, u32[]{:S(2)}) collective-permute-start(f16[528,128]{1,0:T(8,128)(2,1)S(1)} %pad_maximum_fusion.17), channel_id=1, source_target_pairs={{0,8},{1,9},{2,10},{3,11},{4,12},{5,13},{6,14},{7,15},{8,0},{9,1},... | collective-permute-start | bytes 405512 | tf_op jit(solution)/shard_map/outer/ppermute | solution.py:155
  40.8 2.7 %collective-permute-done.3 = f16[1040,128]{1,0:T(8,128)(2,1)S(1)} collective-permute-done((f16[1040,128]{1,0:T(8,128)(2,1)S(1)}, f16[1040,128]{1,0:T(8,128)(2,1)S(1)}, u32[]{:S(2)}, u32[]{:S(2)}) %collective-permute-start.3) | collective-permute-done | bytes 266272 | tf_op jit(solution)/shard_map/up/ppermute | solution.py:155
  43.5 4.3 %collective-permute-done.4 = f16[1040,128]{1,0:T(8,128)(2,1)S(1)} collective-permute-done((f16[1040,128]{1,0:T(8,128)(2,1)S(1)}, f16[1040,128]{1,0:T(8,128)(2,1)S(1)}, u32[]{:S(2)}, u32[]{:S(2)}) %collective-permute-start.4) | collective-permute-done | bytes 266272 | tf_op jit(solution)/shard_map/up/ppermute | solution.py:155
  48.2 1.8 %collective-permute-start.5 = (f16[528,128]{1,0:T(8,128)(2,1)S(1)}, f16[528,128]{1,0:T(8,128)(2,1)S(1)}, u32[]{:S(2)}, u32[]{:S(2)}) collective-permute-start(f16[528,128]{1,0:T(8,128)(2,1)S(1)} %pad_maximum_fusion.16), channel_id=1, source_target_pairs={{0,8},{1,9},{2,10},{3,11},{4,12},{5,13},{6,14},{7,15},{8,0},{9,1},... | collective-permute-start | bytes 405512 | tf_op jit(solution)/shard_map/outer/ppermute | solution.py:155
  50.3 1.1 fusion.32
  51.5 2.5 %collective-permute-start.17 = (f16[272,128]{1,0:T(8,128)(2,1)S(1)}, f16[272,128]{1,0:T(8,128)(2,1)S(1)}, u32[]{:S(2)}, u32[]{:S(2)}) collective-permute-start(f16[272,128]{1,0:T(8,128)(2,1)S(1)} %pad_maximum_fusion.19), channel_id=1, source_target_pairs={{0,24},{1,25},{2,26},{3,27},{4,28},{5,29},{6,30},{7,31},{8,16},{9,... | collective-permute-start | bytes 208904 | tf_op jit(solution)/shard_map/outer/ppermute | solution.py:155
  54.2 1.1 fusion.53
  55.4 3.0 %collective-permute-start.6 = (f16[272,128]{1,0:T(8,128)(2,1)S(1)}, f16[272,128]{1,0:T(8,128)(2,1)S(1)}, u32[]{:S(2)}, u32[]{:S(2)}) collective-permute-start(f16[272,128]{1,0:T(8,128)(2,1)S(1)} %pad_maximum_fusion.18), channel_id=1, source_target_pairs={{0,24},{1,25},{2,26},{3,27},{4,28},{5,29},{6,30},{7,31},{8,16},{9,... | collective-permute-start | bytes 208904 | tf_op jit(solution)/shard_map/outer/ppermute | solution.py:155
  62.1 1.6 %collective-permute-start.18 = (f16[1040,128]{1,0:T(8,128)(2,1)S(1)}, f16[1040,128]{1,0:T(8,128)(2,1)S(1)}, u32[]{:S(2)}, u32[]{:S(2)}) collective-permute-start(f16[1040,128]{1,0:T(8,128)(2,1)S(1)} %get-tuple-element.131), channel_id=1, source_target_pairs={{0,1},{1,0},{2,3},{3,2},{4,5},{5,4},{6,7},{7,6},{8,9},{9,8},{10,11... | collective-permute-start | bytes 798728 | tf_op jit(solution)/shard_map/down/ppermute | solution.py:155
  63.7 1.5 %collective-permute-start.19 = (f16[1040,128]{1,0:T(8,128)(2,1)S(1)}, f16[1040,128]{1,0:T(8,128)(2,1)S(1)}, u32[]{:S(2)}, u32[]{:S(2)}) collective-permute-start(f16[1040,128]{1,0:T(8,128)(2,1)S(1)} %get-tuple-element.130), channel_id=1, source_target_pairs={{0,4},{1,5},{2,6},{3,7},{4,0},{5,1},{6,2},{7,3},{8,12},{9,13},{10,... | collective-permute-start | bytes 798728 | tf_op jit(solution)/shard_map/down/ppermute | solution.py:155
  68.1 1.6 %collective-permute-start.7 = (f16[1040,128]{1,0:T(8,128)(2,1)S(1)}, f16[1040,128]{1,0:T(8,128)(2,1)S(1)}, u32[]{:S(2)}, u32[]{:S(2)}) collective-permute-start(f16[1040,128]{1,0:T(8,128)(2,1)S(1)} %get-tuple-element.137), channel_id=1, source_target_pairs={{0,1},{1,0},{2,3},{3,2},{4,5},{5,4},{6,7},{7,6},{8,9},{9,8},{10,11... | collective-permute-start | bytes 798728 | tf_op jit(solution)/shard_map/down/ppermute | solution.py:155
  69.7 1.5 %collective-permute-start.8 = (f16[1040,128]{1,0:T(8,128)(2,1)S(1)}, f16[1040,128]{1,0:T(8,128)(2,1)S(1)}, u32[]{:S(2)}, u32[]{:S(2)}) collective-permute-start(f16[1040,128]{1,0:T(8,128)(2,1)S(1)} %get-tuple-element.136), channel_id=1, source_target_pairs={{0,4},{1,5},{2,6},{3,7},{4,0},{5,1},{6,2},{7,3},{8,12},{9,13},{10,... | collective-permute-start | bytes 798728 | tf_op jit(solution)/shard_map/down/ppermute | solution.py:155
  71.7 2.3 %collective-permute-done.18 = f16[1040,128]{1,0:T(8,128)(2,1)S(1)} collective-permute-done((f16[1040,128]{1,0:T(8,128)(2,1)S(1)}, f16[1040,128]{1,0:T(8,128)(2,1)S(1)}, u32[]{:S(2)}, u32[]{:S(2)}) %collective-permute-start.18) | collective-permute-done | bytes 266272 | tf_op jit(solution)/shard_map/down/ppermute | solution.py:155
  74.0 2.4 %collective-permute-start.9 = (f16[1040,128]{1,0:T(8,128)(2,1)S(1)}, f16[1040,128]{1,0:T(8,128)(2,1)S(1)}, u32[]{:S(2)}, u32[]{:S(2)}) collective-permute-start(f16[1040,128]{1,0:T(8,128)(2,1)S(1)} %get-tuple-element.135), channel_id=1, source_target_pairs={{0,5},{1,4},{2,7},{3,6},{4,1},{5,0},{6,3},{7,2},{8,13},{9,12},{10,... | collective-permute-start | bytes 798728 | tf_op jit(solution)/shard_map/down/ppermute | solution.py:155
  80.0 2.8 %collective-permute-done.7 = f16[1040,128]{1,0:T(8,128)(2,1)S(1)} collective-permute-done((f16[1040,128]{1,0:T(8,128)(2,1)S(1)}, f16[1040,128]{1,0:T(8,128)(2,1)S(1)}, u32[]{:S(2)}, u32[]{:S(2)}) %collective-permute-start.7) | collective-permute-done | bytes 266272 | tf_op jit(solution)/shard_map/down/ppermute | solution.py:155
  83.6 2.8 %collective-permute-done.9 = f16[1040,128]{1,0:T(8,128)(2,1)S(1)} collective-permute-done((f16[1040,128]{1,0:T(8,128)(2,1)S(1)}, f16[1040,128]{1,0:T(8,128)(2,1)S(1)}, u32[]{:S(2)}, u32[]{:S(2)}) %collective-permute-start.9) | collective-permute-done | bytes 266272 | tf_op jit(solution)/shard_map/down/ppermute | solution.py:155
  89.6 1.1 pad_maximum_fusion.3.state
  91.8 5.8 %group_gradients.4 = (bf16[128,4096]{1,0:T(8,128)(2,1)}, bf16[128,4096]{1,0:T(8,128)(2,1)}, bf16[128,4096]{1,0:T(8,128)(2,1)}) custom-call(s32[4]{0:T(128)} %get-tuple-element.153.order, bf16[128,4096]{1,0:T(8,128)(2,1)} %q.7, bf16[128,4096]{1,0:T(8,128)(2,1)} %k.7, bf16[128,4096]{1,0:T(8,128)(2,1)} %v.7, bf16[128,4096]{1,0:T(8,128)(2,1)} %d.7, ...), custom_call_target="tpu_custom_call" | custom-call | flops 369098752 | bytes 2883584 | tf_op jit(solution)/shard_map/gradients/group_gradients/pallas_call | solution.py:100
  99.2 1.1 pad_maximum_fusion.state
  100.3 5.7 %group_gradients.5 = (bf16[128,4096]{1,0:T(8,128)(2,1)}, bf16[128,4096]{1,0:T(8,128)(2,1)}, bf16[128,4096]{1,0:T(8,128)(2,1)}) custom-call(s32[4]{0:T(128)} %get-tuple-element.154.order, bf16[128,4096]{1,0:T(8,128)(2,1)} %q.7, bf16[128,4096]{1,0:T(8,128)(2,1)} %k.7, bf16[128,4096]{1,0:T(8,128)(2,1)} %v.7, ...), custom_call_target="tpu_custom_call", output_to_operand_aliasing={{0}: (6, {}), {1}: (7, {}), {2}: (8, {})} | custom-call | flops 369098752 | bytes 2883584 | tf_op jit(solution)/shard_map/gradients/group_gradients/pallas_call | solution.py:100
  105.9 5.7 %group_gradients.6 = (bf16[128,4096]{1,0:T(8,128)(2,1)}, bf16[128,4096]{1,0:T(8,128)(2,1)}, bf16[128,4096]{1,0:T(8,128)(2,1)}) custom-call(s32[4]{0:T(128)} %get-tuple-element.157.order, bf16[128,4096]{1,0:T(8,128)(2,1)} %q.7, bf16[128,4096]{1,0:T(8,128)(2,1)} %k.7, bf16[128,4096]{1,0:T(8,128)(2,1)} %v.7, ...), custom_call_target="tpu_custom_call", output_to_operand_aliasing={{0}: (6, {}), {1}: (7, {}), {2}: (8, {})} | custom-call | flops 369098752 | bytes 2883584 | tf_op jit(solution)/shard_map/gradients/group_gradients/pallas_call | solution.py:100
  111.6 5.7 %group_gradients.7 = (bf16[128,4096]{1,0:T(8,128)(2,1)}, bf16[128,4096]{1,0:T(8,128)(2,1)}, bf16[128,4096]{1,0:T(8,128)(2,1)}) custom-call(s32[4]{0:T(128)} %get-tuple-element.158.order, bf16[128,4096]{1,0:T(8,128)(2,1)} %q.7, bf16[128,4096]{1,0:T(8,128)(2,1)} %k.7, bf16[128,4096]{1,0:T(8,128)(2,1)} %v.7, ...), custom_call_target="tpu_custom_call", output_to_operand_aliasing={{0}: (6, {}), {1}: (7, {}), {2}: (8, {})} | custom-call | flops 369098752 | bytes 2883584 | tf_op jit(solution)/shard_map/gradients/group_gradients/pallas_call | solution.py:100
  (202 shorter events, 27.1 us)
Async XLA Ops:
  6.4 11.1 %collective-permute-start.12 = (f32[16,128]{1,0:T(8,128)}, f32[16,128]{1,0:T(8,128)S(1)}, u32[]{:S(2)}, u32[]{:S(2)}) collective-permute-start(f32[16,128]{1,0:T(8,128)} %get-tuple-element.23), channel_id=1, source_target_pairs={{0,2},{1,3},{2,0},{3,1},{4,6},{5,7},{6,4},{7,5},{8,10},{9,11},{10,... | collective-permute-start | bytes 24584 | tf_op jit(solution)/shard_map/core_exchange/ppermute | solution.py:155
  6.9 11.3 %collective-permute-start.11 = (f32[4,2,256,128]{3,2,1,0:T(8,128)}, f32[4,2,256,128]{3,2,1,0:T(8,128)S(1)}, u32[]{:S(2)}, u32[]{:S(2)}) collective-permute-start(f32[4,2,256,128]{3,2,1,0:T(8,128)} %get-tuple-element.22), channel_id=1, source_target_pairs={{0,2},{1,3},{2,0},{3,1},{4,6},{5,7},{6,4},{7,5},{8,10},{9,11},{10,... | collective-permute-start | bytes 3145736 | tf_op jit(solution)/shard_map/core_exchange/ppermute | solution.py:155
  7.0 5.8 %copy-start = (f32[4,2,256,128]{3,2,1,0:T(8,128)S(1)}, f32[4,2,256,128]{3,2,1,0:T(8,128)}, u32[]{:S(2)}) copy-start(f32[4,2,256,128]{3,2,1,0:T(8,128)} %get-tuple-element.21) | copy-start | bytes 3145732
  12.2 6.0 %collective-permute-start.1 = (f32[16,128]{1,0:T(8,128)}, f32[16,128]{1,0:T(8,128)S(1)}, u32[]{:S(2)}, u32[]{:S(2)}) collective-permute-start(f32[16,128]{1,0:T(8,128)} %get-tuple-element.20), channel_id=1, source_target_pairs={{0,2},{1,3},{2,0},{3,1},{4,6},{5,7},{6,4},{7,5},{8,10},{9,11},{10,... | collective-permute-start | bytes 24584 | tf_op jit(solution)/shard_map/core_exchange/ppermute | solution.py:155
  12.7 11.6 %collective-permute-start = (f32[4,2,256,128]{3,2,1,0:T(8,128)}, f32[4,2,256,128]{3,2,1,0:T(8,128)S(1)}, u32[]{:S(2)}, u32[]{:S(2)}) collective-permute-start(f32[4,2,256,128]{3,2,1,0:T(8,128)} %get-tuple-element.19), channel_id=1, source_target_pairs={{0,2},{1,3},{2,0},{3,1},{4,6},{5,7},{6,4},{7,5},{8,10},{9,11},{10,... | collective-permute-start | bytes 3145736 | tf_op jit(solution)/shard_map/core_exchange/ppermute | solution.py:155
  15.5 1.3 %copy-start.11 = (s32[8]{0:T(128)S(1)}, s32[8]{0:T(128)}, u32[]{:S(2)}) copy-start(s32[8]{0:T(128)} %get-tuple-element.156.order) | copy-start | bytes 100
  17.4 0.7 copy-start.5
  18.2 1.0 copy-start.1
  18.2 1.0 copy-start.2
  18.2 1.1 copy-start.3
  19.7 10.4 %collective-permute-start.13 = (f16[1040,128]{1,0:T(8,128)(2,1)S(1)}, f16[1040,128]{1,0:T(8,128)(2,1)S(1)}, u32[]{:S(2)}, u32[]{:S(2)}) collective-permute-start(f16[1040,128]{1,0:T(8,128)(2,1)S(1)} %get-tuple-element.132), channel_id=1, source_target_pairs={{0,1},{1,0},{2,3},{3,2},{4,5},{5,4},{6,7},{7,6},{8,9},{9,8},{10,11... | collective-permute-start | bytes 798728 | tf_op jit(solution)/shard_map/up/ppermute | solution.py:155
  22.7 11.1 %collective-permute-start.14 = (f16[1040,128]{1,0:T(8,128)(2,1)S(1)}, f16[1040,128]{1,0:T(8,128)(2,1)S(1)}, u32[]{:S(2)}, u32[]{:S(2)}) collective-permute-start(f16[1040,128]{1,0:T(8,128)(2,1)S(1)} %get-tuple-element.133), channel_id=1, source_target_pairs={{0,4},{1,5},{2,6},{3,7},{4,0},{5,1},{6,2},{7,3},{8,12},{9,13},{10,... | collective-permute-start | bytes 798728 | tf_op jit(solution)/shard_map/up/ppermute | solution.py:155
  24.2 13.0 %collective-permute-start.15 = (f16[1040,128]{1,0:T(8,128)(2,1)S(1)}, f16[1040,128]{1,0:T(8,128)(2,1)S(1)}, u32[]{:S(2)}, u32[]{:S(2)}) collective-permute-start(f16[1040,128]{1,0:T(8,128)(2,1)S(1)} %get-tuple-element.134), channel_id=1, source_target_pairs={{0,5},{1,4},{2,7},{3,6},{4,1},{5,0},{6,3},{7,2},{8,13},{9,12},{10,... | collective-permute-start | bytes 798728 | tf_op jit(solution)/shard_map/up/ppermute | solution.py:155
  24.8 16.0 %collective-permute-start.2 = (f16[1040,128]{1,0:T(8,128)(2,1)S(1)}, f16[1040,128]{1,0:T(8,128)(2,1)S(1)}, u32[]{:S(2)}, u32[]{:S(2)}) collective-permute-start(f16[1040,128]{1,0:T(8,128)(2,1)S(1)} %get-tuple-element.138), channel_id=1, source_target_pairs={{0,1},{1,0},{2,3},{3,2},{4,5},{5,4},{6,7},{7,6},{8,9},{9,8},{10,11... | collective-permute-start | bytes 798728 | tf_op jit(solution)/shard_map/up/ppermute | solution.py:155
  26.8 16.7 %collective-permute-start.3 = (f16[1040,128]{1,0:T(8,128)(2,1)S(1)}, f16[1040,128]{1,0:T(8,128)(2,1)S(1)}, u32[]{:S(2)}, u32[]{:S(2)}) collective-permute-start(f16[1040,128]{1,0:T(8,128)(2,1)S(1)} %get-tuple-element.139), channel_id=1, source_target_pairs={{0,4},{1,5},{2,6},{3,7},{4,0},{5,1},{6,2},{7,3},{8,12},{9,13},{10,... | collective-permute-start | bytes 798728 | tf_op jit(solution)/shard_map/up/ppermute | solution.py:155
  30.1 17.7 %collective-permute-start.4 = (f16[1040,128]{1,0:T(8,128)(2,1)S(1)}, f16[1040,128]{1,0:T(8,128)(2,1)S(1)}, u32[]{:S(2)}, u32[]{:S(2)}) collective-permute-start(f16[1040,128]{1,0:T(8,128)(2,1)S(1)} %get-tuple-element.140), channel_id=1, source_target_pairs={{0,5},{1,4},{2,7},{3,6},{4,1},{5,0},{6,3},{7,2},{8,13},{9,12},{10,... | collective-permute-start | bytes 798728 | tf_op jit(solution)/shard_map/up/ppermute | solution.py:155
  37.6 12.6 %collective-permute-start.16 = (f16[528,128]{1,0:T(8,128)(2,1)S(1)}, f16[528,128]{1,0:T(8,128)(2,1)S(1)}, u32[]{:S(2)}, u32[]{:S(2)}) collective-permute-start(f16[528,128]{1,0:T(8,128)(2,1)S(1)} %pad_maximum_fusion.17), channel_id=1, source_target_pairs={{0,8},{1,9},{2,10},{3,11},{4,12},{5,13},{6,14},{7,15},{8,0},{9,1},... | collective-permute-start | bytes 405512 | tf_op jit(solution)/shard_map/outer/ppermute | solution.py:155
  48.2 5.9 %collective-permute-start.5 = (f16[528,128]{1,0:T(8,128)(2,1)S(1)}, f16[528,128]{1,0:T(8,128)(2,1)S(1)}, u32[]{:S(2)}, u32[]{:S(2)}) collective-permute-start(f16[528,128]{1,0:T(8,128)(2,1)S(1)} %pad_maximum_fusion.16), channel_id=1, source_target_pairs={{0,8},{1,9},{2,10},{3,11},{4,12},{5,13},{6,14},{7,15},{8,0},{9,1},... | collective-permute-start | bytes 405512 | tf_op jit(solution)/shard_map/outer/ppermute | solution.py:155
  51.5 6.8 %collective-permute-start.17 = (f16[272,128]{1,0:T(8,128)(2,1)S(1)}, f16[272,128]{1,0:T(8,128)(2,1)S(1)}, u32[]{:S(2)}, u32[]{:S(2)}) collective-permute-start(f16[272,128]{1,0:T(8,128)(2,1)S(1)} %pad_maximum_fusion.19), channel_id=1, source_target_pairs={{0,24},{1,25},{2,26},{3,27},{4,28},{5,29},{6,30},{7,31},{8,16},{9,... | collective-permute-start | bytes 208904 | tf_op jit(solution)/shard_map/outer/ppermute | solution.py:155
  55.4 10.3 %collective-permute-start.6 = (f16[272,128]{1,0:T(8,128)(2,1)S(1)}, f16[272,128]{1,0:T(8,128)(2,1)S(1)}, u32[]{:S(2)}, u32[]{:S(2)}) collective-permute-start(f16[272,128]{1,0:T(8,128)(2,1)S(1)} %pad_maximum_fusion.18), channel_id=1, source_target_pairs={{0,24},{1,25},{2,26},{3,27},{4,28},{5,29},{6,30},{7,31},{8,16},{9,... | collective-permute-start | bytes 208904 | tf_op jit(solution)/shard_map/outer/ppermute | solution.py:155
  62.1 11.9 %collective-permute-start.18 = (f16[1040,128]{1,0:T(8,128)(2,1)S(1)}, f16[1040,128]{1,0:T(8,128)(2,1)S(1)}, u32[]{:S(2)}, u32[]{:S(2)}) collective-permute-start(f16[1040,128]{1,0:T(8,128)(2,1)S(1)} %get-tuple-element.131), channel_id=1, source_target_pairs={{0,1},{1,0},{2,3},{3,2},{4,5},{5,4},{6,7},{7,6},{8,9},{9,8},{10,11... | collective-permute-start | bytes 798728 | tf_op jit(solution)/shard_map/down/ppermute | solution.py:155
  63.7 13.4 %collective-permute-start.19 = (f16[1040,128]{1,0:T(8,128)(2,1)S(1)}, f16[1040,128]{1,0:T(8,128)(2,1)S(1)}, u32[]{:S(2)}, u32[]{:S(2)}) collective-permute-start(f16[1040,128]{1,0:T(8,128)(2,1)S(1)} %get-tuple-element.130), channel_id=1, source_target_pairs={{0,4},{1,5},{2,6},{3,7},{4,0},{5,1},{6,2},{7,3},{8,12},{9,13},{10,... | collective-permute-start | bytes 798728 | tf_op jit(solution)/shard_map/down/ppermute | solution.py:155
  65.1 13.6 %collective-permute-start.20 = (f16[1040,128]{1,0:T(8,128)(2,1)S(1)}, f16[1040,128]{1,0:T(8,128)(2,1)S(1)}, u32[]{:S(2)}, u32[]{:S(2)}) collective-permute-start(f16[1040,128]{1,0:T(8,128)(2,1)S(1)} %get-tuple-element.129), channel_id=1, source_target_pairs={{0,5},{1,4},{2,7},{3,6},{4,1},{5,0},{6,3},{7,2},{8,13},{9,12},{10,... | collective-permute-start | bytes 798728 | tf_op jit(solution)/shard_map/down/ppermute | solution.py:155
  68.1 14.7 %collective-permute-start.7 = (f16[1040,128]{1,0:T(8,128)(2,1)S(1)}, f16[1040,128]{1,0:T(8,128)(2,1)S(1)}, u32[]{:S(2)}, u32[]{:S(2)}) collective-permute-start(f16[1040,128]{1,0:T(8,128)(2,1)S(1)} %get-tuple-element.137), channel_id=1, source_target_pairs={{0,1},{1,0},{2,3},{3,2},{4,5},{5,4},{6,7},{7,6},{8,9},{9,8},{10,11... | collective-permute-start | bytes 798728 | tf_op jit(solution)/shard_map/down/ppermute | solution.py:155
  69.7 13.8 %collective-permute-start.8 = (f16[1040,128]{1,0:T(8,128)(2,1)S(1)}, f16[1040,128]{1,0:T(8,128)(2,1)S(1)}, u32[]{:S(2)}, u32[]{:S(2)}) collective-permute-start(f16[1040,128]{1,0:T(8,128)(2,1)S(1)} %get-tuple-element.136), channel_id=1, source_target_pairs={{0,4},{1,5},{2,6},{3,7},{4,0},{5,1},{6,2},{7,3},{8,12},{9,13},{10,... | collective-permute-start | bytes 798728 | tf_op jit(solution)/shard_map/down/ppermute | solution.py:155
  74.0 12.4 %collective-permute-start.9 = (f16[1040,128]{1,0:T(8,128)(2,1)S(1)}, f16[1040,128]{1,0:T(8,128)(2,1)S(1)}, u32[]{:S(2)}, u32[]{:S(2)}) collective-permute-start(f16[1040,128]{1,0:T(8,128)(2,1)S(1)} %get-tuple-element.135), channel_id=1, source_target_pairs={{0,5},{1,4},{2,7},{3,6},{4,1},{5,0},{6,3},{7,2},{8,13},{9,12},{10,... | collective-permute-start | bytes 798728 | tf_op jit(solution)/shard_map/down/ppermute | solution.py:155
  77.1 2.4 %copy-start.7 = (f32[2,8,128]{2,1,0:T(8,128)}, f32[2,8,128]{2,1,0:T(8,128)S(1)}, u32[]{:S(2)}) copy-start(f32[2,8,128]{2,1,0:T(8,128)S(1)} %exponential_bitcast_fusion.2) | copy-start | bytes 24580
  80.0 17.5 %collective-permute-start.21 = (f16[2112,128]{1,0:T(8,128)(2,1)}, f16[2112,128]{1,0:T(8,128)(2,1)S(1)}, u32[]{:S(2)}, u32[]{:S(2)}) collective-permute-start(f16[2112,128]{1,0:T(8,128)(2,1)} %slice_dynamic-update-slice_fusion), channel_id=1, source_target_pairs={{0,2},{1,3},{2,0},{3,1},{4,6},{5,7},{6,4},{7,5},{8,10},{9,11},{10,... | collective-permute-start | bytes 1622024 | tf_op jit(solution)/shard_map/core_return/ppermute | solution.py:155
  83.5 2.8 %copy-start.10 = (f32[2,8,128]{2,1,0:T(8,128)}, f32[2,8,128]{2,1,0:T(8,128)S(1)}, u32[]{:S(2)}) copy-start(f32[2,8,128]{2,1,0:T(8,128)S(1)} %exponential_bitcast_fusion.11) | copy-start | bytes 24580
  86.3 3.3 %copy-start.4 = (f16[1040,128]{1,0:T(8,128)(2,1)}, f16[1040,128]{1,0:T(8,128)(2,1)S(1)}, u32[]{:S(2)}) copy-start(f16[1040,128]{1,0:T(8,128)(2,1)S(1)} %collective-permute-done.9) | copy-start | bytes 798724
  86.5 11.3 %collective-permute-start.10 = (f16[2112,128]{1,0:T(8,128)(2,1)S(1)}, f16[2112,128]{1,0:T(8,128)(2,1)S(1)}, u32[]{:S(2)}, u32[]{:S(2)}) collective-permute-start(f16[2112,128]{1,0:T(8,128)(2,1)S(1)} %slice_dynamic-update-slice_fusion.3), channel_id=1, source_target_pairs={{0,2},{1,3},{2,0},{3,1},{4,6},{5,7},{6,4},{7,5},{8,10},{9,11},{10,... | collective-permute-start | bytes 1622024 | tf_op jit(solution)/shard_map/core_return/ppermute | solution.py:155
  89.6 1.1 slice-start
  (8 other events, 5.4 us)

commit v2 on v1

v2 whole, which is shorter than its diff:
```python
import functools

import jax
import jax.numpy as jnp
from jax import lax
from jax.experimental import pallas as pl
from jax.experimental.pallas import tpu as pltpu
from jax.sharding import PartitionSpec as P

HEAD_DIM = 128
GROUP = 128
AXES = ("ctx", "head")
F32 = jnp.float32
BF16 = jnp.bfloat16
HALF = jnp.float16
TAIL = 16
CUTS = (2, 2)
TOP = 15.0


VMEM = pl.BlockSpec(memory_space=pltpu.VMEM)
ANY = pl.BlockSpec(memory_space=pl.ANY)
NN, NT, TN = ((1,), (0,)), ((1,), (1,)), ((0,), (0,))
PLANE = (0, 1, 4, 5)
CORE = 2
CUBE = PLANE + tuple(m ^ CORE for m in PLANE)


def dot(a, b, dims):
    return lax.dot_general(a, b, (dims, ((), ())), preferred_element_type=F32)


def my_place():
    return lax.axis_index("ctx") * lax.axis_size("head") + lax.axis_index("head")


def block_columns(mask, chunk):
    first, count = chunk
    return pl.multiple_of((8 * first + ((my_place() & 7) ^ mask) * count) * HEAD_DIM, HEAD_DIM)


def state_kernel(chunks, q, k, v, d, *rest):
    outs, (held, in_sems, out_sems) = rest[: 2 * len(chunks)], rest[-3:]
    found = rest[2 * len(chunks) : -3]
    copies, leaving = {}, []
    for c, (first, count) in enumerate(chunks):
        cols = pl.ds(8 * first * HEAD_DIM, 8 * count * HEAD_DIM)
        for i, ref in ((1, k), (2, v), (3, d), (0, q)):
            copies[c, i] = pltpu.make_async_copy(ref.at[:, cols], held.at[i, :, cols], in_sems.at[c, i])
            copies[c, i].start()

    def leave(c, slot, begin, size, sem):
        rows = pl.ds(begin, size)
        copy = pltpu.make_async_copy(found[c].at[slot, rows], outs[2 * c + slot].at[rows], out_sems.at[c, sem])
        copy.start()
        leaving.append(copy)

    for c, (first, count) in enumerate(chunks):
        width = count * HEAD_DIM
        peaks = [jnp.zeros((8, HEAD_DIM), F32)] * 2
        for kind, (left, right) in enumerate(((2, 1), (3, 0))):
            copies[c, left].wait()
            copies[c, right].wait()
            for b in (4, 5, 6, 7, 0, 1, 2, 3):
                begin = block_columns(CUBE[b], chunks[c])
                for head in range(count):
                    cols = pl.ds(pl.multiple_of(begin + head * HEAD_DIM, HEAD_DIM), HEAD_DIM)
                    state = dot(held[left, :, cols], held[right, :, cols], TN)
                    start = (b % 4 * 2 + kind) * width + head * HEAD_DIM
                    found[c][b // 4, start : start + HEAD_DIM, :] = state
                    peak = jnp.max(jnp.abs(state).reshape(HEAD_DIM // 8, 8, HEAD_DIM), axis=0)
                    peaks[kind] = jnp.maximum(peaks[kind], peak)
                if kind == 1:
                    leave(c, b // 4, b % 4 * 2 * width, 2 * width, b)
        for kind in range(2):
            exps = exponents(jnp.full((8, HEAD_DIM), jnp.max(peaks[kind]), F32))
            for slot in range(2):
                row = 8 * width + kind * 8
                found[c][slot, row : row + 8, :] = exps
                found[c][slot, row + TAIL : row + TAIL + 8, :] = jnp.exp2(TOP - exps)
        for slot in range(2):
            leave(c, slot, 8 * width, 2 * TAIL, 8 + slot)
    for copy in leaving:
        copy.wait()


def states(arrays, chunks):
    rows, columns = arrays[0].shape
    flats = [jax.ShapeDtypeStruct((8 * n * HEAD_DIM + 2 * TAIL, HEAD_DIM), F32) for _, n in chunks]
    return pl.pallas_call(
        functools.partial(state_kernel, chunks),
        in_specs=[ANY] * 4,
        out_specs=(ANY,) * (2 * len(chunks)),
        out_shape=tuple(flat for flat in flats for _ in range(2)),
        scratch_shapes=[pltpu.VMEM((2,) + flat.shape, F32) for flat in flats]
        + [
            pltpu.VMEM((4, rows, columns), BF16),
            pltpu.SemaphoreType.DMA((len(chunks), 4)),
            pltpu.SemaphoreType.DMA((len(chunks), 10)),
        ],
        compiler_params=pltpu.CompilerParams(vmem_limit_bytes=56 << 20),
        cost_estimate=pl.CostEstimate(
            flops=4 * rows * columns * HEAD_DIM, bytes_accessed=24 * rows * columns, transcendentals=0
        ),
        name="group_states",
    )(*arrays)


def join_kernel(near, away, own, bound, *rest):
    messages, both, sems = rest[:3], rest[3], rest[4]
    width = (near.shape[0] - 2 * TAIL) // 8
    copies = []
    for i, ref in enumerate((near, away)):
        pieces = []
        for r in range(4):
            rows = pl.ds(2 * width * r, 2 * width + (2 * TAIL if r == 3 else 0))
            pieces.append(pltpu.make_async_copy(ref.at[rows], both.at[i, rows], sems.at[i, r]))
        copies.append(pieces)
    for r in (3, 0, 1, 2):
        for i in range(2):
            copies[i][r].start()
    for i in range(2):
        copies[i][3].wait()
        exps = both[i, 8 * width : 8 * width + TAIL, :]
        for message in messages:
            message[4 * width + i * TAIL : 4 * width + (i + 1) * TAIL, :] = exps
        bound[...] = jnp.exp2(exps) if i == 0 else bound[...] + jnp.exp2(exps)
    for r in range(4):
        for i in range(2):
            if r < 3:
                copies[i][r].wait()
            for kind in range(2):
                start = (r * 2 + kind) * width
                block = both[i, start : start + width, :]
                if r == 0:
                    own[i, kind] = block
                else:
                    row = 8 * width + TAIL + 8 * kind
                    to = (2 * i + kind) * width
                    messages[r - 1][to : to + width, :] = block * both[i, row : row + 1, :]


def join(mine, peer):
    width = (mine.shape[0] - 2 * TAIL) // 8
    message = jax.ShapeDtypeStruct((4 * width + 2 * TAIL, HEAD_DIM), F32)
    return pl.pallas_call(
        join_kernel,
        in_specs=[ANY, ANY],
        out_specs=(VMEM,) * 5,
        out_shape=(
            jax.ShapeDtypeStruct((2, 2, width, HEAD_DIM), F32),
            jax.ShapeDtypeStruct((TAIL, HEAD_DIM), F32),
            message,
            message,
            message,
        ),
        scratch_shapes=[pltpu.VMEM((2,) + mine.shape, F32), pltpu.SemaphoreType.DMA((2, 4))],
        compiler_params=pltpu.CompilerParams(vmem_limit_bytes=16 << 20),
        cost_estimate=pl.CostEstimate(
            flops=8 * width * HEAD_DIM, bytes_accessed=128 * width * HEAD_DIM, transcendentals=0
        ),
        name="join_groups",
    )(mine, peer)


def inside_kernel(scale, part, chunk, q, k, v, d, inner):
    rows, columns = q.shape
    first = lax.broadcasted_iota(jnp.int32, (rows, rows), 0)
    second = lax.broadcasted_iota(jnp.int32, (rows, rows), 1)
    for b, mask in enumerate(CUBE[4 * part : 4 * part + 4]):
        begin = block_columns(mask, chunk)
        for head in range(chunk[1]):
            cols = slice(head * HEAD_DIM, (head + 1) * HEAD_DIM)
            from_cols = pl.ds(pl.multiple_of(begin + head * HEAD_DIM, HEAD_DIM), HEAD_DIM)
            qh, kh, vh, dh = (ref[:, from_cols] for ref in (q, k, v, d))
            scores_t = jnp.where(second >= first, dot(kh, qh, NT) * scale, 0.0).astype(BF16)
            dscores_t = jnp.where(second >= first, dot(vh, dh, NT), 0.0).astype(BF16)
            dscores = jnp.where(first >= second, dot(dh, vh, NT), 0.0).astype(BF16)
            inner[b, 0, :, cols] = dot(dscores, kh, NN) * scale
            inner[b, 1, :, cols] = dot(dscores_t, qh, NN) * scale
            inner[b, 2, :, cols] = dot(scores_t, dh, NN)


def inside(arrays, part, chunk, scale):
    rows, width = arrays[0].shape[0], chunk[1] * HEAD_DIM
    return pl.pallas_call(
        functools.partial(inside_kernel, scale, part, chunk),
        in_specs=[VMEM] * 4,
        out_specs=VMEM,
        out_shape=jax.ShapeDtypeStruct((4, 3, rows, width), F32),
        compiler_params=pltpu.CompilerParams(vmem_limit_bytes=16 << 20),
        cost_estimate=pl.CostEstimate(
            flops=48 * rows * width * HEAD_DIM, bytes_accessed=80 * rows * width, transcendentals=0
        ),
        name="inside_group",
    )(*arrays)


def gradient_kernel(scale, part, picked, chunk, k, v, d, inner, *rest):
    inputs, outs, (done, sems) = rest[: len(picked)], rest[-5:-2], rest[-2:]
    first, count = chunk
    width = count * HEAD_DIM
    copies = []
    for state, b in zip(inputs, picked):
        mask = CUBE[4 * part + b]
        start = block_columns(mask, chunk)
        for head in range(count):
            cols = slice(head * HEAD_DIM, (head + 1) * HEAD_DIM)
            from_cols = pl.ds(pl.multiple_of(start + head * HEAD_DIM, HEAD_DIM), HEAD_DIM)
            kh, vh, dh = (ref[:, from_cols] for ref in (k, v, d))
            kv, g = state[0, cols, :] * scale, state[1, cols, :] * scale
            kv_hi, g_hi = kv.astype(BF16), g.astype(BF16)
            kv_lo = (kv - kv_hi.astype(F32)).astype(BF16)
            g_lo = (g - g_hi.astype(F32)).astype(BF16)
            out_q = inner[b, 0, :, cols] + (dot(dh, kv_hi, NN) + dot(dh, kv_lo, NN))
            out_k = inner[b, 1, :, cols] + (dot(vh, g_hi, NN) + dot(vh, g_lo, NN))
            out_v = inner[b, 2, :, cols] + (dot(kh, g_hi, NT) + dot(kh, g_lo, NT))
            for i, value in enumerate((out_q, out_k, out_v)):
                done[b, i, :, cols] = value.astype(BF16)
        for i in range(3):
            copy = pltpu.make_async_copy(done.at[b, i], outs[i].at[:, pl.ds(start, width)], sems.at[b, i])
            copy.start()
            copies.append(copy)
    for copy in copies:
        copy.wait()


def gradients(part, chunk, arrays, inner, blocks, scale, before):
    picked = tuple(sorted(blocks))
    rows, columns = arrays[0].shape
    width = chunk[1] * HEAD_DIM
    out = jax.ShapeDtypeStruct((rows, columns), BF16)
    extra = () if before is None else tuple(before)
    return pl.pallas_call(
        functools.partial(gradient_kernel, scale, part, picked, chunk),
        in_specs=[VMEM] * (4 + len(picked)) + [ANY] * len(extra),
        out_specs=(ANY,) * 3,
        out_shape=(out,) * 3,
        input_output_aliases={4 + len(picked) + i: i for i in range(len(extra))},
        scratch_shapes=[
            pltpu.VMEM((4, 3, rows, width), BF16),
            pltpu.SemaphoreType.DMA((4, 3)),
        ],
        compiler_params=pltpu.CompilerParams(vmem_limit_bytes=16 << 20),
        cost_estimate=pl.CostEstimate(
            flops=12 * len(picked) * rows * width * HEAD_DIM,
            bytes_accessed=18 * len(picked) * rows * width,
            transcendentals=0,
        ),
        name="gradients",
    )(*arrays[1:], inner, *(blocks[b] for b in picked), *extra)


def exponents(bound):
    return jnp.clip(jnp.ceil(jnp.log2(jnp.maximum(bound, 1e-30))) + 1.0, -100.0, 60.0)


def per_kind(rows):
    return rows.reshape(2, 8, HEAD_DIM)[:, :1, :]


def encode(parts):
    flat = [(part * per_kind(factor)[: part.shape[0]]).reshape(-1, HEAD_DIM) for part, _, factor in parts]
    return jnp.concatenate(flat + [exps for _, exps, _ in parts], axis=0).astype(HALF)


def tail(message, i, parts):
    start = message.shape[0] - (parts - i) * TAIL
    return message[start : start + TAIL].astype(F32)


def decode(rows, exps, kinds):
    factor = per_kind(jnp.exp2(exps - TOP))
    return rows.reshape(kinds, -1, HEAD_DIM).astype(F32) * factor[:kinds]


def after(values, *earlier):
    return lax.optimization_barrier((values, earlier))[0]


def whole_groups(queries, key_rows, value_rows, grad_out):
    arrays = (queries, key_rows, value_rows, grad_out)
    rows = queries.shape[0]
    heads = queries.shape[1] // HEAD_DIM
    devices = lax.axis_size("ctx") * lax.axis_size("head")
    place = my_place()
    scale = (HEAD_DIM * rows * devices) ** (-0.5)
    outer = (devices // 8).bit_length() - 1
    per = heads // 8

    def move(x, mask):
        return lax.ppermute(x, AXES, [(p, p ^ mask) for p in range(devices)])

    bit = [((place >> b) & 1).astype(F32) for b in range(3 + outer)]

    def weight(b):
        return jnp.stack([bit[b], 1.0 - bit[b]]).reshape(2, 1, 1)

    cuts = CUTS if sum(CUTS) == per else (per,)
    chunks = [(sum(cuts[:i]), count) for i, count in enumerate(cuts)]
    wy, wc, wx = weight(0), weight(1), weight(2)


    with jax.named_scope("states"):
        found = [x for chunk in chunks for x in states(arrays, (chunk,))]
        peers = [move(sent, CORE) for sent in found[1::2]]

    def send_up(mine, peer):
        with jax.named_scope("up"):
            own, bound, *messages = join(mine, peer)
            messages = [m.astype(HALF) for m in messages]
            got = [move(m, PLANE[r]) for r, m in zip((1, 2, 3), messages)]
            return (own, bound, got), messages

    def within(c, part, *earlier):
        with jax.named_scope("inside"):
            return inside(after(arrays, *earlier), part, chunks[c], scale)

    def exchange(c, state):
        first, count = chunks[c]
        width = count * HEAD_DIM
        with jax.named_scope("cube_total"):
            own, bound, got = state
            blocks = {(0, 0): own[0], (1, 0): own[1]}
            for r in (1, 2, 3):
                halves = got[r - 1][: -2 * TAIL].reshape(2, 2, width, HEAD_DIM)
                for i in (0, 1):
                    e = tail(got[r - 1], i, 2)
                    bound = bound + jnp.exp2(e)
                    blocks[i, r] = decode(halves[i], e, 2)
            total = functools.reduce(jnp.add, blocks.values())
        with jax.named_scope("outer"):
            sent_z = [total]
            entering = jnp.zeros_like(total)
            entering_bound = jnp.zeros_like(bound)
            running, running_bound = total, bound
            for b in range(outer):
                mask = 8 << b
                w = weight(3 + b)
                e = exponents(running_bound)
                if b < outer - 1:
                    sent_z.append(running)
                    reply = move(encode([(running, e, jnp.exp2(TOP - e))]), mask)
                    e = tail(reply, 0, 1)
                    other = decode(reply[:-TAIL], e, 2)
                    running = running + other
                    running_bound = running_bound + jnp.exp2(e)
                else:
                    up = bit[3 + b] > 0.5
                    payload = jnp.where(up, running[1], running[0])
                    e = jnp.tile(jnp.where(up, e[8:], e[:8]), (2, 1))
                    sent_z.append(payload)
                    reply = move(encode([(payload[None], e, jnp.exp2(TOP - e))]), mask)
                    e = tail(reply, 0, 1)
                    other = decode(reply[:-TAIL], e, 1)
                entering = entering + w * other
                entering_bound = entering_bound + jnp.exp2(e)
        with jax.named_scope("cube_before"):
            pair = {(i, x): blocks[i, 2 * x] + blocks[i, 2 * x + 1] for i in (0, 1) for x in (0, 1)}
            quad = {x: pair[0, x] + pair[1, x] for x in (0, 1)}
            local = {}
            for i in (0, 1):
                for x in (0, 1):
                    for y in (0, 1):
                        near = blocks[i, 2 * x + 1 - y] * (wy if y == 0 else 1.0 - wy)
                        mid = pair[1 - i, x] * (wc if i == 0 else 1.0 - wc)
                        far = quad[1 - x] * (wx if x == 0 else 1.0 - wx)
                        local[i, 2 * x + y] = near + mid + far
            local = lax.optimization_barrier(local)
        with jax.named_scope("down"):
            e = exponents(entering_bound + bound)
            factor = jnp.exp2(TOP - e)
            messages = [
                encode([(jnp.concatenate([local[0, r] + entering, local[1, r] + entering], 1), e, factor)])
                for r in (1, 2, 3)
            ]
            back = [move(m, PLANE[r]) for r, m in zip((1, 2, 3), messages)]
            return (local[0, 0] + entering, local[1, 0] + entering, e, factor, back), sent_z, messages

    def finish(c, state, inner, done, rounds):
        width = chunks[c][1] * HEAD_DIM
        own, other, e, factor, back = state
        near, far, handed = {0: own}, {}, {0: encode([(other, e, factor)])}
        for turn, blocks in enumerate(rounds):
            with jax.named_scope("core_return"):
                parts = []
                if turn:
                    back = after(back, done[:1])
                for r in blocks:
                    if r == 0:
                        parts.append(handed[0])
                        continue
                    m = back[r - 1]
                    both = m[:-TAIL].reshape(2, 2, width, HEAD_DIM)
                    near[r] = decode(both[:, 0], m[-TAIL:].astype(F32), 2)
                    parts += [both[:, 1].reshape(-1, HEAD_DIM), m[-TAIL:]]
                forward = move(jnp.concatenate(parts, axis=0), CORE)
            with jax.named_scope("gradients"):
                done = gradients(0, chunks[c], arrays, inner[0], {r: near[r] for r in blocks}, scale, done)
                pieces = forward.reshape(len(blocks), 2 * width + TAIL, HEAD_DIM)
                far = {r: decode(p[:-TAIL], p[-TAIL:].astype(F32), 2) for r, p in zip(blocks, pieces)}
                done = gradients(1, chunks[c], arrays, inner[1], far, scale, done)
        return done

    ups, inner, downs, done = [], [], [], None
    for c in range(len(chunks)):
        up, last = send_up(found[2 * c], peers[c])
        ups.append(up)
    for c in range(len(chunks)):
        inner.append([within(c, part, last) for part in (0, 1)])
    last = inner
    for c in range(len(chunks)):
        down, sent_z, last = exchange(c, after(ups[c], last))
        downs.append(down)
    for c in range(len(chunks)):
        final = c == len(chunks) - 1
        state = downs[c] if done is None else after(downs[c], done[:1])
        done = finish(c, state, inner[c], done, ((0, 1, 2), (3,)) if final else ((0, 1, 2, 3),))
    return tuple(done)


def entering(part, axis, reverse):
    count = lax.axis_size(axis)
    place = lax.axis_index(axis)
    ahead = count - 1 - place if reverse else place
    gathered = lax.all_gather(part, axis)

    def one(turn, state):
        source = count - 1 - turn if reverse else turn
        return state + lax.dynamic_index_in_dim(gathered, source, 0, False)

    return lax.fori_loop(0, ahead, one, jnp.zeros_like(part))


def split_groups(queries, key_rows, value_rows, grad_out):
    q_all, k_all, v_all, d_all = (
        lax.all_to_all(a, "head", split_axis=1, concat_axis=0, tiled=True)
        for a in (queries, key_rows, value_rows, grad_out)
    )
    rows_here = q_all.shape[0]
    heads_here = q_all.shape[1] // HEAD_DIM
    scale = (HEAD_DIM * rows_here * lax.axis_size("ctx")) ** (-0.5)
    highest = lax.Precision.HIGHEST
    block = GROUP
    nblocks = rows_here // block
    shape_four = (nblocks, block, heads_here, HEAD_DIM)
    q_four = q_all.reshape(shape_four)
    k_four = k_all.reshape(shape_four)
    v_four = v_all.reshape(shape_four)
    d_four = d_all.reshape(shape_four)
    kv_blocks = jnp.einsum("ntha,nthb->nhab", v_four, k_four, preferred_element_type=F32)
    g_blocks = jnp.einsum("ntha,nthb->nhab", d_four, q_four, preferred_element_type=F32)
    kv_before = entering(jnp.sum(kv_blocks, axis=0), "ctx", False)
    g_after = entering(jnp.sum(g_blocks, axis=0), "ctx", True)
    row_ids = lax.broadcasted_iota(jnp.int32, (nblocks, nblocks), 0)
    col_ids = lax.broadcasted_iota(jnp.int32, (nblocks, nblocks), 1)
    strict_lower = (col_ids < row_ids).astype(F32)
    strict_upper = (col_ids > row_ids).astype(F32)
    kv_in = kv_before[None] + jnp.einsum("mn,nhab->mhab", strict_lower, kv_blocks, precision=highest)
    g_in = g_after[None] + jnp.einsum("mn,nhab->mhab", strict_upper, g_blocks, precision=highest)
    later = lax.broadcasted_iota(jnp.int32, (block, block), 0)
    earlier = lax.broadcasted_iota(jnp.int32, (block, block), 1)
    causal = (later >= earlier).astype(F32)
    scores = (
        jnp.einsum("nthd,nshd->nhts", q_four, k_four, preferred_element_type=F32) * (scale * causal)
    ).astype(BF16)
    dscores = (jnp.einsum("nthd,nshd->nhts", d_four, v_four, preferred_element_type=F32) * causal).astype(BF16)
    k_float, v_float, d_float = (a.astype(F32) for a in (k_four, v_four, d_four))
    grad_q = scale * (
        jnp.einsum("nhts,nshd->nthd", dscores, k_four, preferred_element_type=F32)
        + jnp.einsum("ntha,nhab->nthb", d_float, kv_in, precision=highest)
    )
    grad_k = scale * (
        jnp.einsum("nhts,nthd->nshd", dscores, q_four, preferred_element_type=F32)
        + jnp.einsum("ntha,nhab->nthb", v_float, g_in, precision=highest)
    )
    grad_v = jnp.einsum(
        "nhts,nthd->nshd", scores, d_four, preferred_element_type=F32
    ) + scale * jnp.einsum("nthb,nhab->ntha", k_float, g_in, precision=highest)
    flat_shape = (rows_here, heads_here * HEAD_DIM)
    return tuple(
        lax.all_to_all(
            a.reshape(flat_shape).astype(BF16), "head", split_axis=0, concat_axis=1, tiled=True
        )
        for a in (grad_q, grad_k, grad_v)
    )


def per_device(*arrays):
    rows, columns = arrays[0].shape
    devices = lax.axis_size("ctx") * lax.axis_size("head")
    whole = rows == GROUP and lax.axis_size("head") == 2 and devices >= 16 and devices & (devices - 1) == 0
    if whole and columns % (16 * HEAD_DIM) == 0:
        return whole_groups(*arrays)
    return split_groups(*arrays)


def solution(mesh):
    placed = P(AXES, None)
    return jax.shard_map(
        per_device, mesh=mesh, in_specs=(placed,) * 4, out_specs=(placed,) * 3, check_vma=False
    )
```

time: 118 us -> 73.1 us (0.62)
  local copies, waits for them, and re-layouts: 12.8 us -> 1.28 us
  other arithmetic: 15.5 us -> 5.05 us
  Pallas kernels: 33 us -> 23.7 us
  waiting for transfers between devices: 22.8 us -> 13.7 us
  starting transfers between devices: 31.5 us -> 27.3 us
    pallas_call x6 -> x14, Pallas kernels: 33 us -> 23.7 us  [the longest x6 8.44 us: gradients(): pl.pallas_call(functools.partial(gradient_kernel, scale, part, picked, ch...]
    ppermute x22 -> x21, waiting for transfers between devices: 22.8 us -> 13.7 us  [move(): return lax.ppermute(x, AXES, [(p, p ^ mask) for p in range(devices)])]
    another operation x20 -> x8, other arithmetic: 9.07 us -> 0.81 us
    unnamed x45 -> x22, local copies, waits for them, and re-layouts: 5.35 us -> 0.36 us
    ppermute x22 -> x21, starting transfers between devices: 31.5 us -> 27.3 us  [move(): return lax.ppermute(x, AXES, [(p, p ^ mask) for p in range(devices)])]
    slice x15 -> x18, local copies, waits for them, and re-layouts: 3.9 us -> 0.79 us  [the longest x6 0.33 us: finish(): both = m[:-TAIL].reshape(2, 2, width, HEAD_DIM)]
    slice x32 -> x33, local copies, waits for them, and re-layouts: 2.75 us -> 0.09 us  [per_kind(): return rows.reshape(2, 8, HEAD_DIM)[:, :1, :]]
    add x4 -> x12, other arithmetic: 2.71 us -> 2.26 us  [the longest x6 1.31 us: exchange(): local[i, 2 * x + y] = near + mid + far]
  transfers between devices with their start and end apart: 22 -> 21, of which waited for: 10 -> 8; matrix products, arithmetic and copies ran while one was open for 17% -> 8% of each run, Pallas kernels for 9% -> 24%
where the time goes in v2:
time: 73.1 us; the launch traced here: 72.9 us
  starting transfers between devices  27.3 us (37%)
  Pallas kernels  23.7 us (32%)
  waiting for transfers between devices  13.7 us (19%)
  other arithmetic  5.05 us (7%)
  between operations  1.94 us (3%)
  local copies, waits for them, and re-layouts  1.28 us (2%)
    ppermute x21, starting transfers between devices, move(): return lax.ppermute(x, AXES, [(p, p ^ mask) for p in range(devices)])  27.3 us
    ppermute x21, waiting for transfers between devices, move(): return lax.ppermute(x, AXES, [(p, p ^ mask) for p in range(devices)])  13.7 us
    pallas_call x6, Pallas kernels, gradients(): pl.pallas_call(functools.partial(gradient_kernel, scale, part, picked, ch...  8.44 us
    pallas_call x4, Pallas kernels, inside(): pl.pallas_call(functools.partial(inside_kernel, scale, part, chunk), in_s...  7.2 us
    pallas_call x2, Pallas kernels, states(): pl.pallas_call(functools.partial(state_kernel, chunks), in_specs=[ANY] *...  6.98 us
  transfers between devices with their start and end apart: 21, of which 8 were waited for; matrix products, arithmetic and copies ran while one was open for 8% of the time, Pallas kernels for 24%

profile of v2, /device:TPU:0, one launch (start us, length us, event | category | flops | bytes accessed | tf_op | source)
XLA Modules:
  0.0 72.9 jit_solution(8005595566898018443)
XLA Ops:
  0.6 3.5 %group_states.3 = (f32[2080,128]{1,0:T(8,128)}, f32[2080,128]{1,0:T(8,128)}) custom-call(bf16[128,4096]{1,0:T(8,128)(2,1)} %q.7, bf16[128,4096]{1,0:T(8,128)(2,1)} %k.19, bf16[128,4096]{1,0:T(8,128)(2,1)} %v.19, bf16[128,4096]{1,0:T(8,128)(2,1)} %d.19), custom_call_target="tpu_custom_call" | custom-call | flops 268435456 | bytes 12582912 | tf_op jit(solution)/shard_map/states/group_states/pallas_call | solution.py:90
  4.1 0.5 collective-permute-start.4
  4.6 3.5 %group_states.2 = (f32[2080,128]{1,0:T(8,128)}, f32[2080,128]{1,0:T(8,128)}) custom-call(bf16[128,4096]{1,0:T(8,128)(2,1)} %q.7, bf16[128,4096]{1,0:T(8,128)(2,1)} %k.19, bf16[128,4096]{1,0:T(8,128)(2,1)} %v.19, bf16[128,4096]{1,0:T(8,128)(2,1)} %d.19), custom_call_target="tpu_custom_call" | custom-call | flops 268435456 | bytes 12582912 | tf_op jit(solution)/shard_map/states/group_states/pallas_call | solution.py:90
  8.9 3.0 %collective-permute-start.5 = (f16[1056,128]{1,0:T(8,128)(2,1)S(1)}, f16[1056,128]{1,0:T(8,128)(2,1)S(1)}, u32[]{:S(2)}, u32[]{:S(2)}) collective-permute-start(f16[1056,128]{1,0:T(8,128)(2,1)S(1)} %convert_element_type.350), channel_id=1, source_target_pairs={{0,1},{1,0},{2,3},{3,2},{4,5},{5,4},{6,7},{7,6},{8,9},{9,8},{10,11... | collective-permute-start | bytes 811016 | tf_op jit(solution)/shard_map/up/ppermute | solution.py:292
  11.9 1.6 %collective-permute-start.6 = (f16[1056,128]{1,0:T(8,128)(2,1)S(1)}, f16[1056,128]{1,0:T(8,128)(2,1)S(1)}, u32[]{:S(2)}, u32[]{:S(2)}) collective-permute-start(f16[1056,128]{1,0:T(8,128)(2,1)S(1)} %convert_element_type.351), channel_id=1, source_target_pairs={{0,4},{1,5},{2,6},{3,7},{4,0},{5,1},{6,2},{7,3},{8,12},{9,13},{10,... | collective-permute-start | bytes 811016 | tf_op jit(solution)/shard_map/up/ppermute | solution.py:292
  13.8 0.6 join_groups.2
  14.6 2.0 %collective-permute-start.1 = (f16[1056,128]{1,0:T(8,128)(2,1)S(1)}, f16[1056,128]{1,0:T(8,128)(2,1)S(1)}, u32[]{:S(2)}, u32[]{:S(2)}) collective-permute-start(f16[1056,128]{1,0:T(8,128)(2,1)S(1)} %convert_element_type.347), channel_id=1, source_target_pairs={{0,1},{1,0},{2,3},{3,2},{4,5},{5,4},{6,7},{7,6},{8,9},{9,8},{10,11... | collective-permute-start | bytes 811016 | tf_op jit(solution)/shard_map/up/ppermute | solution.py:292
  16.6 1.5 %collective-permute-start.2 = (f16[1056,128]{1,0:T(8,128)(2,1)S(1)}, f16[1056,128]{1,0:T(8,128)(2,1)S(1)}, u32[]{:S(2)}, u32[]{:S(2)}) collective-permute-start(f16[1056,128]{1,0:T(8,128)(2,1)S(1)} %convert_element_type.348), channel_id=1, source_target_pairs={{0,4},{1,5},{2,6},{3,7},{4,0},{5,1},{6,2},{7,3},{8,12},{9,13},{10,... | collective-permute-start | bytes 811016 | tf_op jit(solution)/shard_map/up/ppermute | solution.py:292
  18.1 1.8 %inside_group.4.inner = f32[4,3,128,256]{3,2,1,0:T(8,128)S(1)} custom-call(bf16[128,4096]{1,0:T(8,128)(2,1)S(1)} %copy-done.3, bf16[128,4096]{1,0:T(8,128)(2,1)S(1)} %copy-done, bf16[128,4096]{1,0:T(8,128)(2,1)S(1)} %copy-done.1, bf16[128,4096]{1,0:T(8,128)(2,1)S(1)} %copy-done.2), custom_call_target="tpu_custom_call" | custom-call | flops 201326592 | bytes 2621440 | tf_op jit(solution)/shard_map/inside/inside_group/pallas_call | solution.py:186
  19.9 1.8 %inside_group.5.inner = f32[4,3,128,256]{3,2,1,0:T(8,128)S(1)} custom-call(bf16[128,4096]{1,0:T(8,128)(2,1)S(1)} %copy-done.3, bf16[128,4096]{1,0:T(8,128)(2,1)S(1)} %copy-done, bf16[128,4096]{1,0:T(8,128)(2,1)S(1)} %copy-done.1, bf16[128,4096]{1,0:T(8,128)(2,1)S(1)} %copy-done.2), custom_call_target="tpu_custom_call" | custom-call | flops 201326592 | bytes 2621440 | tf_op jit(solution)/shard_map/inside/inside_group/pallas_call | solution.py:186
  21.7 1.8 %inside_group.6.inner = f32[4,3,128,256]{3,2,1,0:T(8,128)S(1)} custom-call(bf16[128,4096]{1,0:T(8,128)(2,1)S(1)} %copy-done.3, bf16[128,4096]{1,0:T(8,128)(2,1)S(1)} %copy-done, bf16[128,4096]{1,0:T(8,128)(2,1)S(1)} %copy-done.1, bf16[128,4096]{1,0:T(8,128)(2,1)S(1)} %copy-done.2), custom_call_target="tpu_custom_call" | custom-call | flops 201326592 | bytes 2621440 | tf_op jit(solution)/shard_map/inside/inside_group/pallas_call | solution.py:186
  23.5 1.8 %inside_group.7.inner = f32[4,3,128,256]{3,2,1,0:T(8,128)S(1)} custom-call(bf16[128,4096]{1,0:T(8,128)(2,1)S(1)} %copy-done.3, bf16[128,4096]{1,0:T(8,128)(2,1)S(1)} %copy-done, bf16[128,4096]{1,0:T(8,128)(2,1)S(1)} %copy-done.1, bf16[128,4096]{1,0:T(8,128)(2,1)S(1)} %copy-done.2), custom_call_target="tpu_custom_call" | custom-call | flops 201326592 | bytes 2621440 | tf_op jit(solution)/shard_map/inside/inside_group/pallas_call | solution.py:186
  25.4 0.9 %collective-permute-start.3 = (f16[1056,128]{1,0:T(8,128)(2,1)S(1)}, f16[1056,128]{1,0:T(8,128)(2,1)S(1)}, u32[]{:S(2)}, u32[]{:S(2)}) collective-permute-start(f16[1056,128]{1,0:T(8,128)(2,1)S(1)} %convert_element_type.349), channel_id=1, source_target_pairs={{0,5},{1,4},{2,7},{3,6},{4,1},{5,0},{6,3},{7,2},{8,13},{9,12},{10,... | collective-permute-start | bytes 811016 | tf_op jit(solution)/shard_map/up/ppermute | solution.py:292
  27.2 2.2 %collective-permute-start.8 = (f16[528,128]{1,0:T(8,128)(2,1)S(1)}, f16[528,128]{1,0:T(8,128)(2,1)S(1)}, u32[]{:S(2)}, u32[]{:S(2)}) collective-permute-start(f16[528,128]{1,0:T(8,128)(2,1)S(1)} %pad_maximum_fusion.6), channel_id=1, source_target_pairs={{0,8},{1,9},{2,10},{3,11},{4,12},{5,13},{6,14},{7,15},{8,0},{9,1},... | collective-permute-start | bytes 405512 | tf_op jit(solution)/shard_map/outer/ppermute | solution.py:292
  29.7 2.6 %collective-permute-done.8 = f16[528,128]{1,0:T(8,128)(2,1)S(1)} collective-permute-done((f16[528,128]{1,0:T(8,128)(2,1)S(1)}, f16[528,128]{1,0:T(8,128)(2,1)S(1)}, u32[]{:S(2)}, u32[]{:S(2)}) %collective-permute-start.8) | collective-permute-done | bytes 135200 | tf_op jit(solution)/shard_map/outer/ppermute | solution.py:292
  32.7 3.1 %collective-permute-start.9 = (f16[272,128]{1,0:T(8,128)(2,1)S(1)}, f16[272,128]{1,0:T(8,128)(2,1)S(1)}, u32[]{:S(2)}, u32[]{:S(2)}) collective-permute-start(f16[272,128]{1,0:T(8,128)(2,1)S(1)} %pad_maximum_fusion.9), channel_id=1, source_target_pairs={{0,16},{1,17},{2,18},{3,19},{4,20},{5,21},{6,22},{7,23},{8,24},{9,... | collective-permute-start | bytes 208904 | tf_op jit(solution)/shard_map/outer/ppermute | solution.py:292
  36.1 2.0 %collective-permute-done.9 = f16[272,128]{1,0:T(8,128)(2,1)S(1)} collective-permute-done((f16[272,128]{1,0:T(8,128)(2,1)S(1)}, f16[272,128]{1,0:T(8,128)(2,1)S(1)}, u32[]{:S(2)}, u32[]{:S(2)}) %collective-permute-start.9) | collective-permute-done | bytes 69664 | tf_op jit(solution)/shard_map/outer/ppermute | solution.py:292
  38.9 1.9 %collective-permute-start.15 = (f16[1040,128]{1,0:T(8,128)(2,1)S(1)}, f16[1040,128]{1,0:T(8,128)(2,1)S(1)}, u32[]{:S(2)}, u32[]{:S(2)}) collective-permute-start(f16[1040,128]{1,0:T(8,128)(2,1)S(1)} %get-tuple-element.251), channel_id=1, source_target_pairs={{0,1},{1,0},{2,3},{3,2},{4,5},{5,4},{6,7},{7,6},{8,9},{9,8},{10,11... | collective-permute-start | bytes 798728 | tf_op jit(solution)/shard_map/down/ppermute | solution.py:292
  40.8 1.5 %collective-permute-start.16 = (f16[1040,128]{1,0:T(8,128)(2,1)S(1)}, f16[1040,128]{1,0:T(8,128)(2,1)S(1)}, u32[]{:S(2)}, u32[]{:S(2)}) collective-permute-start(f16[1040,128]{1,0:T(8,128)(2,1)S(1)} %get-tuple-element.250), channel_id=1, source_target_pairs={{0,4},{1,5},{2,6},{3,7},{4,0},{5,1},{6,2},{7,3},{8,12},{9,13},{10,... | collective-permute-start | bytes 798728 | tf_op jit(solution)/shard_map/down/ppermute | solution.py:292
  43.0 2.0 %collective-permute-start.10 = (f16[528,128]{1,0:T(8,128)(2,1)S(1)}, f16[528,128]{1,0:T(8,128)(2,1)S(1)}, u32[]{:S(2)}, u32[]{:S(2)}) collective-permute-start(f16[528,128]{1,0:T(8,128)(2,1)S(1)} %pad_maximum_fusion.7), channel_id=1, source_target_pairs={{0,8},{1,9},{2,10},{3,11},{4,12},{5,13},{6,14},{7,15},{8,0},{9,1},... | collective-permute-start | bytes 405512 | tf_op jit(solution)/shard_map/outer/ppermute | solution.py:292
  45.3 3.5 %collective-permute-done.10 = f16[528,128]{1,0:T(8,128)(2,1)S(1)} collective-permute-done((f16[528,128]{1,0:T(8,128)(2,1)S(1)}, f16[528,128]{1,0:T(8,128)(2,1)S(1)}, u32[]{:S(2)}, u32[]{:S(2)}) %collective-permute-start.10) | collective-permute-done | bytes 135200 | tf_op jit(solution)/shard_map/outer/ppermute | solution.py:292
  49.2 2.7 %collective-permute-start.11 = (f16[272,128]{1,0:T(8,128)(2,1)S(1)}, f16[272,128]{1,0:T(8,128)(2,1)S(1)}, u32[]{:S(2)}, u32[]{:S(2)}) collective-permute-start(f16[272,128]{1,0:T(8,128)(2,1)S(1)} %pad_maximum_fusion.10), channel_id=1, source_target_pairs={{0,16},{1,17},{2,18},{3,19},{4,20},{5,21},{6,22},{7,23},{8,24},{9,... | collective-permute-start | bytes 208904 | tf_op jit(solution)/shard_map/outer/ppermute | solution.py:292
  52.2 2.3 %collective-permute-done.11 = f16[272,128]{1,0:T(8,128)(2,1)S(1)} collective-permute-done((f16[272,128]{1,0:T(8,128)(2,1)S(1)}, f16[272,128]{1,0:T(8,128)(2,1)S(1)}, u32[]{:S(2)}, u32[]{:S(2)}) %collective-permute-start.11) | collective-permute-done | bytes 69664 | tf_op jit(solution)/shard_map/outer/ppermute | solution.py:292
  55.2 1.7 %collective-permute-start.12 = (f16[1040,128]{1,0:T(8,128)(2,1)S(1)}, f16[1040,128]{1,0:T(8,128)(2,1)S(1)}, u32[]{:S(2)}, u32[]{:S(2)}) collective-permute-start(f16[1040,128]{1,0:T(8,128)(2,1)S(1)} %get-tuple-element.248), channel_id=1, source_target_pairs={{0,1},{1,0},{2,3},{3,2},{4,5},{5,4},{6,7},{7,6},{8,9},{9,8},{10,11... | collective-permute-start | bytes 798728 | tf_op jit(solution)/shard_map/down/ppermute | solution.py:292
  57.0 1.5 %collective-permute-start.13 = (f16[1040,128]{1,0:T(8,128)(2,1)S(1)}, f16[1040,128]{1,0:T(8,128)(2,1)S(1)}, u32[]{:S(2)}, u32[]{:S(2)}) collective-permute-start(f16[1040,128]{1,0:T(8,128)(2,1)S(1)} %get-tuple-element.247), channel_id=1, source_target_pairs={{0,4},{1,5},{2,6},{3,7},{4,0},{5,1},{6,2},{7,3},{8,12},{9,13},{10,... | collective-permute-start | bytes 798728 | tf_op jit(solution)/shard_map/down/ppermute | solution.py:292
  59.5 1.6 %gradients.6 = (bf16[128,4096]{1,0:T(8,128)(2,1)}, bf16[128,4096]{1,0:T(8,128)(2,1)}, bf16[128,4096]{1,0:T(8,128)(2,1)}) custom-call(bf16[128,4096]{1,0:T(8,128)(2,1)S(1)} %copy-done, bf16[128,4096]{1,0:T(8,128)(2,1)S(1)} %copy-done.1, bf16[128,4096]{1,0:T(8,128)(2,1)S(1)} %copy-done.2, f32[4,3,128,256]{3,2,1,0:T(8,128)S(1)} %inside_group.5.inner, ...), custom_call_target="tpu_custom_call" | custom-call | flops 201326592 | bytes 2359296 | tf_op jit(solution)/shard_map/gradients/gradients/pallas_call | solution.py:234
  61.6 1.8 %gradients.7 = (bf16[128,4096]{1,0:T(8,128)(2,1)}, bf16[128,4096]{1,0:T(8,128)(2,1)}, bf16[128,4096]{1,0:T(8,128)(2,1)}) custom-call(bf16[128,4096]{1,0:T(8,128)(2,1)S(1)} %copy-done, bf16[128,4096]{1,0:T(8,128)(2,1)S(1)} %copy-done.1, bf16[128,4096]{1,0:T(8,128)(2,1)S(1)} %copy-done.2, ...), custom_call_target="tpu_custom_call", output_to_operand_aliasing={{0}: (8, {}), {1}: (9, {}), {2}: (10, {})} | custom-call | flops 201326592 | bytes 2359296 | tf_op jit(solution)/shard_map/gradients/gradients/pallas_call | solution.py:234
  63.4 2.6 %collective-permute-done.14 = f16[1040,128]{1,0:T(8,128)(2,1)S(1)} collective-permute-done((f16[1040,128]{1,0:T(8,128)(2,1)S(1)}, f16[1040,128]{1,0:T(8,128)(2,1)S(1)}, u32[]{:S(2)}, u32[]{:S(2)}) %collective-permute-start.14) | collective-permute-done | bytes 266272 | tf_op jit(solution)/shard_map/down/ppermute | solution.py:292
  66.6 1.4 %gradients.8 = (bf16[128,4096]{1,0:T(8,128)(2,1)}, bf16[128,4096]{1,0:T(8,128)(2,1)}, bf16[128,4096]{1,0:T(8,128)(2,1)}) custom-call(bf16[128,4096]{1,0:T(8,128)(2,1)S(1)} %copy-done, bf16[128,4096]{1,0:T(8,128)(2,1)S(1)} %copy-done.1, bf16[128,4096]{1,0:T(8,128)(2,1)S(1)} %copy-done.2, ...), custom_call_target="tpu_custom_call", output_to_operand_aliasing={{0}: (7, {}), {1}: (8, {}), {2}: (9, {})} | custom-call | flops 150994944 | bytes 1769472 | tf_op jit(solution)/shard_map/gradients/gradients/pallas_call | solution.py:234
  68.5 1.4 %gradients.9 = (bf16[128,4096]{1,0:T(8,128)(2,1)}, bf16[128,4096]{1,0:T(8,128)(2,1)}, bf16[128,4096]{1,0:T(8,128)(2,1)}) custom-call(bf16[128,4096]{1,0:T(8,128)(2,1)S(1)} %copy-done, bf16[128,4096]{1,0:T(8,128)(2,1)S(1)} %copy-done.1, bf16[128,4096]{1,0:T(8,128)(2,1)S(1)} %copy-done.2, ...), custom_call_target="tpu_custom_call", output_to_operand_aliasing={{0}: (7, {}), {1}: (8, {}), {2}: (9, {})} | custom-call | flops 150994944 | bytes 1769472 | tf_op jit(solution)/shard_map/gradients/gradients/pallas_call | solution.py:234
  70.5 1.1 %gradients.10 = (bf16[128,4096]{1,0:T(8,128)(2,1)}, bf16[128,4096]{1,0:T(8,128)(2,1)}, bf16[128,4096]{1,0:T(8,128)(2,1)}) custom-call(bf16[128,4096]{1,0:T(8,128)(2,1)S(1)} %copy-done, bf16[128,4096]{1,0:T(8,128)(2,1)S(1)} %copy-done.1, bf16[128,4096]{1,0:T(8,128)(2,1)S(1)} %copy-done.2, ...), custom_call_target="tpu_custom_call", output_to_operand_aliasing={{0}: (5, {}), {1}: (6, {}), {2}: (7, {})} | custom-call | flops 50331648 | bytes 589824 | tf_op jit(solution)/shard_map/gradients/gradients/pallas_call | solution.py:234
  71.7 1.1 %gradients.11 = (bf16[128,4096]{1,0:T(8,128)(2,1)}, bf16[128,4096]{1,0:T(8,128)(2,1)}, bf16[128,4096]{1,0:T(8,128)(2,1)}) custom-call(bf16[128,4096]{1,0:T(8,128)(2,1)S(1)} %copy-done, bf16[128,4096]{1,0:T(8,128)(2,1)S(1)} %copy-done.1, bf16[128,4096]{1,0:T(8,128)(2,1)S(1)} %copy-done.2, ...), custom_call_target="tpu_custom_call", output_to_operand_aliasing={{0}: (5, {}), {1}: (6, {}), {2}: (7, {})} | custom-call | flops 50331648 | bytes 589824 | tf_op jit(solution)/shard_map/gradients/gradients/pallas_call | solution.py:234
  (183 shorter events, 8.7 us)
Async XLA Ops:
  4.1 4.3 %copy-start.5 = (f32[2080,128]{1,0:T(8,128)S(1)}, f32[2080,128]{1,0:T(8,128)}, u32[]{:S(2)}) copy-start(f32[2080,128]{1,0:T(8,128)} %get-tuple-element.81.near) | copy-start | bytes 3194884
  4.1 4.3 %collective-permute-start.4 = (f32[2080,128]{1,0:T(8,128)}, f32[2080,128]{1,0:T(8,128)S(1)}, u32[]{:S(2)}, u32[]{:S(2)}) collective-permute-start(f32[2080,128]{1,0:T(8,128)} %get-tuple-element.82), channel_id=1, source_target_pairs={{0,2},{1,3},{2,0},{3,1},{4,6},{5,7},{6,4},{7,5},{8,10},{9,11},{10,... | collective-permute-start | bytes 3194888 | tf_op jit(solution)/shard_map/states/ppermute | solution.py:292
  8.2 5.6 %collective-permute-start = (f32[2080,128]{1,0:T(8,128)}, f32[2080,128]{1,0:T(8,128)S(1)}, u32[]{:S(2)}, u32[]{:S(2)}) collective-permute-start(f32[2080,128]{1,0:T(8,128)} %get-tuple-element.71), channel_id=1, source_target_pairs={{0,2},{1,3},{2,0},{3,1},{4,6},{5,7},{6,4},{7,5},{8,10},{9,11},{10,... | collective-permute-start | bytes 3194888 | tf_op jit(solution)/shard_map/states/ppermute | solution.py:292
  8.9 4.9 %copy-start.4 = (f32[2080,128]{1,0:T(8,128)S(1)}, f32[2080,128]{1,0:T(8,128)}, u32[]{:S(2)}) copy-start(f32[2080,128]{1,0:T(8,128)} %get-tuple-element.70.near) | copy-start | bytes 3194884
  8.9 16.4 %collective-permute-start.5 = (f16[1056,128]{1,0:T(8,128)(2,1)S(1)}, f16[1056,128]{1,0:T(8,128)(2,1)S(1)}, u32[]{:S(2)}, u32[]{:S(2)}) collective-permute-start(f16[1056,128]{1,0:T(8,128)(2,1)S(1)} %convert_element_type.350), channel_id=1, source_target_pairs={{0,1},{1,0},{2,3},{3,2},{4,5},{5,4},{6,7},{7,6},{8,9},{9,8},{10,11... | collective-permute-start | bytes 811016 | tf_op jit(solution)/shard_map/up/ppermute | solution.py:292
  11.9 14.4 %collective-permute-start.6 = (f16[1056,128]{1,0:T(8,128)(2,1)S(1)}, f16[1056,128]{1,0:T(8,128)(2,1)S(1)}, u32[]{:S(2)}, u32[]{:S(2)}) collective-permute-start(f16[1056,128]{1,0:T(8,128)(2,1)S(1)} %convert_element_type.351), channel_id=1, source_target_pairs={{0,4},{1,5},{2,6},{3,7},{4,0},{5,1},{6,2},{7,3},{8,12},{9,13},{10,... | collective-permute-start | bytes 811016 | tf_op jit(solution)/shard_map/up/ppermute | solution.py:292
  13.5 13.1 %collective-permute-start.7 = (f16[1056,128]{1,0:T(8,128)(2,1)S(1)}, f16[1056,128]{1,0:T(8,128)(2,1)S(1)}, u32[]{:S(2)}, u32[]{:S(2)}) collective-permute-start(f16[1056,128]{1,0:T(8,128)(2,1)S(1)} %convert_element_type.352), channel_id=1, source_target_pairs={{0,5},{1,4},{2,7},{3,6},{4,1},{5,0},{6,3},{7,2},{8,13},{9,12},{10,... | collective-permute-start | bytes 811016 | tf_op jit(solution)/shard_map/up/ppermute | solution.py:292
  13.8 4.3 %copy-start.2 = (bf16[128,4096]{1,0:T(8,128)(2,1)S(1)}, bf16[128,4096]{1,0:T(8,128)(2,1)}, u32[]{:S(2)}) copy-start(bf16[128,4096]{1,0:T(8,128)(2,1)} %d.19) | copy-start | bytes 3145732
  13.8 4.3 %copy-start.3 = (bf16[128,4096]{1,0:T(8,128)(2,1)S(1)}, bf16[128,4096]{1,0:T(8,128)(2,1)}, u32[]{:S(2)}) copy-start(bf16[128,4096]{1,0:T(8,128)(2,1)} %q.7) | copy-start | bytes 3145732
  14.4 3.7 %copy-start = (bf16[128,4096]{1,0:T(8,128)(2,1)S(1)}, bf16[128,4096]{1,0:T(8,128)(2,1)}, u32[]{:S(2)}) copy-start(bf16[128,4096]{1,0:T(8,128)(2,1)} %k.19) | copy-start | bytes 3145732
  14.4 3.7 %copy-start.1 = (bf16[128,4096]{1,0:T(8,128)(2,1)S(1)}, bf16[128,4096]{1,0:T(8,128)(2,1)}, u32[]{:S(2)}) copy-start(bf16[128,4096]{1,0:T(8,128)(2,1)} %v.19) | copy-start | bytes 3145732
  14.6 27.7 %collective-permute-start.1 = (f16[1056,128]{1,0:T(8,128)(2,1)S(1)}, f16[1056,128]{1,0:T(8,128)(2,1)S(1)}, u32[]{:S(2)}, u32[]{:S(2)}) collective-permute-start(f16[1056,128]{1,0:T(8,128)(2,1)S(1)} %convert_element_type.347), channel_id=1, source_target_pairs={{0,1},{1,0},{2,3},{3,2},{4,5},{5,4},{6,7},{7,6},{8,9},{9,8},{10,11... | collective-permute-start | bytes 811016 | tf_op jit(solution)/shard_map/up/ppermute | solution.py:292
  16.6 25.8 %collective-permute-start.2 = (f16[1056,128]{1,0:T(8,128)(2,1)S(1)}, f16[1056,128]{1,0:T(8,128)(2,1)S(1)}, u32[]{:S(2)}, u32[]{:S(2)}) collective-permute-start(f16[1056,128]{1,0:T(8,128)(2,1)S(1)} %convert_element_type.348), channel_id=1, source_target_pairs={{0,4},{1,5},{2,6},{3,7},{4,0},{5,1},{6,2},{7,3},{8,12},{9,13},{10,... | collective-permute-start | bytes 811016 | tf_op jit(solution)/shard_map/up/ppermute | solution.py:292
  25.4 17.1 %collective-permute-start.3 = (f16[1056,128]{1,0:T(8,128)(2,1)S(1)}, f16[1056,128]{1,0:T(8,128)(2,1)S(1)}, u32[]{:S(2)}, u32[]{:S(2)}) collective-permute-start(f16[1056,128]{1,0:T(8,128)(2,1)S(1)} %convert_element_type.349), channel_id=1, source_target_pairs={{0,5},{1,4},{2,7},{3,6},{4,1},{5,0},{6,3},{7,2},{8,13},{9,12},{10,... | collective-permute-start | bytes 811016 | tf_op jit(solution)/shard_map/up/ppermute | solution.py:292
  27.2 5.2 %collective-permute-start.8 = (f16[528,128]{1,0:T(8,128)(2,1)S(1)}, f16[528,128]{1,0:T(8,128)(2,1)S(1)}, u32[]{:S(2)}, u32[]{:S(2)}) collective-permute-start(f16[528,128]{1,0:T(8,128)(2,1)S(1)} %pad_maximum_fusion.6), channel_id=1, source_target_pairs={{0,8},{1,9},{2,10},{3,11},{4,12},{5,13},{6,14},{7,15},{8,0},{9,1},... | collective-permute-start | bytes 405512 | tf_op jit(solution)/shard_map/outer/ppermute | solution.py:292
  32.7 5.4 %collective-permute-start.9 = (f16[272,128]{1,0:T(8,128)(2,1)S(1)}, f16[272,128]{1,0:T(8,128)(2,1)S(1)}, u32[]{:S(2)}, u32[]{:S(2)}) collective-permute-start(f16[272,128]{1,0:T(8,128)(2,1)S(1)} %pad_maximum_fusion.9), channel_id=1, source_target_pairs={{0,16},{1,17},{2,18},{3,19},{4,20},{5,21},{6,22},{7,23},{8,24},{9,... | collective-permute-start | bytes 208904 | tf_op jit(solution)/shard_map/outer/ppermute | solution.py:292
  38.9 19.6 %collective-permute-start.15 = (f16[1040,128]{1,0:T(8,128)(2,1)S(1)}, f16[1040,128]{1,0:T(8,128)(2,1)S(1)}, u32[]{:S(2)}, u32[]{:S(2)}) collective-permute-start(f16[1040,128]{1,0:T(8,128)(2,1)S(1)} %get-tuple-element.251), channel_id=1, source_target_pairs={{0,1},{1,0},{2,3},{3,2},{4,5},{5,4},{6,7},{7,6},{8,9},{9,8},{10,11... | collective-permute-start | bytes 798728 | tf_op jit(solution)/shard_map/down/ppermute | solution.py:292
  40.8 18.1 %collective-permute-start.16 = (f16[1040,128]{1,0:T(8,128)(2,1)S(1)}, f16[1040,128]{1,0:T(8,128)(2,1)S(1)}, u32[]{:S(2)}, u32[]{:S(2)}) collective-permute-start(f16[1040,128]{1,0:T(8,128)(2,1)S(1)} %get-tuple-element.250), channel_id=1, source_target_pairs={{0,4},{1,5},{2,6},{3,7},{4,0},{5,1},{6,2},{7,3},{8,12},{9,13},{10,... | collective-permute-start | bytes 798728 | tf_op jit(solution)/shard_map/down/ppermute | solution.py:292
  42.3 16.7 %collective-permute-start.17 = (f16[1040,128]{1,0:T(8,128)(2,1)S(1)}, f16[1040,128]{1,0:T(8,128)(2,1)S(1)}, u32[]{:S(2)}, u32[]{:S(2)}) collective-permute-start(f16[1040,128]{1,0:T(8,128)(2,1)S(1)} %get-tuple-element.249), channel_id=1, source_target_pairs={{0,5},{1,4},{2,7},{3,6},{4,1},{5,0},{6,3},{7,2},{8,13},{9,12},{10,... | collective-permute-start | bytes 798728 | tf_op jit(solution)/shard_map/down/ppermute | solution.py:292
  43.0 5.8 %collective-permute-start.10 = (f16[528,128]{1,0:T(8,128)(2,1)S(1)}, f16[528,128]{1,0:T(8,128)(2,1)S(1)}, u32[]{:S(2)}, u32[]{:S(2)}) collective-permute-start(f16[528,128]{1,0:T(8,128)(2,1)S(1)} %pad_maximum_fusion.7), channel_id=1, source_target_pairs={{0,8},{1,9},{2,10},{3,11},{4,12},{5,13},{6,14},{7,15},{8,0},{9,1},... | collective-permute-start | bytes 405512 | tf_op jit(solution)/shard_map/outer/ppermute | solution.py:292
  49.2 5.3 %collective-permute-start.11 = (f16[272,128]{1,0:T(8,128)(2,1)S(1)}, f16[272,128]{1,0:T(8,128)(2,1)S(1)}, u32[]{:S(2)}, u32[]{:S(2)}) collective-permute-start(f16[272,128]{1,0:T(8,128)(2,1)S(1)} %pad_maximum_fusion.10), channel_id=1, source_target_pairs={{0,16},{1,17},{2,18},{3,19},{4,20},{5,21},{6,22},{7,23},{8,24},{9,... | collective-permute-start | bytes 208904 | tf_op jit(solution)/shard_map/outer/ppermute | solution.py:292
  55.2 8.2 %collective-permute-start.12 = (f16[1040,128]{1,0:T(8,128)(2,1)S(1)}, f16[1040,128]{1,0:T(8,128)(2,1)S(1)}, u32[]{:S(2)}, u32[]{:S(2)}) collective-permute-start(f16[1040,128]{1,0:T(8,128)(2,1)S(1)} %get-tuple-element.248), channel_id=1, source_target_pairs={{0,1},{1,0},{2,3},{3,2},{4,5},{5,4},{6,7},{7,6},{8,9},{9,8},{10,11... | collective-permute-start | bytes 798728 | tf_op jit(solution)/shard_map/down/ppermute | solution.py:292
  57.0 6.5 %collective-permute-start.13 = (f16[1040,128]{1,0:T(8,128)(2,1)S(1)}, f16[1040,128]{1,0:T(8,128)(2,1)S(1)}, u32[]{:S(2)}, u32[]{:S(2)}) collective-permute-start(f16[1040,128]{1,0:T(8,128)(2,1)S(1)} %get-tuple-element.247), channel_id=1, source_target_pairs={{0,4},{1,5},{2,6},{3,7},{4,0},{5,1},{6,2},{7,3},{8,12},{9,13},{10,... | collective-permute-start | bytes 798728 | tf_op jit(solution)/shard_map/down/ppermute | solution.py:292
  58.4 7.6 %collective-permute-start.14 = (f16[1040,128]{1,0:T(8,128)(2,1)S(1)}, f16[1040,128]{1,0:T(8,128)(2,1)S(1)}, u32[]{:S(2)}, u32[]{:S(2)}) collective-permute-start(f16[1040,128]{1,0:T(8,128)(2,1)S(1)} %get-tuple-element.246), channel_id=1, source_target_pairs={{0,5},{1,4},{2,7},{3,6},{4,1},{5,0},{6,3},{7,2},{8,13},{9,12},{10,... | collective-permute-start | bytes 798728 | tf_op jit(solution)/shard_map/down/ppermute | solution.py:292
  59.3 2.0 %collective-permute-start.18 = (f16[2112,128]{1,0:T(8,128)(2,1)S(1)}, f16[2112,128]{1,0:T(8,128)(2,1)S(1)}, u32[]{:S(2)}, u32[]{:S(2)}) collective-permute-start(f16[2112,128]{1,0:T(8,128)(2,1)S(1)} %constant_dynamic-update-slice_fusion), channel_id=1, source_target_pairs={{0,2},{1,3},{2,0},{3,1},{4,6},{5,7},{6,4},{7,5},{8,10},{9,11},{10,... | collective-permute-start | bytes 1622024 | tf_op jit(solution)/shard_map/core_return/ppermute | solution.py:292
  66.5 1.8 %collective-permute-start.19 = (f16[1584,128]{1,0:T(8,128)(2,1)S(1)}, f16[1584,128]{1,0:T(8,128)(2,1)S(1)}, u32[]{:S(2)}, u32[]{:S(2)}) collective-permute-start(f16[1584,128]{1,0:T(8,128)(2,1)S(1)} %constant_dynamic-update-slice_fusion.8), channel_id=1, source_target_pairs={{0,2},{1,3},{2,0},{3,1},{4,6},{5,7},{6,4},{7,5},{8,10},{9,11},{10,... | collective-permute-start | bytes 1216520 | tf_op jit(solution)/shard_map/core_return/ppermute | solution.py:292
  70.1 1.5 %collective-permute-start.20 = (f16[528,128]{1,0:T(8,128)(2,1)S(1)}, f16[528,128]{1,0:T(8,128)(2,1)S(1)}, u32[]{:S(2)}, u32[]{:S(2)}) collective-permute-start(f16[528,128]{1,0:T(8,128)(2,1)S(1)} %pad_maximum_fusion.8), channel_id=1, source_target_pairs={{0,2},{1,3},{2,0},{3,1},{4,6},{5,7},{6,4},{7,5},{8,10},{9,11},{10,... | collective-permute-start | bytes 405512 | tf_op jit(solution)/shard_map/core_return/ppermute | solution.py:292

commit v3 on v2

--- a/solution.py
+++ b/solution.py
@@ -380,23 +380,23 @@
     def finish(c, state, inner, done, rounds):
         width = chunks[c][1] * HEAD_DIM
         own, other, e, factor, back = state
-        near, far, handed = {0: own}, {}, {0: encode([(other, e, factor)])}
-        for turn, blocks in enumerate(rounds):
+        for blocks in rounds:
             with jax.named_scope("core_return"):
-                parts = []
-                if turn:
-                    back = after(back, done[:1])
+                here = {r: back[r - 1] for r in blocks if r}
+                if done is not None:
+                    here = after(here, done[:1])
+                near, parts = {}, []
                 for r in blocks:
                     if r == 0:
-                        parts.append(handed[0])
+                        near[0] = own
+                        parts.append(encode([(other, e, factor)]))
                         continue
-                    m = back[r - 1]
-                    both = m[:-TAIL].reshape(2, 2, width, HEAD_DIM)
-                    near[r] = decode(both[:, 0], m[-TAIL:].astype(F32), 2)
-                    parts += [both[:, 1].reshape(-1, HEAD_DIM), m[-TAIL:]]
+                    both = here[r][:-TAIL].reshape(2, 2, width, HEAD_DIM)
+                    near[r] = decode(both[:, 0], here[r][-TAIL:].astype(F32), 2)
+                    parts += [both[:, 1].reshape(-1, HEAD_DIM), here[r][-TAIL:]]
                 forward = move(jnp.concatenate(parts, axis=0), CORE)
             with jax.named_scope("gradients"):
-                done = gradients(0, chunks[c], arrays, inner[0], {r: near[r] for r in blocks}, scale, done)
+                done = gradients(0, chunks[c], arrays, inner[0], near, scale, done)
                 pieces = forward.reshape(len(blocks), 2 * width + TAIL, HEAD_DIM)
                 far = {r: decode(p[:-TAIL], p[-TAIL:].astype(F32), 2) for r, p in zip(blocks, pieces)}
                 done = gradients(1, chunks[c], arrays, inner[1], far, scale, done)
@@ -413,9 +413,7 @@
         down, sent_z, last = exchange(c, after(ups[c], last))
         downs.append(down)
     for c in range(len(chunks)):
-        final = c == len(chunks) - 1
-        state = downs[c] if done is None else after(downs[c], done[:1])
-        done = finish(c, state, inner[c], done, ((0, 1, 2), (3,)) if final else ((0, 1, 2, 3),))
+        done = finish(c, downs[c], inner[c], done, ((0, 1, 2, 3),))
     return tuple(done)
 
 

time: 73.1 us -> 70.7 us (0.967)
  Pallas kernels: 23.7 us -> 21.8 us
    pallas_call x6 -> x4, Pallas kernels: 8.44 us -> 6.59 us  [gradients(): pl.pallas_call(functools.partial(gradient_kernel, scale, part, picked, ch...]
    ppermute x21 -> x20, starting transfers between devices: 27.3 us -> 27 us  [move(): return lax.ppermute(x, AXES, [(p, p ^ mask) for p in range(devices)])]
    ppermute x21 -> x20, waiting for transfers between devices: 13.7 us -> 13.7 us  [move(): return lax.ppermute(x, AXES, [(p, p ^ mask) for p in range(devices)])]
  transfers between devices with their start and end apart: 21 -> 20, of which waited for: 8 -> 8; matrix products, arithmetic and copies ran while one was open for 8% -> 8% of each run, Pallas kernels for 24% -> 24%
where the time goes in v3:
time: 70.7 us; the launch traced here: 70.6 us
  starting transfers between devices  27 us (38%)
  Pallas kernels  21.8 us (31%)
  waiting for transfers between devices  13.7 us (19%)
  other arithmetic  4.96 us (7%)
  between operations  1.88 us (3%)
  local copies, waits for them, and re-layouts  1.32 us (2%)
    ppermute x20, starting transfers between devices, move(): return lax.ppermute(x, AXES, [(p, p ^ mask) for p in range(devices)])  27 us
    ppermute x20, waiting for transfers between devices, move(): return lax.ppermute(x, AXES, [(p, p ^ mask) for p in range(devices)])  13.7 us
    pallas_call x4, Pallas kernels, inside(): pl.pallas_call(functools.partial(inside_kernel, scale, part, chunk), in_s...  7.2 us
    pallas_call x2, Pallas kernels, states(): pl.pallas_call(functools.partial(state_kernel, chunks), in_specs=[ANY] *...  6.93 us
    pallas_call x4, Pallas kernels, gradients(): pl.pallas_call(functools.partial(gradient_kernel, scale, part, picked, ch...  6.59 us
  transfers between devices with their start and end apart: 20, of which 8 were waited for; matrix products, arithmetic and copies ran while one was open for 8% of the time, Pallas kernels for 24%

profile of v3, /device:TPU:0, one launch (start us, length us, event | category | flops | bytes accessed | tf_op | source)
XLA Modules:
  0.0 70.6 jit_solution(399954379907255930)
XLA Ops:
  0.6 3.4 %group_states.3 = (f32[2080,128]{1,0:T(8,128)}, f32[2080,128]{1,0:T(8,128)}) custom-call(bf16[128,4096]{1,0:T(8,128)(2,1)} %q.7, bf16[128,4096]{1,0:T(8,128)(2,1)} %k.15, bf16[128,4096]{1,0:T(8,128)(2,1)} %v.15, bf16[128,4096]{1,0:T(8,128)(2,1)} %d.15), custom_call_target="tpu_custom_call" | custom-call | flops 268435456 | bytes 12582912 | tf_op jit(solution)/shard_map/states/group_states/pallas_call | solution.py:90
  4.1 0.5 collective-permute-start.4
  4.6 3.5 %group_states.2 = (f32[2080,128]{1,0:T(8,128)}, f32[2080,128]{1,0:T(8,128)}) custom-call(bf16[128,4096]{1,0:T(8,128)(2,1)} %q.7, bf16[128,4096]{1,0:T(8,128)(2,1)} %k.15, bf16[128,4096]{1,0:T(8,128)(2,1)} %v.15, bf16[128,4096]{1,0:T(8,128)(2,1)} %d.15), custom_call_target="tpu_custom_call" | custom-call | flops 268435456 | bytes 12582912 | tf_op jit(solution)/shard_map/states/group_states/pallas_call | solution.py:90
  8.4 0.4 join_groups.3
  8.9 3.0 %collective-permute-start.5 = (f16[1056,128]{1,0:T(8,128)(2,1)S(1)}, f16[1056,128]{1,0:T(8,128)(2,1)S(1)}, u32[]{:S(2)}, u32[]{:S(2)}) collective-permute-start(f16[1056,128]{1,0:T(8,128)(2,1)S(1)} %convert_element_type.350), channel_id=1, source_target_pairs={{0,1},{1,0},{2,3},{3,2},{4,5},{5,4},{6,7},{7,6},{8,9},{9,8},{10,11... | collective-permute-start | bytes 811016 | tf_op jit(solution)/shard_map/up/ppermute | solution.py:292
  11.9 1.6 %collective-permute-start.6 = (f16[1056,128]{1,0:T(8,128)(2,1)S(1)}, f16[1056,128]{1,0:T(8,128)(2,1)S(1)}, u32[]{:S(2)}, u32[]{:S(2)}) collective-permute-start(f16[1056,128]{1,0:T(8,128)(2,1)S(1)} %convert_element_type.351), channel_id=1, source_target_pairs={{0,4},{1,5},{2,6},{3,7},{4,0},{5,1},{6,2},{7,3},{8,12},{9,13},{10,... | collective-permute-start | bytes 811016 | tf_op jit(solution)/shard_map/up/ppermute | solution.py:292
  13.7 0.6 join_groups.2
  14.5 2.0 %collective-permute-start.1 = (f16[1056,128]{1,0:T(8,128)(2,1)S(1)}, f16[1056,128]{1,0:T(8,128)(2,1)S(1)}, u32[]{:S(2)}, u32[]{:S(2)}) collective-permute-start(f16[1056,128]{1,0:T(8,128)(2,1)S(1)} %convert_element_type.347), channel_id=1, source_target_pairs={{0,1},{1,0},{2,3},{3,2},{4,5},{5,4},{6,7},{7,6},{8,9},{9,8},{10,11... | collective-permute-start | bytes 811016 | tf_op jit(solution)/shard_map/up/ppermute | solution.py:292
  16.6 1.5 %collective-permute-start.2 = (f16[1056,128]{1,0:T(8,128)(2,1)S(1)}, f16[1056,128]{1,0:T(8,128)(2,1)S(1)}, u32[]{:S(2)}, u32[]{:S(2)}) collective-permute-start(f16[1056,128]{1,0:T(8,128)(2,1)S(1)} %convert_element_type.348), channel_id=1, source_target_pairs={{0,4},{1,5},{2,6},{3,7},{4,0},{5,1},{6,2},{7,3},{8,12},{9,13},{10,... | collective-permute-start | bytes 811016 | tf_op jit(solution)/shard_map/up/ppermute | solution.py:292
  18.1 1.8 %inside_group.4.inner = f32[4,3,128,256]{3,2,1,0:T(8,128)S(1)} custom-call(bf16[128,4096]{1,0:T(8,128)(2,1)S(1)} %copy-done.3, bf16[128,4096]{1,0:T(8,128)(2,1)S(1)} %copy-done, bf16[128,4096]{1,0:T(8,128)(2,1)S(1)} %copy-done.1, bf16[128,4096]{1,0:T(8,128)(2,1)S(1)} %copy-done.2), custom_call_target="tpu_custom_call" | custom-call | flops 201326592 | bytes 2621440 | tf_op jit(solution)/shard_map/inside/inside_group/pallas_call | solution.py:186
  19.9 1.8 %inside_group.5.inner = f32[4,3,128,256]{3,2,1,0:T(8,128)S(1)} custom-call(bf16[128,4096]{1,0:T(8,128)(2,1)S(1)} %copy-done.3, bf16[128,4096]{1,0:T(8,128)(2,1)S(1)} %copy-done, bf16[128,4096]{1,0:T(8,128)(2,1)S(1)} %copy-done.1, bf16[128,4096]{1,0:T(8,128)(2,1)S(1)} %copy-done.2), custom_call_target="tpu_custom_call" | custom-call | flops 201326592 | bytes 2621440 | tf_op jit(solution)/shard_map/inside/inside_group/pallas_call | solution.py:186
  21.7 1.8 %inside_group.6.inner = f32[4,3,128,256]{3,2,1,0:T(8,128)S(1)} custom-call(bf16[128,4096]{1,0:T(8,128)(2,1)S(1)} %copy-done.3, bf16[128,4096]{1,0:T(8,128)(2,1)S(1)} %copy-done, bf16[128,4096]{1,0:T(8,128)(2,1)S(1)} %copy-done.1, bf16[128,4096]{1,0:T(8,128)(2,1)S(1)} %copy-done.2), custom_call_target="tpu_custom_call" | custom-call | flops 201326592 | bytes 2621440 | tf_op jit(solution)/shard_map/inside/inside_group/pallas_call | solution.py:186
  23.5 1.8 %inside_group.7.inner = f32[4,3,128,256]{3,2,1,0:T(8,128)S(1)} custom-call(bf16[128,4096]{1,0:T(8,128)(2,1)S(1)} %copy-done.3, bf16[128,4096]{1,0:T(8,128)(2,1)S(1)} %copy-done, bf16[128,4096]{1,0:T(8,128)(2,1)S(1)} %copy-done.1, bf16[128,4096]{1,0:T(8,128)(2,1)S(1)} %copy-done.2), custom_call_target="tpu_custom_call" | custom-call | flops 201326592 | bytes 2621440 | tf_op jit(solution)/shard_map/inside/inside_group/pallas_call | solution.py:186
  25.3 0.9 %collective-permute-start.3 = (f16[1056,128]{1,0:T(8,128)(2,1)S(1)}, f16[1056,128]{1,0:T(8,128)(2,1)S(1)}, u32[]{:S(2)}, u32[]{:S(2)}) collective-permute-start(f16[1056,128]{1,0:T(8,128)(2,1)S(1)} %convert_element_type.349), channel_id=1, source_target_pairs={{0,5},{1,4},{2,7},{3,6},{4,1},{5,0},{6,3},{7,2},{8,13},{9,12},{10,... | collective-permute-start | bytes 811016 | tf_op jit(solution)/shard_map/up/ppermute | solution.py:292
  27.1 2.2 %collective-permute-start.8 = (f16[528,128]{1,0:T(8,128)(2,1)S(1)}, f16[528,128]{1,0:T(8,128)(2,1)S(1)}, u32[]{:S(2)}, u32[]{:S(2)}) collective-permute-start(f16[528,128]{1,0:T(8,128)(2,1)S(1)} %pad_maximum_fusion.6), channel_id=1, source_target_pairs={{0,8},{1,9},{2,10},{3,11},{4,12},{5,13},{6,14},{7,15},{8,0},{9,1},... | collective-permute-start | bytes 405512 | tf_op jit(solution)/shard_map/outer/ppermute | solution.py:292
  29.7 2.6 %collective-permute-done.8 = f16[528,128]{1,0:T(8,128)(2,1)S(1)} collective-permute-done((f16[528,128]{1,0:T(8,128)(2,1)S(1)}, f16[528,128]{1,0:T(8,128)(2,1)S(1)}, u32[]{:S(2)}, u32[]{:S(2)}) %collective-permute-start.8) | collective-permute-done | bytes 135200 | tf_op jit(solution)/shard_map/outer/ppermute | solution.py:292
  32.6 3.1 %collective-permute-start.9 = (f16[272,128]{1,0:T(8,128)(2,1)S(1)}, f16[272,128]{1,0:T(8,128)(2,1)S(1)}, u32[]{:S(2)}, u32[]{:S(2)}) collective-permute-start(f16[272,128]{1,0:T(8,128)(2,1)S(1)} %pad_maximum_fusion.8), channel_id=1, source_target_pairs={{0,16},{1,17},{2,18},{3,19},{4,20},{5,21},{6,22},{7,23},{8,24},{9,... | collective-permute-start | bytes 208904 | tf_op jit(solution)/shard_map/outer/ppermute | solution.py:292
  36.0 2.0 %collective-permute-done.9 = f16[272,128]{1,0:T(8,128)(2,1)S(1)} collective-permute-done((f16[272,128]{1,0:T(8,128)(2,1)S(1)}, f16[272,128]{1,0:T(8,128)(2,1)S(1)}, u32[]{:S(2)}, u32[]{:S(2)}) %collective-permute-start.9) | collective-permute-done | bytes 69664 | tf_op jit(solution)/shard_map/outer/ppermute | solution.py:292
  38.8 1.9 %collective-permute-start.15 = (f16[1040,128]{1,0:T(8,128)(2,1)S(1)}, f16[1040,128]{1,0:T(8,128)(2,1)S(1)}, u32[]{:S(2)}, u32[]{:S(2)}) collective-permute-start(f16[1040,128]{1,0:T(8,128)(2,1)S(1)} %get-tuple-element.230), channel_id=1, source_target_pairs={{0,1},{1,0},{2,3},{3,2},{4,5},{5,4},{6,7},{7,6},{8,9},{9,8},{10,11... | collective-permute-start | bytes 798728 | tf_op jit(solution)/shard_map/down/ppermute | solution.py:292
  40.7 1.5 %collective-permute-start.16 = (f16[1040,128]{1,0:T(8,128)(2,1)S(1)}, f16[1040,128]{1,0:T(8,128)(2,1)S(1)}, u32[]{:S(2)}, u32[]{:S(2)}) collective-permute-start(f16[1040,128]{1,0:T(8,128)(2,1)S(1)} %get-tuple-element.229), channel_id=1, source_target_pairs={{0,4},{1,5},{2,6},{3,7},{4,0},{5,1},{6,2},{7,3},{8,12},{9,13},{10,... | collective-permute-start | bytes 798728 | tf_op jit(solution)/shard_map/down/ppermute | solution.py:292
  43.0 2.0 %collective-permute-start.10 = (f16[528,128]{1,0:T(8,128)(2,1)S(1)}, f16[528,128]{1,0:T(8,128)(2,1)S(1)}, u32[]{:S(2)}, u32[]{:S(2)}) collective-permute-start(f16[528,128]{1,0:T(8,128)(2,1)S(1)} %pad_maximum_fusion.7), channel_id=1, source_target_pairs={{0,8},{1,9},{2,10},{3,11},{4,12},{5,13},{6,14},{7,15},{8,0},{9,1},... | collective-permute-start | bytes 405512 | tf_op jit(solution)/shard_map/outer/ppermute | solution.py:292
  45.3 3.5 %collective-permute-done.10 = f16[528,128]{1,0:T(8,128)(2,1)S(1)} collective-permute-done((f16[528,128]{1,0:T(8,128)(2,1)S(1)}, f16[528,128]{1,0:T(8,128)(2,1)S(1)}, u32[]{:S(2)}, u32[]{:S(2)}) %collective-permute-start.10) | collective-permute-done | bytes 135200 | tf_op jit(solution)/shard_map/outer/ppermute | solution.py:292
  49.1 2.7 %collective-permute-start.11 = (f16[272,128]{1,0:T(8,128)(2,1)S(1)}, f16[272,128]{1,0:T(8,128)(2,1)S(1)}, u32[]{:S(2)}, u32[]{:S(2)}) collective-permute-start(f16[272,128]{1,0:T(8,128)(2,1)S(1)} %pad_maximum_fusion.9), channel_id=1, source_target_pairs={{0,16},{1,17},{2,18},{3,19},{4,20},{5,21},{6,22},{7,23},{8,24},{9,... | collective-permute-start | bytes 208904 | tf_op jit(solution)/shard_map/outer/ppermute | solution.py:292
  52.1 2.3 %collective-permute-done.11 = f16[272,128]{1,0:T(8,128)(2,1)S(1)} collective-permute-done((f16[272,128]{1,0:T(8,128)(2,1)S(1)}, f16[272,128]{1,0:T(8,128)(2,1)S(1)}, u32[]{:S(2)}, u32[]{:S(2)}) %collective-permute-start.11) | collective-permute-done | bytes 69664 | tf_op jit(solution)/shard_map/outer/ppermute | solution.py:292
  55.2 1.7 %collective-permute-start.12 = (f16[1040,128]{1,0:T(8,128)(2,1)S(1)}, f16[1040,128]{1,0:T(8,128)(2,1)S(1)}, u32[]{:S(2)}, u32[]{:S(2)}) collective-permute-start(f16[1040,128]{1,0:T(8,128)(2,1)S(1)} %get-tuple-element.227), channel_id=1, source_target_pairs={{0,1},{1,0},{2,3},{3,2},{4,5},{5,4},{6,7},{7,6},{8,9},{9,8},{10,11... | collective-permute-start | bytes 798728 | tf_op jit(solution)/shard_map/down/ppermute | solution.py:292
  56.9 1.5 %collective-permute-start.13 = (f16[1040,128]{1,0:T(8,128)(2,1)S(1)}, f16[1040,128]{1,0:T(8,128)(2,1)S(1)}, u32[]{:S(2)}, u32[]{:S(2)}) collective-permute-start(f16[1040,128]{1,0:T(8,128)(2,1)S(1)} %get-tuple-element.226), channel_id=1, source_target_pairs={{0,4},{1,5},{2,6},{3,7},{4,0},{5,1},{6,2},{7,3},{8,12},{9,13},{10,... | collective-permute-start | bytes 798728 | tf_op jit(solution)/shard_map/down/ppermute | solution.py:292
  58.4 0.3 collective-permute-start.14
  59.5 1.6 %gradients.4 = (bf16[128,4096]{1,0:T(8,128)(2,1)}, bf16[128,4096]{1,0:T(8,128)(2,1)}, bf16[128,4096]{1,0:T(8,128)(2,1)}) custom-call(bf16[128,4096]{1,0:T(8,128)(2,1)S(1)} %copy-done, bf16[128,4096]{1,0:T(8,128)(2,1)S(1)} %copy-done.1, bf16[128,4096]{1,0:T(8,128)(2,1)S(1)} %copy-done.2, f32[4,3,128,256]{3,2,1,0:T(8,128)S(1)} %inside_group.5.inner, ...), custom_call_target="tpu_custom_call" | custom-call | flops 201326592 | bytes 2359296 | tf_op jit(solution)/shard_map/gradients/gradients/pallas_call | solution.py:234
  61.5 1.8 %gradients.5 = (bf16[128,4096]{1,0:T(8,128)(2,1)}, bf16[128,4096]{1,0:T(8,128)(2,1)}, bf16[128,4096]{1,0:T(8,128)(2,1)}) custom-call(bf16[128,4096]{1,0:T(8,128)(2,1)S(1)} %copy-done, bf16[128,4096]{1,0:T(8,128)(2,1)S(1)} %copy-done.1, bf16[128,4096]{1,0:T(8,128)(2,1)S(1)} %copy-done.2, ...), custom_call_target="tpu_custom_call", output_to_operand_aliasing={{0}: (8, {}), {1}: (9, {}), {2}: (10, {})} | custom-call | flops 201326592 | bytes 2359296 | tf_op jit(solution)/shard_map/gradients/gradients/pallas_call | solution.py:234
  63.4 2.6 %collective-permute-done.14 = f16[1040,128]{1,0:T(8,128)(2,1)S(1)} collective-permute-done((f16[1040,128]{1,0:T(8,128)(2,1)S(1)}, f16[1040,128]{1,0:T(8,128)(2,1)S(1)}, u32[]{:S(2)}, u32[]{:S(2)}) %collective-permute-start.14) | collective-permute-done | bytes 266272 | tf_op jit(solution)/shard_map/down/ppermute | solution.py:292
  66.7 1.6 %gradients.6 = (bf16[128,4096]{1,0:T(8,128)(2,1)}, bf16[128,4096]{1,0:T(8,128)(2,1)}, bf16[128,4096]{1,0:T(8,128)(2,1)}) custom-call(bf16[128,4096]{1,0:T(8,128)(2,1)S(1)} %copy-done, bf16[128,4096]{1,0:T(8,128)(2,1)S(1)} %copy-done.1, bf16[128,4096]{1,0:T(8,128)(2,1)S(1)} %copy-done.2, ...), custom_call_target="tpu_custom_call", output_to_operand_aliasing={{0}: (8, {}), {1}: (9, {}), {2}: (10, {})} | custom-call | flops 201326592 | bytes 2359296 | tf_op jit(solution)/shard_map/gradients/gradients/pallas_call | solution.py:234
  68.8 1.6 %gradients.7 = (bf16[128,4096]{1,0:T(8,128)(2,1)}, bf16[128,4096]{1,0:T(8,128)(2,1)}, bf16[128,4096]{1,0:T(8,128)(2,1)}) custom-call(bf16[128,4096]{1,0:T(8,128)(2,1)S(1)} %copy-done, bf16[128,4096]{1,0:T(8,128)(2,1)S(1)} %copy-done.1, bf16[128,4096]{1,0:T(8,128)(2,1)S(1)} %copy-done.2, ...), custom_call_target="tpu_custom_call", output_to_operand_aliasing={{0}: (8, {}), {1}: (9, {}), {2}: (10, {})} | custom-call | flops 201326592 | bytes 2359296 | tf_op jit(solution)/shard_map/gradients/gradients/pallas_call | solution.py:234
  (174 shorter events, 7.5 us)
Async XLA Ops:
  4.1 4.3 %copy-start.5 = (f32[2080,128]{1,0:T(8,128)S(1)}, f32[2080,128]{1,0:T(8,128)}, u32[]{:S(2)}) copy-start(f32[2080,128]{1,0:T(8,128)} %get-tuple-element.70.near) | copy-start | bytes 3194884
  4.1 4.3 %collective-permute-start.4 = (f32[2080,128]{1,0:T(8,128)}, f32[2080,128]{1,0:T(8,128)S(1)}, u32[]{:S(2)}, u32[]{:S(2)}) collective-permute-start(f32[2080,128]{1,0:T(8,128)} %get-tuple-element.71), channel_id=1, source_target_pairs={{0,2},{1,3},{2,0},{3,1},{4,6},{5,7},{6,4},{7,5},{8,10},{9,11},{10,... | collective-permute-start | bytes 3194888 | tf_op jit(solution)/shard_map/states/ppermute | solution.py:292
  8.1 5.6 %collective-permute-start = (f32[2080,128]{1,0:T(8,128)}, f32[2080,128]{1,0:T(8,128)S(1)}, u32[]{:S(2)}, u32[]{:S(2)}) collective-permute-start(f32[2080,128]{1,0:T(8,128)} %get-tuple-element.60), channel_id=1, source_target_pairs={{0,2},{1,3},{2,0},{3,1},{4,6},{5,7},{6,4},{7,5},{8,10},{9,11},{10,... | collective-permute-start | bytes 3194888 | tf_op jit(solution)/shard_map/states/ppermute | solution.py:292
  8.8 4.9 %copy-start.4 = (f32[2080,128]{1,0:T(8,128)S(1)}, f32[2080,128]{1,0:T(8,128)}, u32[]{:S(2)}) copy-start(f32[2080,128]{1,0:T(8,128)} %get-tuple-element.59.near) | copy-start | bytes 3194884
  8.9 16.4 %collective-permute-start.5 = (f16[1056,128]{1,0:T(8,128)(2,1)S(1)}, f16[1056,128]{1,0:T(8,128)(2,1)S(1)}, u32[]{:S(2)}, u32[]{:S(2)}) collective-permute-start(f16[1056,128]{1,0:T(8,128)(2,1)S(1)} %convert_element_type.350), channel_id=1, source_target_pairs={{0,1},{1,0},{2,3},{3,2},{4,5},{5,4},{6,7},{7,6},{8,9},{9,8},{10,11... | collective-permute-start | bytes 811016 | tf_op jit(solution)/shard_map/up/ppermute | solution.py:292
  11.9 14.4 %collective-permute-start.6 = (f16[1056,128]{1,0:T(8,128)(2,1)S(1)}, f16[1056,128]{1,0:T(8,128)(2,1)S(1)}, u32[]{:S(2)}, u32[]{:S(2)}) collective-permute-start(f16[1056,128]{1,0:T(8,128)(2,1)S(1)} %convert_element_type.351), channel_id=1, source_target_pairs={{0,4},{1,5},{2,6},{3,7},{4,0},{5,1},{6,2},{7,3},{8,12},{9,13},{10,... | collective-permute-start | bytes 811016 | tf_op jit(solution)/shard_map/up/ppermute | solution.py:292
  13.5 13.1 %collective-permute-start.7 = (f16[1056,128]{1,0:T(8,128)(2,1)S(1)}, f16[1056,128]{1,0:T(8,128)(2,1)S(1)}, u32[]{:S(2)}, u32[]{:S(2)}) collective-permute-start(f16[1056,128]{1,0:T(8,128)(2,1)S(1)} %convert_element_type.352), channel_id=1, source_target_pairs={{0,5},{1,4},{2,7},{3,6},{4,1},{5,0},{6,3},{7,2},{8,13},{9,12},{10,... | collective-permute-start | bytes 811016 | tf_op jit(solution)/shard_map/up/ppermute | solution.py:292
  13.7 4.3 %copy-start.2 = (bf16[128,4096]{1,0:T(8,128)(2,1)S(1)}, bf16[128,4096]{1,0:T(8,128)(2,1)}, u32[]{:S(2)}) copy-start(bf16[128,4096]{1,0:T(8,128)(2,1)} %d.15) | copy-start | bytes 3145732
  13.7 4.3 %copy-start.3 = (bf16[128,4096]{1,0:T(8,128)(2,1)S(1)}, bf16[128,4096]{1,0:T(8,128)(2,1)}, u32[]{:S(2)}) copy-start(bf16[128,4096]{1,0:T(8,128)(2,1)} %q.7) | copy-start | bytes 3145732
  14.4 3.7 %copy-start = (bf16[128,4096]{1,0:T(8,128)(2,1)S(1)}, bf16[128,4096]{1,0:T(8,128)(2,1)}, u32[]{:S(2)}) copy-start(bf16[128,4096]{1,0:T(8,128)(2,1)} %k.15) | copy-start | bytes 3145732
  14.4 3.7 %copy-start.1 = (bf16[128,4096]{1,0:T(8,128)(2,1)S(1)}, bf16[128,4096]{1,0:T(8,128)(2,1)}, u32[]{:S(2)}) copy-start(bf16[128,4096]{1,0:T(8,128)(2,1)} %v.15) | copy-start | bytes 3145732
  14.5 27.7 %collective-permute-start.1 = (f16[1056,128]{1,0:T(8,128)(2,1)S(1)}, f16[1056,128]{1,0:T(8,128)(2,1)S(1)}, u32[]{:S(2)}, u32[]{:S(2)}) collective-permute-start(f16[1056,128]{1,0:T(8,128)(2,1)S(1)} %convert_element_type.347), channel_id=1, source_target_pairs={{0,1},{1,0},{2,3},{3,2},{4,5},{5,4},{6,7},{7,6},{8,9},{9,8},{10,11... | collective-permute-start | bytes 811016 | tf_op jit(solution)/shard_map/up/ppermute | solution.py:292
  16.6 25.8 %collective-permute-start.2 = (f16[1056,128]{1,0:T(8,128)(2,1)S(1)}, f16[1056,128]{1,0:T(8,128)(2,1)S(1)}, u32[]{:S(2)}, u32[]{:S(2)}) collective-permute-start(f16[1056,128]{1,0:T(8,128)(2,1)S(1)} %convert_element_type.348), channel_id=1, source_target_pairs={{0,4},{1,5},{2,6},{3,7},{4,0},{5,1},{6,2},{7,3},{8,12},{9,13},{10,... | collective-permute-start | bytes 811016 | tf_op jit(solution)/shard_map/up/ppermute | solution.py:292
  25.3 17.1 %collective-permute-start.3 = (f16[1056,128]{1,0:T(8,128)(2,1)S(1)}, f16[1056,128]{1,0:T(8,128)(2,1)S(1)}, u32[]{:S(2)}, u32[]{:S(2)}) collective-permute-start(f16[1056,128]{1,0:T(8,128)(2,1)S(1)} %convert_element_type.349), channel_id=1, source_target_pairs={{0,5},{1,4},{2,7},{3,6},{4,1},{5,0},{6,3},{7,2},{8,13},{9,12},{10,... | collective-permute-start | bytes 811016 | tf_op jit(solution)/shard_map/up/ppermute | solution.py:292
  27.1 5.2 %collective-permute-start.8 = (f16[528,128]{1,0:T(8,128)(2,1)S(1)}, f16[528,128]{1,0:T(8,128)(2,1)S(1)}, u32[]{:S(2)}, u32[]{:S(2)}) collective-permute-start(f16[528,128]{1,0:T(8,128)(2,1)S(1)} %pad_maximum_fusion.6), channel_id=1, source_target_pairs={{0,8},{1,9},{2,10},{3,11},{4,12},{5,13},{6,14},{7,15},{8,0},{9,1},... | collective-permute-start | bytes 405512 | tf_op jit(solution)/shard_map/outer/ppermute | solution.py:292
  32.6 5.4 %collective-permute-start.9 = (f16[272,128]{1,0:T(8,128)(2,1)S(1)}, f16[272,128]{1,0:T(8,128)(2,1)S(1)}, u32[]{:S(2)}, u32[]{:S(2)}) collective-permute-start(f16[272,128]{1,0:T(8,128)(2,1)S(1)} %pad_maximum_fusion.8), channel_id=1, source_target_pairs={{0,16},{1,17},{2,18},{3,19},{4,20},{5,21},{6,22},{7,23},{8,24},{9,... | collective-permute-start | bytes 208904 | tf_op jit(solution)/shard_map/outer/ppermute | solution.py:292
  38.8 19.6 %collective-permute-start.15 = (f16[1040,128]{1,0:T(8,128)(2,1)S(1)}, f16[1040,128]{1,0:T(8,128)(2,1)S(1)}, u32[]{:S(2)}, u32[]{:S(2)}) collective-permute-start(f16[1040,128]{1,0:T(8,128)(2,1)S(1)} %get-tuple-element.230), channel_id=1, source_target_pairs={{0,1},{1,0},{2,3},{3,2},{4,5},{5,4},{6,7},{7,6},{8,9},{9,8},{10,11... | collective-permute-start | bytes 798728 | tf_op jit(solution)/shard_map/down/ppermute | solution.py:292
  40.7 18.1 %collective-permute-start.16 = (f16[1040,128]{1,0:T(8,128)(2,1)S(1)}, f16[1040,128]{1,0:T(8,128)(2,1)S(1)}, u32[]{:S(2)}, u32[]{:S(2)}) collective-permute-start(f16[1040,128]{1,0:T(8,128)(2,1)S(1)} %get-tuple-element.229), channel_id=1, source_target_pairs={{0,4},{1,5},{2,6},{3,7},{4,0},{5,1},{6,2},{7,3},{8,12},{9,13},{10,... | collective-permute-start | bytes 798728 | tf_op jit(solution)/shard_map/down/ppermute | solution.py:292
  42.2 16.7 %collective-permute-start.17 = (f16[1040,128]{1,0:T(8,128)(2,1)S(1)}, f16[1040,128]{1,0:T(8,128)(2,1)S(1)}, u32[]{:S(2)}, u32[]{:S(2)}) collective-permute-start(f16[1040,128]{1,0:T(8,128)(2,1)S(1)} %get-tuple-element.228), channel_id=1, source_target_pairs={{0,5},{1,4},{2,7},{3,6},{4,1},{5,0},{6,3},{7,2},{8,13},{9,12},{10,... | collective-permute-start | bytes 798728 | tf_op jit(solution)/shard_map/down/ppermute | solution.py:292
  43.0 5.8 %collective-permute-start.10 = (f16[528,128]{1,0:T(8,128)(2,1)S(1)}, f16[528,128]{1,0:T(8,128)(2,1)S(1)}, u32[]{:S(2)}, u32[]{:S(2)}) collective-permute-start(f16[528,128]{1,0:T(8,128)(2,1)S(1)} %pad_maximum_fusion.7), channel_id=1, source_target_pairs={{0,8},{1,9},{2,10},{3,11},{4,12},{5,13},{6,14},{7,15},{8,0},{9,1},... | collective-permute-start | bytes 405512 | tf_op jit(solution)/shard_map/outer/ppermute | solution.py:292
  49.1 5.3 %collective-permute-start.11 = (f16[272,128]{1,0:T(8,128)(2,1)S(1)}, f16[272,128]{1,0:T(8,128)(2,1)S(1)}, u32[]{:S(2)}, u32[]{:S(2)}) collective-permute-start(f16[272,128]{1,0:T(8,128)(2,1)S(1)} %pad_maximum_fusion.9), channel_id=1, source_target_pairs={{0,16},{1,17},{2,18},{3,19},{4,20},{5,21},{6,22},{7,23},{8,24},{9,... | collective-permute-start | bytes 208904 | tf_op jit(solution)/shard_map/outer/ppermute | solution.py:292
  55.2 8.2 %collective-permute-start.12 = (f16[1040,128]{1,0:T(8,128)(2,1)S(1)}, f16[1040,128]{1,0:T(8,128)(2,1)S(1)}, u32[]{:S(2)}, u32[]{:S(2)}) collective-permute-start(f16[1040,128]{1,0:T(8,128)(2,1)S(1)} %get-tuple-element.227), channel_id=1, source_target_pairs={{0,1},{1,0},{2,3},{3,2},{4,5},{5,4},{6,7},{7,6},{8,9},{9,8},{10,11... | collective-permute-start | bytes 798728 | tf_op jit(solution)/shard_map/down/ppermute | solution.py:292
  56.9 6.4 %collective-permute-start.13 = (f16[1040,128]{1,0:T(8,128)(2,1)S(1)}, f16[1040,128]{1,0:T(8,128)(2,1)S(1)}, u32[]{:S(2)}, u32[]{:S(2)}) collective-permute-start(f16[1040,128]{1,0:T(8,128)(2,1)S(1)} %get-tuple-element.226), channel_id=1, source_target_pairs={{0,4},{1,5},{2,6},{3,7},{4,0},{5,1},{6,2},{7,3},{8,12},{9,13},{10,... | collective-permute-start | bytes 798728 | tf_op jit(solution)/shard_map/down/ppermute | solution.py:292
  58.4 7.6 %collective-permute-start.14 = (f16[1040,128]{1,0:T(8,128)(2,1)S(1)}, f16[1040,128]{1,0:T(8,128)(2,1)S(1)}, u32[]{:S(2)}, u32[]{:S(2)}) collective-permute-start(f16[1040,128]{1,0:T(8,128)(2,1)S(1)} %get-tuple-element.225), channel_id=1, source_target_pairs={{0,5},{1,4},{2,7},{3,6},{4,1},{5,0},{6,3},{7,2},{8,13},{9,12},{10,... | collective-permute-start | bytes 798728 | tf_op jit(solution)/shard_map/down/ppermute | solution.py:292
  59.3 2.0 %collective-permute-start.18 = (f16[2112,128]{1,0:T(8,128)(2,1)S(1)}, f16[2112,128]{1,0:T(8,128)(2,1)S(1)}, u32[]{:S(2)}, u32[]{:S(2)}) collective-permute-start(f16[2112,128]{1,0:T(8,128)(2,1)S(1)} %constant_dynamic-update-slice_fusion), channel_id=1, source_target_pairs={{0,2},{1,3},{2,0},{3,1},{4,6},{5,7},{6,4},{7,5},{8,10},{9,11},{10,... | collective-permute-start | bytes 1622024 | tf_op jit(solution)/shard_map/core_return/ppermute | solution.py:292
  66.5 2.0 %collective-permute-start.19 = (f16[2112,128]{1,0:T(8,128)(2,1)S(1)}, f16[2112,128]{1,0:T(8,128)(2,1)S(1)}, u32[]{:S(2)}, u32[]{:S(2)}) collective-permute-start(f16[2112,128]{1,0:T(8,128)(2,1)S(1)} %constant_dynamic-update-slice_fusion.8), channel_id=1, source_target_pairs={{0,2},{1,3},{2,0},{3,1},{4,6},{5,7},{6,4},{7,5},{8,10},{9,11},{10,... | collective-permute-start | bytes 1622024 | tf_op jit(solution)/shard_map/core_return/ppermute | solution.py:292

commit v4 on v3

--- a/solution.py
+++ b/solution.py
@@ -39,105 +39,106 @@
     return pl.multiple_of((8 * first + ((my_place() & 7) ^ mask) * count) * HEAD_DIM, HEAD_DIM)
 
 
-def state_kernel(chunks, q, k, v, d, *rest):
-    outs, (held, in_sems, out_sems) = rest[: 2 * len(chunks)], rest[-3:]
-    found = rest[2 * len(chunks) : -3]
-    copies, leaving = {}, []
-    for c, (first, count) in enumerate(chunks):
-        cols = pl.ds(8 * first * HEAD_DIM, 8 * count * HEAD_DIM)
+def state_kernel(chunk, q, k, v, d, mine, sent, held, found, in_sems, out_sems):
+    first, count = chunk
+    width = count * HEAD_DIM
+    place = my_place()
+    here = 2 * ((place >> 2) & 1) + (place & 1)
+    arriving, leaving = {}, []
+    for half in (1, 0):
+        core = ((place >> 1) & 1) ^ half
         for i, ref in ((1, k), (2, v), (3, d), (0, q)):
-            copies[c, i] = pltpu.make_async_copy(ref.at[:, cols], held.at[i, :, cols], in_sems.at[c, i])
-            copies[c, i].start()
-
-    def leave(c, slot, begin, size, sem):
-        rows = pl.ds(begin, size)
-        copy = pltpu.make_async_copy(found[c].at[slot, rows], outs[2 * c + slot].at[rows], out_sems.at[c, sem])
-        copy.start()
-        leaving.append(copy)
-
-    for c, (first, count) in enumerate(chunks):
-        width = count * HEAD_DIM
-        peaks = [jnp.zeros((8, HEAD_DIM), F32)] * 2
+            for x in range(2):
+                begin = pl.multiple_of((8 * first + (4 * x + 2 * core) * count) * HEAD_DIM, HEAD_DIM)
+                source = ref.at[:, pl.ds(begin, 2 * width)]
+                to = held.at[half, i, :, pl.ds(2 * x * width, 2 * width)]
+                arriving[half, i, x] = pltpu.make_async_copy(source, to, in_sems.at[half, i, x])
+                arriving[half, i, x].start()
+    for half in (1, 0):
+        out = found if half else mine
+        exps = []
         for kind, (left, right) in enumerate(((2, 1), (3, 0))):
-            copies[c, left].wait()
-            copies[c, right].wait()
-            for b in (4, 5, 6, 7, 0, 1, 2, 3):
-                begin = block_columns(CUBE[b], chunks[c])
+            for x in range(2):
+                arriving[half, left, x].wait()
+                arriving[half, right, x].wait()
+            peaks = jnp.zeros((8, HEAD_DIM), F32)
+            for b in range(4):
                 for head in range(count):
-                    cols = pl.ds(pl.multiple_of(begin + head * HEAD_DIM, HEAD_DIM), HEAD_DIM)
-                    state = dot(held[left, :, cols], held[right, :, cols], TN)
-                    start = (b % 4 * 2 + kind) * width + head * HEAD_DIM
-                    found[c][b // 4, start : start + HEAD_DIM, :] = state
+                    cols = pl.ds(pl.multiple_of(((here ^ b) * count + head) * HEAD_DIM, HEAD_DIM), HEAD_DIM)
+                    state = dot(held[half, left, :, cols], held[half, right, :, cols], TN)
+                    start = (kind * 4 + b) * width + head * HEAD_DIM
+                    out[start : start + HEAD_DIM, :] = state
                     peak = jnp.max(jnp.abs(state).reshape(HEAD_DIM // 8, 8, HEAD_DIM), axis=0)
-                    peaks[kind] = jnp.maximum(peaks[kind], peak)
-                if kind == 1:
-                    leave(c, b // 4, b % 4 * 2 * width, 2 * width, b)
-        for kind in range(2):
-            exps = exponents(jnp.full((8, HEAD_DIM), jnp.max(peaks[kind]), F32))
-            for slot in range(2):
-                row = 8 * width + kind * 8
-                found[c][slot, row : row + 8, :] = exps
-                found[c][slot, row + TAIL : row + TAIL + 8, :] = jnp.exp2(TOP - exps)
-        for slot in range(2):
-            leave(c, slot, 8 * width, 2 * TAIL, 8 + slot)
+                    peaks = jnp.maximum(peaks, peak)
+            rows = pl.ds(4 * kind * width, 4 * width)
+            if half:
+                leaving.append(pltpu.make_async_copy(out.at[rows], sent.at[rows], out_sems.at[kind]))
+                leaving[-1].start()
+            for shift in (4, 2, 1):
+                peaks = jnp.maximum(peaks, pltpu.roll(peaks, shift, 0))
+            exps.append(peaks)
+        for kind, peaks in enumerate(exps):
+            both = exponents(jnp.broadcast_to(jnp.max(peaks, axis=1, keepdims=True), peaks.shape))
+            row = 8 * width + kind * 8
+            out[row : row + 8, :] = both
+            out[row + TAIL : row + TAIL + 8, :] = jnp.exp2(TOP - both)
+        rows = pl.ds(8 * width, 2 * TAIL)
+        if half:
+            leaving.append(pltpu.make_async_copy(out.at[rows], sent.at[rows], out_sems.at[2]))
+            leaving[-1].start()
     for copy in leaving:
         copy.wait()
 
 
-def states(arrays, chunks):
+def states(arrays, chunk):
     rows, columns = arrays[0].shape
-    flats = [jax.ShapeDtypeStruct((8 * n * HEAD_DIM + 2 * TAIL, HEAD_DIM), F32) for _, n in chunks]
+    width = chunk[1] * HEAD_DIM
+    flat = jax.ShapeDtypeStruct((8 * width + 2 * TAIL, HEAD_DIM), F32)
     return pl.pallas_call(
-        functools.partial(state_kernel, chunks),
+        functools.partial(state_kernel, chunk),
         in_specs=[ANY] * 4,
-        out_specs=(ANY,) * (2 * len(chunks)),
-        out_shape=tuple(flat for flat in flats for _ in range(2)),
-        scratch_shapes=[pltpu.VMEM((2,) + flat.shape, F32) for flat in flats]
-        + [
-            pltpu.VMEM((4, rows, columns), BF16),
-            pltpu.SemaphoreType.DMA((len(chunks), 4)),
-            pltpu.SemaphoreType.DMA((len(chunks), 10)),
+        out_specs=(VMEM, ANY),
+        out_shape=(flat, flat),
+        scratch_shapes=[
+            pltpu.VMEM((2, 4, rows, 4 * width), BF16),
+            pltpu.VMEM(flat.shape, F32),
+            pltpu.SemaphoreType.DMA((2, 4, 2)),
+            pltpu.SemaphoreType.DMA((3,)),
         ],
-        compiler_params=pltpu.CompilerParams(vmem_limit_bytes=56 << 20),
+        compiler_params=pltpu.CompilerParams(vmem_limit_bytes=16 << 20),
         cost_estimate=pl.CostEstimate(
-            flops=4 * rows * columns * HEAD_DIM, bytes_accessed=24 * rows * columns, transcendentals=0
+            flops=32 * rows * width * HEAD_DIM, bytes_accessed=128 * rows * width, transcendentals=0
         ),
         name="group_states",
     )(*arrays)
 
 
 def join_kernel(near, away, own, bound, *rest):
-    messages, both, sems = rest[:3], rest[3], rest[4]
+    messages, peer, sems = rest[:3], rest[3], rest[4]
     width = (near.shape[0] - 2 * TAIL) // 8
-    copies = []
-    for i, ref in enumerate((near, away)):
-        pieces = []
-        for r in range(4):
-            rows = pl.ds(2 * width * r, 2 * width + (2 * TAIL if r == 3 else 0))
-            pieces.append(pltpu.make_async_copy(ref.at[rows], both.at[i, rows], sems.at[i, r]))
-        copies.append(pieces)
-    for r in (3, 0, 1, 2):
-        for i in range(2):
-            copies[i][r].start()
-    for i in range(2):
-        copies[i][3].wait()
-        exps = both[i, 8 * width : 8 * width + TAIL, :]
-        for message in messages:
-            message[4 * width + i * TAIL : 4 * width + (i + 1) * TAIL, :] = exps
-        bound[...] = jnp.exp2(exps) if i == 0 else bound[...] + jnp.exp2(exps)
-    for r in range(4):
-        for i in range(2):
-            if r < 3:
-                copies[i][r].wait()
-            for kind in range(2):
-                start = (r * 2 + kind) * width
-                block = both[i, start : start + width, :]
+    copies = {}
+    for kind in (1, 0):
+        rows = pl.ds(4 * kind * width, 4 * width + 2 * TAIL * kind)
+        copies[kind] = pltpu.make_async_copy(away.at[rows], peer.at[rows], sems.at[kind])
+        copies[kind].start()
+    for kind in (1, 0):
+        for i, ref in enumerate((near, peer)):
+            if i:
+                copies[kind].wait()
+            if kind == 1:
+                exps = ref[8 * width : 8 * width + TAIL, :]
+                for message in messages:
+                    message[4 * width + i * TAIL : 4 * width + (i + 1) * TAIL, :] = exps
+                bound[...] = jnp.exp2(exps) if i == 0 else bound[...] + jnp.exp2(exps)
+            for r in range(4):
+                start = (kind * 4 + r) * width
+                block = ref[start : start + width, :]
                 if r == 0:
                     own[i, kind] = block
                 else:
                     row = 8 * width + TAIL + 8 * kind
                     to = (2 * i + kind) * width
-                    messages[r - 1][to : to + width, :] = block * both[i, row : row + 1, :]
+                    messages[r - 1][to : to + width, :] = block * ref[row : row + 1, :]
 
 
 def join(mine, peer):
@@ -145,7 +146,7 @@
     message = jax.ShapeDtypeStruct((4 * width + 2 * TAIL, HEAD_DIM), F32)
     return pl.pallas_call(
         join_kernel,
-        in_specs=[ANY, ANY],
+        in_specs=[VMEM, ANY],
         out_specs=(VMEM,) * 5,
         out_shape=(
             jax.ShapeDtypeStruct((2, 2, width, HEAD_DIM), F32),
@@ -154,7 +155,7 @@
             message,
             message,
         ),
-        scratch_shapes=[pltpu.VMEM((2,) + mine.shape, F32), pltpu.SemaphoreType.DMA((2, 4))],
+        scratch_shapes=[pltpu.VMEM(mine.shape, F32), pltpu.SemaphoreType.DMA((2,))],
         compiler_params=pltpu.CompilerParams(vmem_limit_bytes=16 << 20),
         cost_estimate=pl.CostEstimate(
             flops=8 * width * HEAD_DIM, bytes_accessed=128 * width * HEAD_DIM, transcendentals=0
@@ -302,7 +303,8 @@
 
 
     with jax.named_scope("states"):
-        found = [x for chunk in chunks for x in states(arrays, (chunk,))]
+        placed = tuple(pltpu.with_memory_space_constraint(a, pltpu.HBM) for a in arrays)
+        found = [x for chunk in chunks for x in states(placed, chunk)]
         peers = [move(sent, CORE) for sent in found[1::2]]
 
     def send_up(mine, peer):

time: 70.7 us -> 70 us (0.990)
  Pallas kernels: 21.8 us -> 20.9 us
    pallas_call x4, Pallas kernels: 7.97 us -> 7.06 us  [the longest x2 5.36 us: states(): pl.pallas_call(functools.partial(state_kernel, chunk), in_specs=[ANY] * 4...]
where the time goes in v4:
time: 70 us; the launch traced here: 69.8 us
  starting transfers between devices  27.1 us (39%)
  Pallas kernels  20.9 us (30%)
  waiting for transfers between devices  13.7 us (20%)
  other arithmetic  4.97 us (7%)
  between operations  1.86 us (3%)
  local copies, waits for them, and re-layouts  1.31 us (2%)
    ppermute x20, starting transfers between devices, move(): return lax.ppermute(x, AXES, [(p, p ^ mask) for p in range(devices)])  27.1 us
    ppermute x20, waiting for transfers between devices, move(): return lax.ppermute(x, AXES, [(p, p ^ mask) for p in range(devices)])  13.7 us
    pallas_call x4, Pallas kernels, inside(): pl.pallas_call(functools.partial(inside_kernel, scale, part, chunk), in_s...  7.2 us
    pallas_call x4, Pallas kernels, gradients(): pl.pallas_call(functools.partial(gradient_kernel, scale, part, picked, ch...  6.6 us
    pallas_call x2, Pallas kernels, states(): pl.pallas_call(functools.partial(state_kernel, chunk), in_specs=[ANY] * 4...  5.36 us
    pallas_call x2, Pallas kernels, join(): pl.pallas_call(join_kernel, in_specs=[VMEM, ANY], out_specs=(VMEM,) * 5,...  1.7 us
  transfers between devices with their start and end apart: 20, of which 8 were waited for; matrix products, arithmetic and copies ran while one was open for 8% of the time, Pallas kernels for 24%

profile of v4, /device:TPU:0, one launch (start us, length us, event | category | flops | bytes accessed | tf_op | source)
XLA Modules:
  0.0 69.8 jit_solution(10468001981197120767)
XLA Ops:
  0.6 2.7 %group_states.3 = (f32[2080,128]{1,0:T(8,128)S(1)}, f32[2080,128]{1,0:T(8,128)}) custom-call(bf16[128,4096]{1,0:T(8,128)(2,1)} %q.7, bf16[128,4096]{1,0:T(8,128)(2,1)} %k.15, bf16[128,4096]{1,0:T(8,128)(2,1)} %v.15, bf16[128,4096]{1,0:T(8,128)(2,1)} %d.15), custom_call_target="tpu_custom_call" | custom-call | flops 134217728 | bytes 4194304 | tf_op jit(solution)/shard_map/states/group_states/pallas_call | solution.py:97
  3.3 0.5 collective-permute-start.4
  3.8 2.7 %group_states.2 = (f32[2080,128]{1,0:T(8,128)S(1)}, f32[2080,128]{1,0:T(8,128)}) custom-call(bf16[128,4096]{1,0:T(8,128)(2,1)} %q.7, bf16[128,4096]{1,0:T(8,128)(2,1)} %k.15, bf16[128,4096]{1,0:T(8,128)(2,1)} %v.15, bf16[128,4096]{1,0:T(8,128)(2,1)} %d.15), custom_call_target="tpu_custom_call" | custom-call | flops 134217728 | bytes 4194304 | tf_op jit(solution)/shard_map/states/group_states/pallas_call | solution.py:97
  6.7 1.3 %join_groups.3 = (f32[2,2,256,128]{3,2,1,0:T(8,128)S(1)}, f32[16,128]{1,0:T(8,128)S(1)}, f32[1056,128]{1,0:T(8,128)S(1)}, f32[1056,128]{1,0:T(8,128)S(1)}, f32[1056,128]{1,0:T(8,128)S(1)}) custom-call(f32[2080,128]{1,0:T(8,128)S(1)} %get-tuple-element.70.near, f32[2080,128]{1,0:T(8,128)} %collective-permute-done.4.away), custom_call_target="tpu_custom_call" | custom-call | flops 262144 | bytes 4194304 | tf_op jit(solution)/shard_map/up/join_groups/pallas_call | solution.py:147
  8.0 3.0 %collective-permute-start.5 = (f16[1056,128]{1,0:T(8,128)(2,1)S(1)}, f16[1056,128]{1,0:T(8,128)(2,1)S(1)}, u32[]{:S(2)}, u32[]{:S(2)}) collective-permute-start(f16[1056,128]{1,0:T(8,128)(2,1)S(1)} %convert_element_type.350), channel_id=1, source_target_pairs={{0,1},{1,0},{2,3},{3,2},{4,5},{5,4},{6,7},{7,6},{8,9},{9,8},{10,11... | collective-permute-start | bytes 811016 | tf_op jit(solution)/shard_map/up/ppermute | solution.py:293
  11.1 1.6 %collective-permute-start.6 = (f16[1056,128]{1,0:T(8,128)(2,1)S(1)}, f16[1056,128]{1,0:T(8,128)(2,1)S(1)}, u32[]{:S(2)}, u32[]{:S(2)}) collective-permute-start(f16[1056,128]{1,0:T(8,128)(2,1)S(1)} %convert_element_type.351), channel_id=1, source_target_pairs={{0,4},{1,5},{2,6},{3,7},{4,0},{5,1},{6,2},{7,3},{8,12},{9,13},{10,... | collective-permute-start | bytes 811016 | tf_op jit(solution)/shard_map/up/ppermute | solution.py:293
  13.0 0.4 join_groups.2
  13.6 2.0 %collective-permute-start.1 = (f16[1056,128]{1,0:T(8,128)(2,1)S(1)}, f16[1056,128]{1,0:T(8,128)(2,1)S(1)}, u32[]{:S(2)}, u32[]{:S(2)}) collective-permute-start(f16[1056,128]{1,0:T(8,128)(2,1)S(1)} %convert_element_type.347), channel_id=1, source_target_pairs={{0,1},{1,0},{2,3},{3,2},{4,5},{5,4},{6,7},{7,6},{8,9},{9,8},{10,11... | collective-permute-start | bytes 811016 | tf_op jit(solution)/shard_map/up/ppermute | solution.py:293
  15.6 1.5 %collective-permute-start.2 = (f16[1056,128]{1,0:T(8,128)(2,1)S(1)}, f16[1056,128]{1,0:T(8,128)(2,1)S(1)}, u32[]{:S(2)}, u32[]{:S(2)}) collective-permute-start(f16[1056,128]{1,0:T(8,128)(2,1)S(1)} %convert_element_type.348), channel_id=1, source_target_pairs={{0,4},{1,5},{2,6},{3,7},{4,0},{5,1},{6,2},{7,3},{8,12},{9,13},{10,... | collective-permute-start | bytes 811016 | tf_op jit(solution)/shard_map/up/ppermute | solution.py:293
  17.1 1.8 %inside_group.4.inner = f32[4,3,128,256]{3,2,1,0:T(8,128)S(1)} custom-call(bf16[128,4096]{1,0:T(8,128)(2,1)S(1)} %copy-done.3, bf16[128,4096]{1,0:T(8,128)(2,1)S(1)} %copy-done, bf16[128,4096]{1,0:T(8,128)(2,1)S(1)} %copy-done.1, bf16[128,4096]{1,0:T(8,128)(2,1)S(1)} %copy-done.2), custom_call_target="tpu_custom_call" | custom-call | flops 201326592 | bytes 2621440 | tf_op jit(solution)/shard_map/inside/inside_group/pallas_call | solution.py:187
  18.9 1.8 %inside_group.5.inner = f32[4,3,128,256]{3,2,1,0:T(8,128)S(1)} custom-call(bf16[128,4096]{1,0:T(8,128)(2,1)S(1)} %copy-done.3, bf16[128,4096]{1,0:T(8,128)(2,1)S(1)} %copy-done, bf16[128,4096]{1,0:T(8,128)(2,1)S(1)} %copy-done.1, bf16[128,4096]{1,0:T(8,128)(2,1)S(1)} %copy-done.2), custom_call_target="tpu_custom_call" | custom-call | flops 201326592 | bytes 2621440 | tf_op jit(solution)/shard_map/inside/inside_group/pallas_call | solution.py:187
  20.7 1.8 %inside_group.6.inner = f32[4,3,128,256]{3,2,1,0:T(8,128)S(1)} custom-call(bf16[128,4096]{1,0:T(8,128)(2,1)S(1)} %copy-done.3, bf16[128,4096]{1,0:T(8,128)(2,1)S(1)} %copy-done, bf16[128,4096]{1,0:T(8,128)(2,1)S(1)} %copy-done.1, bf16[128,4096]{1,0:T(8,128)(2,1)S(1)} %copy-done.2), custom_call_target="tpu_custom_call" | custom-call | flops 201326592 | bytes 2621440 | tf_op jit(solution)/shard_map/inside/inside_group/pallas_call | solution.py:187
  22.5 1.8 %inside_group.7.inner = f32[4,3,128,256]{3,2,1,0:T(8,128)S(1)} custom-call(bf16[128,4096]{1,0:T(8,128)(2,1)S(1)} %copy-done.3, bf16[128,4096]{1,0:T(8,128)(2,1)S(1)} %copy-done, bf16[128,4096]{1,0:T(8,128)(2,1)S(1)} %copy-done.1, bf16[128,4096]{1,0:T(8,128)(2,1)S(1)} %copy-done.2), custom_call_target="tpu_custom_call" | custom-call | flops 201326592 | bytes 2621440 | tf_op jit(solution)/shard_map/inside/inside_group/pallas_call | solution.py:187
  24.4 1.1 %collective-permute-start.3 = (f16[1056,128]{1,0:T(8,128)(2,1)S(1)}, f16[1056,128]{1,0:T(8,128)(2,1)S(1)}, u32[]{:S(2)}, u32[]{:S(2)}) collective-permute-start(f16[1056,128]{1,0:T(8,128)(2,1)S(1)} %convert_element_type.349), channel_id=1, source_target_pairs={{0,5},{1,4},{2,7},{3,6},{4,1},{5,0},{6,3},{7,2},{8,13},{9,12},{10,... | collective-permute-start | bytes 811016 | tf_op jit(solution)/shard_map/up/ppermute | solution.py:293
  26.4 2.2 %collective-permute-start.8 = (f16[528,128]{1,0:T(8,128)(2,1)S(1)}, f16[528,128]{1,0:T(8,128)(2,1)S(1)}, u32[]{:S(2)}, u32[]{:S(2)}) collective-permute-start(f16[528,128]{1,0:T(8,128)(2,1)S(1)} %pad_maximum_fusion.6), channel_id=1, source_target_pairs={{0,8},{1,9},{2,10},{3,11},{4,12},{5,13},{6,14},{7,15},{8,0},{9,1},... | collective-permute-start | bytes 405512 | tf_op jit(solution)/shard_map/outer/ppermute | solution.py:293
  28.9 2.6 %collective-permute-done.8 = f16[528,128]{1,0:T(8,128)(2,1)S(1)} collective-permute-done((f16[528,128]{1,0:T(8,128)(2,1)S(1)}, f16[528,128]{1,0:T(8,128)(2,1)S(1)}, u32[]{:S(2)}, u32[]{:S(2)}) %collective-permute-start.8) | collective-permute-done | bytes 135200 | tf_op jit(solution)/shard_map/outer/ppermute | solution.py:293
  31.9 3.1 %collective-permute-start.9 = (f16[272,128]{1,0:T(8,128)(2,1)S(1)}, f16[272,128]{1,0:T(8,128)(2,1)S(1)}, u32[]{:S(2)}, u32[]{:S(2)}) collective-permute-start(f16[272,128]{1,0:T(8,128)(2,1)S(1)} %pad_maximum_fusion.8), channel_id=1, source_target_pairs={{0,16},{1,17},{2,18},{3,19},{4,20},{5,21},{6,22},{7,23},{8,24},{9,... | collective-permute-start | bytes 208904 | tf_op jit(solution)/shard_map/outer/ppermute | solution.py:293
  35.3 2.0 %collective-permute-done.9 = f16[272,128]{1,0:T(8,128)(2,1)S(1)} collective-permute-done((f16[272,128]{1,0:T(8,128)(2,1)S(1)}, f16[272,128]{1,0:T(8,128)(2,1)S(1)}, u32[]{:S(2)}, u32[]{:S(2)}) %collective-permute-start.9) | collective-permute-done | bytes 69664 | tf_op jit(solution)/shard_map/outer/ppermute | solution.py:293
  38.1 1.9 %collective-permute-start.15 = (f16[1040,128]{1,0:T(8,128)(2,1)S(1)}, f16[1040,128]{1,0:T(8,128)(2,1)S(1)}, u32[]{:S(2)}, u32[]{:S(2)}) collective-permute-start(f16[1040,128]{1,0:T(8,128)(2,1)S(1)} %get-tuple-element.230), channel_id=1, source_target_pairs={{0,1},{1,0},{2,3},{3,2},{4,5},{5,4},{6,7},{7,6},{8,9},{9,8},{10,11... | collective-permute-start | bytes 798728 | tf_op jit(solution)/shard_map/down/ppermute | solution.py:293
  40.0 1.5 %collective-permute-start.16 = (f16[1040,128]{1,0:T(8,128)(2,1)S(1)}, f16[1040,128]{1,0:T(8,128)(2,1)S(1)}, u32[]{:S(2)}, u32[]{:S(2)}) collective-permute-start(f16[1040,128]{1,0:T(8,128)(2,1)S(1)} %get-tuple-element.229), channel_id=1, source_target_pairs={{0,4},{1,5},{2,6},{3,7},{4,0},{5,1},{6,2},{7,3},{8,12},{9,13},{10,... | collective-permute-start | bytes 798728 | tf_op jit(solution)/shard_map/down/ppermute | solution.py:293
  42.2 2.0 %collective-permute-start.10 = (f16[528,128]{1,0:T(8,128)(2,1)S(1)}, f16[528,128]{1,0:T(8,128)(2,1)S(1)}, u32[]{:S(2)}, u32[]{:S(2)}) collective-permute-start(f16[528,128]{1,0:T(8,128)(2,1)S(1)} %pad_maximum_fusion.7), channel_id=1, source_target_pairs={{0,8},{1,9},{2,10},{3,11},{4,12},{5,13},{6,14},{7,15},{8,0},{9,1},... | collective-permute-start | bytes 405512 | tf_op jit(solution)/shard_map/outer/ppermute | solution.py:293
  44.6 3.5 %collective-permute-done.10 = f16[528,128]{1,0:T(8,128)(2,1)S(1)} collective-permute-done((f16[528,128]{1,0:T(8,128)(2,1)S(1)}, f16[528,128]{1,0:T(8,128)(2,1)S(1)}, u32[]{:S(2)}, u32[]{:S(2)}) %collective-permute-start.10) | collective-permute-done | bytes 135200 | tf_op jit(solution)/shard_map/outer/ppermute | solution.py:293
  48.4 2.7 %collective-permute-start.11 = (f16[272,128]{1,0:T(8,128)(2,1)S(1)}, f16[272,128]{1,0:T(8,128)(2,1)S(1)}, u32[]{:S(2)}, u32[]{:S(2)}) collective-permute-start(f16[272,128]{1,0:T(8,128)(2,1)S(1)} %pad_maximum_fusion.9), channel_id=1, source_target_pairs={{0,16},{1,17},{2,18},{3,19},{4,20},{5,21},{6,22},{7,23},{8,24},{9,... | collective-permute-start | bytes 208904 | tf_op jit(solution)/shard_map/outer/ppermute | solution.py:293
  51.4 2.3 %collective-permute-done.11 = f16[272,128]{1,0:T(8,128)(2,1)S(1)} collective-permute-done((f16[272,128]{1,0:T(8,128)(2,1)S(1)}, f16[272,128]{1,0:T(8,128)(2,1)S(1)}, u32[]{:S(2)}, u32[]{:S(2)}) %collective-permute-start.11) | collective-permute-done | bytes 69664 | tf_op jit(solution)/shard_map/outer/ppermute | solution.py:293
  54.5 1.6 %collective-permute-start.12 = (f16[1040,128]{1,0:T(8,128)(2,1)S(1)}, f16[1040,128]{1,0:T(8,128)(2,1)S(1)}, u32[]{:S(2)}, u32[]{:S(2)}) collective-permute-start(f16[1040,128]{1,0:T(8,128)(2,1)S(1)} %get-tuple-element.227), channel_id=1, source_target_pairs={{0,1},{1,0},{2,3},{3,2},{4,5},{5,4},{6,7},{7,6},{8,9},{9,8},{10,11... | collective-permute-start | bytes 798728 | tf_op jit(solution)/shard_map/down/ppermute | solution.py:293
  56.1 1.5 %collective-permute-start.13 = (f16[1040,128]{1,0:T(8,128)(2,1)S(1)}, f16[1040,128]{1,0:T(8,128)(2,1)S(1)}, u32[]{:S(2)}, u32[]{:S(2)}) collective-permute-start(f16[1040,128]{1,0:T(8,128)(2,1)S(1)} %get-tuple-element.226), channel_id=1, source_target_pairs={{0,4},{1,5},{2,6},{3,7},{4,0},{5,1},{6,2},{7,3},{8,12},{9,13},{10,... | collective-permute-start | bytes 798728 | tf_op jit(solution)/shard_map/down/ppermute | solution.py:293
  57.6 0.4 collective-permute-start.14
  58.8 1.6 %gradients.4 = (bf16[128,4096]{1,0:T(8,128)(2,1)}, bf16[128,4096]{1,0:T(8,128)(2,1)}, bf16[128,4096]{1,0:T(8,128)(2,1)}) custom-call(bf16[128,4096]{1,0:T(8,128)(2,1)S(1)} %copy-done, bf16[128,4096]{1,0:T(8,128)(2,1)S(1)} %copy-done.1, bf16[128,4096]{1,0:T(8,128)(2,1)S(1)} %copy-done.2, f32[4,3,128,256]{3,2,1,0:T(8,128)S(1)} %inside_group.5.inner, ...), custom_call_target="tpu_custom_call" | custom-call | flops 201326592 | bytes 2359296 | tf_op jit(solution)/shard_map/gradients/gradients/pallas_call | solution.py:235
  60.8 1.8 %gradients.5 = (bf16[128,4096]{1,0:T(8,128)(2,1)}, bf16[128,4096]{1,0:T(8,128)(2,1)}, bf16[128,4096]{1,0:T(8,128)(2,1)}) custom-call(bf16[128,4096]{1,0:T(8,128)(2,1)S(1)} %copy-done, bf16[128,4096]{1,0:T(8,128)(2,1)S(1)} %copy-done.1, bf16[128,4096]{1,0:T(8,128)(2,1)S(1)} %copy-done.2, ...), custom_call_target="tpu_custom_call", output_to_operand_aliasing={{0}: (8, {}), {1}: (9, {}), {2}: (10, {})} | custom-call | flops 201326592 | bytes 2359296 | tf_op jit(solution)/shard_map/gradients/gradients/pallas_call | solution.py:235
  62.7 2.6 %collective-permute-done.14 = f16[1040,128]{1,0:T(8,128)(2,1)S(1)} collective-permute-done((f16[1040,128]{1,0:T(8,128)(2,1)S(1)}, f16[1040,128]{1,0:T(8,128)(2,1)S(1)}, u32[]{:S(2)}, u32[]{:S(2)}) %collective-permute-start.14) | collective-permute-done | bytes 266272 | tf_op jit(solution)/shard_map/down/ppermute | solution.py:293
  66.0 1.6 %gradients.6 = (bf16[128,4096]{1,0:T(8,128)(2,1)}, bf16[128,4096]{1,0:T(8,128)(2,1)}, bf16[128,4096]{1,0:T(8,128)(2,1)}) custom-call(bf16[128,4096]{1,0:T(8,128)(2,1)S(1)} %copy-done, bf16[128,4096]{1,0:T(8,128)(2,1)S(1)} %copy-done.1, bf16[128,4096]{1,0:T(8,128)(2,1)S(1)} %copy-done.2, ...), custom_call_target="tpu_custom_call", output_to_operand_aliasing={{0}: (8, {}), {1}: (9, {}), {2}: (10, {})} | custom-call | flops 201326592 | bytes 2359296 | tf_op jit(solution)/shard_map/gradients/gradients/pallas_call | solution.py:235
  68.1 1.6 %gradients.7 = (bf16[128,4096]{1,0:T(8,128)(2,1)}, bf16[128,4096]{1,0:T(8,128)(2,1)}, bf16[128,4096]{1,0:T(8,128)(2,1)}) custom-call(bf16[128,4096]{1,0:T(8,128)(2,1)S(1)} %copy-done, bf16[128,4096]{1,0:T(8,128)(2,1)S(1)} %copy-done.1, bf16[128,4096]{1,0:T(8,128)(2,1)S(1)} %copy-done.2, ...), custom_call_target="tpu_custom_call", output_to_operand_aliasing={{0}: (8, {}), {1}: (9, {}), {2}: (10, {})} | custom-call | flops 201326592 | bytes 2359296 | tf_op jit(solution)/shard_map/gradients/gradients/pallas_call | solution.py:235
  (170 shorter events, 7.5 us)
Async XLA Ops:
  3.3 3.4 %collective-permute-start.4 = (f32[2080,128]{1,0:T(8,128)}, f32[2080,128]{1,0:T(8,128)}, u32[]{:S(2)}, u32[]{:S(2)}) collective-permute-start(f32[2080,128]{1,0:T(8,128)} %get-tuple-element.71), channel_id=1, source_target_pairs={{0,2},{1,3},{2,0},{3,1},{4,6},{5,7},{6,4},{7,5},{8,10},{9,11},{10,... | collective-permute-start | bytes 3194888 | tf_op jit(solution)/shard_map/states/ppermute | solution.py:293
  6.5 6.4 %collective-permute-start = (f32[2080,128]{1,0:T(8,128)}, f32[2080,128]{1,0:T(8,128)S(1)}, u32[]{:S(2)}, u32[]{:S(2)}) collective-permute-start(f32[2080,128]{1,0:T(8,128)} %get-tuple-element.60), channel_id=1, source_target_pairs={{0,2},{1,3},{2,0},{3,1},{4,6},{5,7},{6,4},{7,5},{8,10},{9,11},{10,... | collective-permute-start | bytes 3194888 | tf_op jit(solution)/shard_map/states/ppermute | solution.py:293
  8.0 16.3 %collective-permute-start.5 = (f16[1056,128]{1,0:T(8,128)(2,1)S(1)}, f16[1056,128]{1,0:T(8,128)(2,1)S(1)}, u32[]{:S(2)}, u32[]{:S(2)}) collective-permute-start(f16[1056,128]{1,0:T(8,128)(2,1)S(1)} %convert_element_type.350), channel_id=1, source_target_pairs={{0,1},{1,0},{2,3},{3,2},{4,5},{5,4},{6,7},{7,6},{8,9},{9,8},{10,11... | collective-permute-start | bytes 811016 | tf_op jit(solution)/shard_map/up/ppermute | solution.py:293
  11.1 14.3 %collective-permute-start.6 = (f16[1056,128]{1,0:T(8,128)(2,1)S(1)}, f16[1056,128]{1,0:T(8,128)(2,1)S(1)}, u32[]{:S(2)}, u32[]{:S(2)}) collective-permute-start(f16[1056,128]{1,0:T(8,128)(2,1)S(1)} %convert_element_type.351), channel_id=1, source_target_pairs={{0,4},{1,5},{2,6},{3,7},{4,0},{5,1},{6,2},{7,3},{8,12},{9,13},{10,... | collective-permute-start | bytes 811016 | tf_op jit(solution)/shard_map/up/ppermute | solution.py:293
  12.7 13.1 %collective-permute-start.7 = (f16[1056,128]{1,0:T(8,128)(2,1)S(1)}, f16[1056,128]{1,0:T(8,128)(2,1)S(1)}, u32[]{:S(2)}, u32[]{:S(2)}) collective-permute-start(f16[1056,128]{1,0:T(8,128)(2,1)S(1)} %convert_element_type.352), channel_id=1, source_target_pairs={{0,5},{1,4},{2,7},{3,6},{4,1},{5,0},{6,3},{7,2},{8,13},{9,12},{10,... | collective-permute-start | bytes 811016 | tf_op jit(solution)/shard_map/up/ppermute | solution.py:293
  12.9 4.2 %copy-start.2 = (bf16[128,4096]{1,0:T(8,128)(2,1)S(1)}, bf16[128,4096]{1,0:T(8,128)(2,1)}, u32[]{:S(2)}) copy-start(bf16[128,4096]{1,0:T(8,128)(2,1)} %d.15) | copy-start | bytes 3145732
  13.0 4.2 %copy-start.3 = (bf16[128,4096]{1,0:T(8,128)(2,1)S(1)}, bf16[128,4096]{1,0:T(8,128)(2,1)}, u32[]{:S(2)}) copy-start(bf16[128,4096]{1,0:T(8,128)(2,1)} %q.7) | copy-start | bytes 3145732
  13.4 3.7 %copy-start = (bf16[128,4096]{1,0:T(8,128)(2,1)S(1)}, bf16[128,4096]{1,0:T(8,128)(2,1)}, u32[]{:S(2)}) copy-start(bf16[128,4096]{1,0:T(8,128)(2,1)} %k.15) | copy-start | bytes 3145732
  13.4 3.7 %copy-start.1 = (bf16[128,4096]{1,0:T(8,128)(2,1)S(1)}, bf16[128,4096]{1,0:T(8,128)(2,1)}, u32[]{:S(2)}) copy-start(bf16[128,4096]{1,0:T(8,128)(2,1)} %v.15) | copy-start | bytes 3145732
  13.6 27.9 %collective-permute-start.1 = (f16[1056,128]{1,0:T(8,128)(2,1)S(1)}, f16[1056,128]{1,0:T(8,128)(2,1)S(1)}, u32[]{:S(2)}, u32[]{:S(2)}) collective-permute-start(f16[1056,128]{1,0:T(8,128)(2,1)S(1)} %convert_element_type.347), channel_id=1, source_target_pairs={{0,1},{1,0},{2,3},{3,2},{4,5},{5,4},{6,7},{7,6},{8,9},{9,8},{10,11... | collective-permute-start | bytes 811016 | tf_op jit(solution)/shard_map/up/ppermute | solution.py:293
  15.6 26.0 %collective-permute-start.2 = (f16[1056,128]{1,0:T(8,128)(2,1)S(1)}, f16[1056,128]{1,0:T(8,128)(2,1)S(1)}, u32[]{:S(2)}, u32[]{:S(2)}) collective-permute-start(f16[1056,128]{1,0:T(8,128)(2,1)S(1)} %convert_element_type.348), channel_id=1, source_target_pairs={{0,4},{1,5},{2,6},{3,7},{4,0},{5,1},{6,2},{7,3},{8,12},{9,13},{10,... | collective-permute-start | bytes 811016 | tf_op jit(solution)/shard_map/up/ppermute | solution.py:293
  24.4 17.3 %collective-permute-start.3 = (f16[1056,128]{1,0:T(8,128)(2,1)S(1)}, f16[1056,128]{1,0:T(8,128)(2,1)S(1)}, u32[]{:S(2)}, u32[]{:S(2)}) collective-permute-start(f16[1056,128]{1,0:T(8,128)(2,1)S(1)} %convert_element_type.349), channel_id=1, source_target_pairs={{0,5},{1,4},{2,7},{3,6},{4,1},{5,0},{6,3},{7,2},{8,13},{9,12},{10,... | collective-permute-start | bytes 811016 | tf_op jit(solution)/shard_map/up/ppermute | solution.py:293
  26.4 5.2 %collective-permute-start.8 = (f16[528,128]{1,0:T(8,128)(2,1)S(1)}, f16[528,128]{1,0:T(8,128)(2,1)S(1)}, u32[]{:S(2)}, u32[]{:S(2)}) collective-permute-start(f16[528,128]{1,0:T(8,128)(2,1)S(1)} %pad_maximum_fusion.6), channel_id=1, source_target_pairs={{0,8},{1,9},{2,10},{3,11},{4,12},{5,13},{6,14},{7,15},{8,0},{9,1},... | collective-permute-start | bytes 405512 | tf_op jit(solution)/shard_map/outer/ppermute | solution.py:293
  31.9 5.4 %collective-permute-start.9 = (f16[272,128]{1,0:T(8,128)(2,1)S(1)}, f16[272,128]{1,0:T(8,128)(2,1)S(1)}, u32[]{:S(2)}, u32[]{:S(2)}) collective-permute-start(f16[272,128]{1,0:T(8,128)(2,1)S(1)} %pad_maximum_fusion.8), channel_id=1, source_target_pairs={{0,16},{1,17},{2,18},{3,19},{4,20},{5,21},{6,22},{7,23},{8,24},{9,... | collective-permute-start | bytes 208904 | tf_op jit(solution)/shard_map/outer/ppermute | solution.py:293
  38.1 19.5 %collective-permute-start.15 = (f16[1040,128]{1,0:T(8,128)(2,1)S(1)}, f16[1040,128]{1,0:T(8,128)(2,1)S(1)}, u32[]{:S(2)}, u32[]{:S(2)}) collective-permute-start(f16[1040,128]{1,0:T(8,128)(2,1)S(1)} %get-tuple-element.230), channel_id=1, source_target_pairs={{0,1},{1,0},{2,3},{3,2},{4,5},{5,4},{6,7},{7,6},{8,9},{9,8},{10,11... | collective-permute-start | bytes 798728 | tf_op jit(solution)/shard_map/down/ppermute | solution.py:293
  40.0 18.1 %collective-permute-start.16 = (f16[1040,128]{1,0:T(8,128)(2,1)S(1)}, f16[1040,128]{1,0:T(8,128)(2,1)S(1)}, u32[]{:S(2)}, u32[]{:S(2)}) collective-permute-start(f16[1040,128]{1,0:T(8,128)(2,1)S(1)} %get-tuple-element.229), channel_id=1, source_target_pairs={{0,4},{1,5},{2,6},{3,7},{4,0},{5,1},{6,2},{7,3},{8,12},{9,13},{10,... | collective-permute-start | bytes 798728 | tf_op jit(solution)/shard_map/down/ppermute | solution.py:293
  41.5 16.7 %collective-permute-start.17 = (f16[1040,128]{1,0:T(8,128)(2,1)S(1)}, f16[1040,128]{1,0:T(8,128)(2,1)S(1)}, u32[]{:S(2)}, u32[]{:S(2)}) collective-permute-start(f16[1040,128]{1,0:T(8,128)(2,1)S(1)} %get-tuple-element.228), channel_id=1, source_target_pairs={{0,5},{1,4},{2,7},{3,6},{4,1},{5,0},{6,3},{7,2},{8,13},{9,12},{10,... | collective-permute-start | bytes 798728 | tf_op jit(solution)/shard_map/down/ppermute | solution.py:293
  42.2 5.8 %collective-permute-start.10 = (f16[528,128]{1,0:T(8,128)(2,1)S(1)}, f16[528,128]{1,0:T(8,128)(2,1)S(1)}, u32[]{:S(2)}, u32[]{:S(2)}) collective-permute-start(f16[528,128]{1,0:T(8,128)(2,1)S(1)} %pad_maximum_fusion.7), channel_id=1, source_target_pairs={{0,8},{1,9},{2,10},{3,11},{4,12},{5,13},{6,14},{7,15},{8,0},{9,1},... | collective-permute-start | bytes 405512 | tf_op jit(solution)/shard_map/outer/ppermute | solution.py:293
  48.4 5.3 %collective-permute-start.11 = (f16[272,128]{1,0:T(8,128)(2,1)S(1)}, f16[272,128]{1,0:T(8,128)(2,1)S(1)}, u32[]{:S(2)}, u32[]{:S(2)}) collective-permute-start(f16[272,128]{1,0:T(8,128)(2,1)S(1)} %pad_maximum_fusion.9), channel_id=1, source_target_pairs={{0,16},{1,17},{2,18},{3,19},{4,20},{5,21},{6,22},{7,23},{8,24},{9,... | collective-permute-start | bytes 208904 | tf_op jit(solution)/shard_map/outer/ppermute | solution.py:293
  54.5 8.2 %collective-permute-start.12 = (f16[1040,128]{1,0:T(8,128)(2,1)S(1)}, f16[1040,128]{1,0:T(8,128)(2,1)S(1)}, u32[]{:S(2)}, u32[]{:S(2)}) collective-permute-start(f16[1040,128]{1,0:T(8,128)(2,1)S(1)} %get-tuple-element.227), channel_id=1, source_target_pairs={{0,1},{1,0},{2,3},{3,2},{4,5},{5,4},{6,7},{7,6},{8,9},{9,8},{10,11... | collective-permute-start | bytes 798728 | tf_op jit(solution)/shard_map/down/ppermute | solution.py:293
  56.1 6.6 %collective-permute-start.13 = (f16[1040,128]{1,0:T(8,128)(2,1)S(1)}, f16[1040,128]{1,0:T(8,128)(2,1)S(1)}, u32[]{:S(2)}, u32[]{:S(2)}) collective-permute-start(f16[1040,128]{1,0:T(8,128)(2,1)S(1)} %get-tuple-element.226), channel_id=1, source_target_pairs={{0,4},{1,5},{2,6},{3,7},{4,0},{5,1},{6,2},{7,3},{8,12},{9,13},{10,... | collective-permute-start | bytes 798728 | tf_op jit(solution)/shard_map/down/ppermute | solution.py:293
  57.6 7.7 %collective-permute-start.14 = (f16[1040,128]{1,0:T(8,128)(2,1)S(1)}, f16[1040,128]{1,0:T(8,128)(2,1)S(1)}, u32[]{:S(2)}, u32[]{:S(2)}) collective-permute-start(f16[1040,128]{1,0:T(8,128)(2,1)S(1)} %get-tuple-element.225), channel_id=1, source_target_pairs={{0,5},{1,4},{2,7},{3,6},{4,1},{5,0},{6,3},{7,2},{8,13},{9,12},{10,... | collective-permute-start | bytes 798728 | tf_op jit(solution)/shard_map/down/ppermute | solution.py:293
  58.5 2.0 %collective-permute-start.18 = (f16[2112,128]{1,0:T(8,128)(2,1)S(1)}, f16[2112,128]{1,0:T(8,128)(2,1)S(1)}, u32[]{:S(2)}, u32[]{:S(2)}) collective-permute-start(f16[2112,128]{1,0:T(8,128)(2,1)S(1)} %constant_dynamic-update-slice_fusion), channel_id=1, source_target_pairs={{0,2},{1,3},{2,0},{3,1},{4,6},{5,7},{6,4},{7,5},{8,10},{9,11},{10,... | collective-permute-start | bytes 1622024 | tf_op jit(solution)/shard_map/core_return/ppermute | solution.py:293
  65.8 2.0 %collective-permute-start.19 = (f16[2112,128]{1,0:T(8,128)(2,1)S(1)}, f16[2112,128]{1,0:T(8,128)(2,1)S(1)}, u32[]{:S(2)}, u32[]{:S(2)}) collective-permute-start(f16[2112,128]{1,0:T(8,128)(2,1)S(1)} %constant_dynamic-update-slice_fusion.8), channel_id=1, source_target_pairs={{0,2},{1,3},{2,0},{3,1},{4,6},{5,7},{6,4},{7,5},{8,10},{9,11},{10,... | collective-permute-start | bytes 1622024 | tf_op jit(solution)/shard_map/core_return/ppermute | solution.py:293

commit v5 on v4

--- a/solution.py
+++ b/solution.py
@@ -356,7 +356,8 @@
                     e = tail(reply, 0, 1)
                     other = decode(reply[:-TAIL], e, 1)
                 entering = entering + w * other
-                entering_bound = entering_bound + jnp.exp2(e)
+                came = jnp.repeat(w.reshape(2, 1), 8, axis=0)
+                entering_bound = entering_bound + came * jnp.exp2(e)
         with jax.named_scope("cube_before"):
             pair = {(i, x): blocks[i, 2 * x] + blocks[i, 2 * x + 1] for i in (0, 1) for x in (0, 1)}
             quad = {x: pair[0, x] + pair[1, x] for x in (0, 1)}

time: 70 us -> 70.4 us (level)
  transfers between devices with their start and end apart: 20 -> 20, of which waited for: 8 -> 8; matrix products, arithmetic and copies ran while one was open for 8% -> 9% of each run, Pallas kernels for 24% -> 24%
where the time goes in v5:
time: 70.4 us; the launch traced here: 70.2 us
  starting transfers between devices  27.1 us (38%)
  Pallas kernels  20.9 us (30%)
  waiting for transfers between devices  13.7 us (19%)
  other arithmetic  5.05 us (7%)
  between operations  1.88 us (3%)
  local copies, waits for them, and re-layouts  1.62 us (2%)
    ppermute x20, starting transfers between devices, move(): return lax.ppermute(x, AXES, [(p, p ^ mask) for p in range(devices)])  27.1 us
    ppermute x20, waiting for transfers between devices, move(): return lax.ppermute(x, AXES, [(p, p ^ mask) for p in range(devices)])  13.7 us
    pallas_call x4, Pallas kernels, inside(): pl.pallas_call(functools.partial(inside_kernel, scale, part, chunk), in_s...  7.2 us
    pallas_call x4, Pallas kernels, gradients(): pl.pallas_call(functools.partial(gradient_kernel, scale, part, picked, ch...  6.61 us
    pallas_call x2, Pallas kernels, states(): pl.pallas_call(functools.partial(state_kernel, chunk), in_specs=[ANY] * 4...  5.36 us
    pallas_call x2, Pallas kernels, join(): pl.pallas_call(join_kernel, in_specs=[VMEM, ANY], out_specs=(VMEM,) * 5,...  1.7 us
  transfers between devices with their start and end apart: 20, of which 8 were waited for; matrix products, arithmetic and copies ran while one was open for 9% of the time, Pallas kernels for 24%

profile of v5, /device:TPU:0, one launch (start us, length us, event | category | flops | bytes accessed | tf_op | source)
XLA Modules:
  0.0 70.2 jit_solution(6854889614695862529)
XLA Ops:
  0.6 2.7 %group_states.3 = (f32[2080,128]{1,0:T(8,128)S(1)}, f32[2080,128]{1,0:T(8,128)}) custom-call(bf16[128,4096]{1,0:T(8,128)(2,1)} %q.7, bf16[128,4096]{1,0:T(8,128)(2,1)} %k.15, bf16[128,4096]{1,0:T(8,128)(2,1)} %v.15, bf16[128,4096]{1,0:T(8,128)(2,1)} %d.15), custom_call_target="tpu_custom_call" | custom-call | flops 134217728 | bytes 4194304 | tf_op jit(solution)/shard_map/states/group_states/pallas_call | solution.py:97
  3.3 0.5 collective-permute-start.4
  3.8 2.7 %group_states.2 = (f32[2080,128]{1,0:T(8,128)S(1)}, f32[2080,128]{1,0:T(8,128)}) custom-call(bf16[128,4096]{1,0:T(8,128)(2,1)} %q.7, bf16[128,4096]{1,0:T(8,128)(2,1)} %k.15, bf16[128,4096]{1,0:T(8,128)(2,1)} %v.15, bf16[128,4096]{1,0:T(8,128)(2,1)} %d.15), custom_call_target="tpu_custom_call" | custom-call | flops 134217728 | bytes 4194304 | tf_op jit(solution)/shard_map/states/group_states/pallas_call | solution.py:97
  7.0 1.3 %join_groups.3 = (f32[2,2,256,128]{3,2,1,0:T(8,128)S(1)}, f32[16,128]{1,0:T(8,128)S(1)}, f32[1056,128]{1,0:T(8,128)S(1)}, f32[1056,128]{1,0:T(8,128)S(1)}, f32[1056,128]{1,0:T(8,128)S(1)}) custom-call(f32[2080,128]{1,0:T(8,128)S(1)} %get-tuple-element.70.near, f32[2080,128]{1,0:T(8,128)} %collective-permute-done.4.away), custom_call_target="tpu_custom_call" | custom-call | flops 262144 | bytes 4194304 | tf_op jit(solution)/shard_map/up/join_groups/pallas_call | solution.py:147
  8.4 3.0 %collective-permute-start.5 = (f16[1056,128]{1,0:T(8,128)(2,1)S(1)}, f16[1056,128]{1,0:T(8,128)(2,1)S(1)}, u32[]{:S(2)}, u32[]{:S(2)}) collective-permute-start(f16[1056,128]{1,0:T(8,128)(2,1)S(1)} %convert_element_type.350), channel_id=1, source_target_pairs={{0,1},{1,0},{2,3},{3,2},{4,5},{5,4},{6,7},{7,6},{8,9},{9,8},{10,11... | collective-permute-start | bytes 811016 | tf_op jit(solution)/shard_map/up/ppermute | solution.py:293
  11.4 1.6 %collective-permute-start.6 = (f16[1056,128]{1,0:T(8,128)(2,1)S(1)}, f16[1056,128]{1,0:T(8,128)(2,1)S(1)}, u32[]{:S(2)}, u32[]{:S(2)}) collective-permute-start(f16[1056,128]{1,0:T(8,128)(2,1)S(1)} %convert_element_type.351), channel_id=1, source_target_pairs={{0,4},{1,5},{2,6},{3,7},{4,0},{5,1},{6,2},{7,3},{8,12},{9,13},{10,... | collective-permute-start | bytes 811016 | tf_op jit(solution)/shard_map/up/ppermute | solution.py:293
  13.3 0.4 join_groups.2
  13.9 2.0 %collective-permute-start.1 = (f16[1056,128]{1,0:T(8,128)(2,1)S(1)}, f16[1056,128]{1,0:T(8,128)(2,1)S(1)}, u32[]{:S(2)}, u32[]{:S(2)}) collective-permute-start(f16[1056,128]{1,0:T(8,128)(2,1)S(1)} %convert_element_type.347), channel_id=1, source_target_pairs={{0,1},{1,0},{2,3},{3,2},{4,5},{5,4},{6,7},{7,6},{8,9},{9,8},{10,11... | collective-permute-start | bytes 811016 | tf_op jit(solution)/shard_map/up/ppermute | solution.py:293
  15.9 1.5 %collective-permute-start.2 = (f16[1056,128]{1,0:T(8,128)(2,1)S(1)}, f16[1056,128]{1,0:T(8,128)(2,1)S(1)}, u32[]{:S(2)}, u32[]{:S(2)}) collective-permute-start(f16[1056,128]{1,0:T(8,128)(2,1)S(1)} %convert_element_type.348), channel_id=1, source_target_pairs={{0,4},{1,5},{2,6},{3,7},{4,0},{5,1},{6,2},{7,3},{8,12},{9,13},{10,... | collective-permute-start | bytes 811016 | tf_op jit(solution)/shard_map/up/ppermute | solution.py:293
  17.4 1.8 %inside_group.4.inner = f32[4,3,128,256]{3,2,1,0:T(8,128)S(1)} custom-call(bf16[128,4096]{1,0:T(8,128)(2,1)S(1)} %copy-done.3, bf16[128,4096]{1,0:T(8,128)(2,1)S(1)} %copy-done, bf16[128,4096]{1,0:T(8,128)(2,1)S(1)} %copy-done.1, bf16[128,4096]{1,0:T(8,128)(2,1)S(1)} %copy-done.2), custom_call_target="tpu_custom_call" | custom-call | flops 201326592 | bytes 2621440 | tf_op jit(solution)/shard_map/inside/inside_group/pallas_call | solution.py:187
  19.2 1.8 %inside_group.5.inner = f32[4,3,128,256]{3,2,1,0:T(8,128)S(1)} custom-call(bf16[128,4096]{1,0:T(8,128)(2,1)S(1)} %copy-done.3, bf16[128,4096]{1,0:T(8,128)(2,1)S(1)} %copy-done, bf16[128,4096]{1,0:T(8,128)(2,1)S(1)} %copy-done.1, bf16[128,4096]{1,0:T(8,128)(2,1)S(1)} %copy-done.2), custom_call_target="tpu_custom_call" | custom-call | flops 201326592 | bytes 2621440 | tf_op jit(solution)/shard_map/inside/inside_group/pallas_call | solution.py:187
  21.0 1.8 %inside_group.6.inner = f32[4,3,128,256]{3,2,1,0:T(8,128)S(1)} custom-call(bf16[128,4096]{1,0:T(8,128)(2,1)S(1)} %copy-done.3, bf16[128,4096]{1,0:T(8,128)(2,1)S(1)} %copy-done, bf16[128,4096]{1,0:T(8,128)(2,1)S(1)} %copy-done.1, bf16[128,4096]{1,0:T(8,128)(2,1)S(1)} %copy-done.2), custom_call_target="tpu_custom_call" | custom-call | flops 201326592 | bytes 2621440 | tf_op jit(solution)/shard_map/inside/inside_group/pallas_call | solution.py:187
  22.9 1.8 %inside_group.7.inner = f32[4,3,128,256]{3,2,1,0:T(8,128)S(1)} custom-call(bf16[128,4096]{1,0:T(8,128)(2,1)S(1)} %copy-done.3, bf16[128,4096]{1,0:T(8,128)(2,1)S(1)} %copy-done, bf16[128,4096]{1,0:T(8,128)(2,1)S(1)} %copy-done.1, bf16[128,4096]{1,0:T(8,128)(2,1)S(1)} %copy-done.2), custom_call_target="tpu_custom_call" | custom-call | flops 201326592 | bytes 2621440 | tf_op jit(solution)/shard_map/inside/inside_group/pallas_call | solution.py:187
  24.7 1.1 %collective-permute-start.3 = (f16[1056,128]{1,0:T(8,128)(2,1)S(1)}, f16[1056,128]{1,0:T(8,128)(2,1)S(1)}, u32[]{:S(2)}, u32[]{:S(2)}) collective-permute-start(f16[1056,128]{1,0:T(8,128)(2,1)S(1)} %convert_element_type.349), channel_id=1, source_target_pairs={{0,5},{1,4},{2,7},{3,6},{4,1},{5,0},{6,3},{7,2},{8,13},{9,12},{10,... | collective-permute-start | bytes 811016 | tf_op jit(solution)/shard_map/up/ppermute | solution.py:293
  26.7 2.2 %collective-permute-start.8 = (f16[528,128]{1,0:T(8,128)(2,1)S(1)}, f16[528,128]{1,0:T(8,128)(2,1)S(1)}, u32[]{:S(2)}, u32[]{:S(2)}) collective-permute-start(f16[528,128]{1,0:T(8,128)(2,1)S(1)} %pad_maximum_fusion.6), channel_id=1, source_target_pairs={{0,8},{1,9},{2,10},{3,11},{4,12},{5,13},{6,14},{7,15},{8,0},{9,1},... | collective-permute-start | bytes 405512 | tf_op jit(solution)/shard_map/outer/ppermute | solution.py:293
  29.2 2.6 %collective-permute-done.8 = f16[528,128]{1,0:T(8,128)(2,1)S(1)} collective-permute-done((f16[528,128]{1,0:T(8,128)(2,1)S(1)}, f16[528,128]{1,0:T(8,128)(2,1)S(1)}, u32[]{:S(2)}, u32[]{:S(2)}) %collective-permute-start.8) | collective-permute-done | bytes 135200 | tf_op jit(solution)/shard_map/outer/ppermute | solution.py:293
  32.2 3.1 %collective-permute-start.9 = (f16[272,128]{1,0:T(8,128)(2,1)S(1)}, f16[272,128]{1,0:T(8,128)(2,1)S(1)}, u32[]{:S(2)}, u32[]{:S(2)}) collective-permute-start(f16[272,128]{1,0:T(8,128)(2,1)S(1)} %pad_maximum_fusion.8), channel_id=1, source_target_pairs={{0,16},{1,17},{2,18},{3,19},{4,20},{5,21},{6,22},{7,23},{8,24},{9,... | collective-permute-start | bytes 208904 | tf_op jit(solution)/shard_map/outer/ppermute | solution.py:293
  35.6 2.0 %collective-permute-done.9 = f16[272,128]{1,0:T(8,128)(2,1)S(1)} collective-permute-done((f16[272,128]{1,0:T(8,128)(2,1)S(1)}, f16[272,128]{1,0:T(8,128)(2,1)S(1)}, u32[]{:S(2)}, u32[]{:S(2)}) %collective-permute-start.9) | collective-permute-done | bytes 69664 | tf_op jit(solution)/shard_map/outer/ppermute | solution.py:293
  38.4 1.9 %collective-permute-start.15 = (f16[1040,128]{1,0:T(8,128)(2,1)S(1)}, f16[1040,128]{1,0:T(8,128)(2,1)S(1)}, u32[]{:S(2)}, u32[]{:S(2)}) collective-permute-start(f16[1040,128]{1,0:T(8,128)(2,1)S(1)} %get-tuple-element.232), channel_id=1, source_target_pairs={{0,1},{1,0},{2,3},{3,2},{4,5},{5,4},{6,7},{7,6},{8,9},{9,8},{10,11... | collective-permute-start | bytes 798728 | tf_op jit(solution)/shard_map/down/ppermute | solution.py:293
  40.4 1.5 %collective-permute-start.16 = (f16[1040,128]{1,0:T(8,128)(2,1)S(1)}, f16[1040,128]{1,0:T(8,128)(2,1)S(1)}, u32[]{:S(2)}, u32[]{:S(2)}) collective-permute-start(f16[1040,128]{1,0:T(8,128)(2,1)S(1)} %get-tuple-element.231), channel_id=1, source_target_pairs={{0,4},{1,5},{2,6},{3,7},{4,0},{5,1},{6,2},{7,3},{8,12},{9,13},{10,... | collective-permute-start | bytes 798728 | tf_op jit(solution)/shard_map/down/ppermute | solution.py:293
  42.6 2.0 %collective-permute-start.10 = (f16[528,128]{1,0:T(8,128)(2,1)S(1)}, f16[528,128]{1,0:T(8,128)(2,1)S(1)}, u32[]{:S(2)}, u32[]{:S(2)}) collective-permute-start(f16[528,128]{1,0:T(8,128)(2,1)S(1)} %pad_maximum_fusion.7), channel_id=1, source_target_pairs={{0,8},{1,9},{2,10},{3,11},{4,12},{5,13},{6,14},{7,15},{8,0},{9,1},... | collective-permute-start | bytes 405512 | tf_op jit(solution)/shard_map/outer/ppermute | solution.py:293
  44.9 3.5 %collective-permute-done.10 = f16[528,128]{1,0:T(8,128)(2,1)S(1)} collective-permute-done((f16[528,128]{1,0:T(8,128)(2,1)S(1)}, f16[528,128]{1,0:T(8,128)(2,1)S(1)}, u32[]{:S(2)}, u32[]{:S(2)}) %collective-permute-start.10) | collective-permute-done | bytes 135200 | tf_op jit(solution)/shard_map/outer/ppermute | solution.py:293
  48.7 2.7 %collective-permute-start.11 = (f16[272,128]{1,0:T(8,128)(2,1)S(1)}, f16[272,128]{1,0:T(8,128)(2,1)S(1)}, u32[]{:S(2)}, u32[]{:S(2)}) collective-permute-start(f16[272,128]{1,0:T(8,128)(2,1)S(1)} %pad_maximum_fusion.9), channel_id=1, source_target_pairs={{0,16},{1,17},{2,18},{3,19},{4,20},{5,21},{6,22},{7,23},{8,24},{9,... | collective-permute-start | bytes 208904 | tf_op jit(solution)/shard_map/outer/ppermute | solution.py:293
  51.7 2.3 %collective-permute-done.11 = f16[272,128]{1,0:T(8,128)(2,1)S(1)} collective-permute-done((f16[272,128]{1,0:T(8,128)(2,1)S(1)}, f16[272,128]{1,0:T(8,128)(2,1)S(1)}, u32[]{:S(2)}, u32[]{:S(2)}) %collective-permute-start.11) | collective-permute-done | bytes 69664 | tf_op jit(solution)/shard_map/outer/ppermute | solution.py:293
  54.9 1.6 %collective-permute-start.12 = (f16[1040,128]{1,0:T(8,128)(2,1)S(1)}, f16[1040,128]{1,0:T(8,128)(2,1)S(1)}, u32[]{:S(2)}, u32[]{:S(2)}) collective-permute-start(f16[1040,128]{1,0:T(8,128)(2,1)S(1)} %get-tuple-element.229), channel_id=1, source_target_pairs={{0,1},{1,0},{2,3},{3,2},{4,5},{5,4},{6,7},{7,6},{8,9},{9,8},{10,11... | collective-permute-start | bytes 798728 | tf_op jit(solution)/shard_map/down/ppermute | solution.py:293
  56.5 1.5 %collective-permute-start.13 = (f16[1040,128]{1,0:T(8,128)(2,1)S(1)}, f16[1040,128]{1,0:T(8,128)(2,1)S(1)}, u32[]{:S(2)}, u32[]{:S(2)}) collective-permute-start(f16[1040,128]{1,0:T(8,128)(2,1)S(1)} %get-tuple-element.228), channel_id=1, source_target_pairs={{0,4},{1,5},{2,6},{3,7},{4,0},{5,1},{6,2},{7,3},{8,12},{9,13},{10,... | collective-permute-start | bytes 798728 | tf_op jit(solution)/shard_map/down/ppermute | solution.py:293
  58.0 0.4 collective-permute-start.14
  59.2 1.6 %gradients.4 = (bf16[128,4096]{1,0:T(8,128)(2,1)}, bf16[128,4096]{1,0:T(8,128)(2,1)}, bf16[128,4096]{1,0:T(8,128)(2,1)}) custom-call(bf16[128,4096]{1,0:T(8,128)(2,1)S(1)} %copy-done, bf16[128,4096]{1,0:T(8,128)(2,1)S(1)} %copy-done.1, bf16[128,4096]{1,0:T(8,128)(2,1)S(1)} %copy-done.2, f32[4,3,128,256]{3,2,1,0:T(8,128)S(1)} %inside_group.5.inner, ...), custom_call_target="tpu_custom_call" | custom-call | flops 201326592 | bytes 2359296 | tf_op jit(solution)/shard_map/gradients/gradients/pallas_call | solution.py:235
  61.2 1.8 %gradients.5 = (bf16[128,4096]{1,0:T(8,128)(2,1)}, bf16[128,4096]{1,0:T(8,128)(2,1)}, bf16[128,4096]{1,0:T(8,128)(2,1)}) custom-call(bf16[128,4096]{1,0:T(8,128)(2,1)S(1)} %copy-done, bf16[128,4096]{1,0:T(8,128)(2,1)S(1)} %copy-done.1, bf16[128,4096]{1,0:T(8,128)(2,1)S(1)} %copy-done.2, ...), custom_call_target="tpu_custom_call", output_to_operand_aliasing={{0}: (8, {}), {1}: (9, {}), {2}: (10, {})} | custom-call | flops 201326592 | bytes 2359296 | tf_op jit(solution)/shard_map/gradients/gradients/pallas_call | solution.py:235
  63.1 2.6 %collective-permute-done.14 = f16[1040,128]{1,0:T(8,128)(2,1)S(1)} collective-permute-done((f16[1040,128]{1,0:T(8,128)(2,1)S(1)}, f16[1040,128]{1,0:T(8,128)(2,1)S(1)}, u32[]{:S(2)}, u32[]{:S(2)}) %collective-permute-start.14) | collective-permute-done | bytes 266272 | tf_op jit(solution)/shard_map/down/ppermute | solution.py:293
  66.4 1.6 %gradients.6 = (bf16[128,4096]{1,0:T(8,128)(2,1)}, bf16[128,4096]{1,0:T(8,128)(2,1)}, bf16[128,4096]{1,0:T(8,128)(2,1)}) custom-call(bf16[128,4096]{1,0:T(8,128)(2,1)S(1)} %copy-done, bf16[128,4096]{1,0:T(8,128)(2,1)S(1)} %copy-done.1, bf16[128,4096]{1,0:T(8,128)(2,1)S(1)} %copy-done.2, ...), custom_call_target="tpu_custom_call", output_to_operand_aliasing={{0}: (8, {}), {1}: (9, {}), {2}: (10, {})} | custom-call | flops 201326592 | bytes 2359296 | tf_op jit(solution)/shard_map/gradients/gradients/pallas_call | solution.py:235
  68.5 1.6 %gradients.7 = (bf16[128,4096]{1,0:T(8,128)(2,1)}, bf16[128,4096]{1,0:T(8,128)(2,1)}, bf16[128,4096]{1,0:T(8,128)(2,1)}) custom-call(bf16[128,4096]{1,0:T(8,128)(2,1)S(1)} %copy-done, bf16[128,4096]{1,0:T(8,128)(2,1)S(1)} %copy-done.1, bf16[128,4096]{1,0:T(8,128)(2,1)S(1)} %copy-done.2, ...), custom_call_target="tpu_custom_call", output_to_operand_aliasing={{0}: (8, {}), {1}: (9, {}), {2}: (10, {})} | custom-call | flops 201326592 | bytes 2359296 | tf_op jit(solution)/shard_map/gradients/gradients/pallas_call | solution.py:235
  (174 shorter events, 7.9 us)
Async XLA Ops:
  3.3 3.7 %collective-permute-start.4 = (f32[2080,128]{1,0:T(8,128)}, f32[2080,128]{1,0:T(8,128)}, u32[]{:S(2)}, u32[]{:S(2)}) collective-permute-start(f32[2080,128]{1,0:T(8,128)} %get-tuple-element.71), channel_id=1, source_target_pairs={{0,2},{1,3},{2,0},{3,1},{4,6},{5,7},{6,4},{7,5},{8,10},{9,11},{10,... | collective-permute-start | bytes 3194888 | tf_op jit(solution)/shard_map/states/ppermute | solution.py:293
  6.5 6.7 %collective-permute-start = (f32[2080,128]{1,0:T(8,128)}, f32[2080,128]{1,0:T(8,128)S(1)}, u32[]{:S(2)}, u32[]{:S(2)}) collective-permute-start(f32[2080,128]{1,0:T(8,128)} %get-tuple-element.60), channel_id=1, source_target_pairs={{0,2},{1,3},{2,0},{3,1},{4,6},{5,7},{6,4},{7,5},{8,10},{9,11},{10,... | collective-permute-start | bytes 3194888 | tf_op jit(solution)/shard_map/states/ppermute | solution.py:293
  8.4 16.3 %collective-permute-start.5 = (f16[1056,128]{1,0:T(8,128)(2,1)S(1)}, f16[1056,128]{1,0:T(8,128)(2,1)S(1)}, u32[]{:S(2)}, u32[]{:S(2)}) collective-permute-start(f16[1056,128]{1,0:T(8,128)(2,1)S(1)} %convert_element_type.350), channel_id=1, source_target_pairs={{0,1},{1,0},{2,3},{3,2},{4,5},{5,4},{6,7},{7,6},{8,9},{9,8},{10,11... | collective-permute-start | bytes 811016 | tf_op jit(solution)/shard_map/up/ppermute | solution.py:293
  11.4 14.3 %collective-permute-start.6 = (f16[1056,128]{1,0:T(8,128)(2,1)S(1)}, f16[1056,128]{1,0:T(8,128)(2,1)S(1)}, u32[]{:S(2)}, u32[]{:S(2)}) collective-permute-start(f16[1056,128]{1,0:T(8,128)(2,1)S(1)} %convert_element_type.351), channel_id=1, source_target_pairs={{0,4},{1,5},{2,6},{3,7},{4,0},{5,1},{6,2},{7,3},{8,12},{9,13},{10,... | collective-permute-start | bytes 811016 | tf_op jit(solution)/shard_map/up/ppermute | solution.py:293
  13.0 13.1 %collective-permute-start.7 = (f16[1056,128]{1,0:T(8,128)(2,1)S(1)}, f16[1056,128]{1,0:T(8,128)(2,1)S(1)}, u32[]{:S(2)}, u32[]{:S(2)}) collective-permute-start(f16[1056,128]{1,0:T(8,128)(2,1)S(1)} %convert_element_type.352), channel_id=1, source_target_pairs={{0,5},{1,4},{2,7},{3,6},{4,1},{5,0},{6,3},{7,2},{8,13},{9,12},{10,... | collective-permute-start | bytes 811016 | tf_op jit(solution)/shard_map/up/ppermute | solution.py:293
  13.3 4.2 %copy-start.2 = (bf16[128,4096]{1,0:T(8,128)(2,1)S(1)}, bf16[128,4096]{1,0:T(8,128)(2,1)}, u32[]{:S(2)}) copy-start(bf16[128,4096]{1,0:T(8,128)(2,1)} %d.15) | copy-start | bytes 3145732
  13.3 4.2 %copy-start.3 = (bf16[128,4096]{1,0:T(8,128)(2,1)S(1)}, bf16[128,4096]{1,0:T(8,128)(2,1)}, u32[]{:S(2)}) copy-start(bf16[128,4096]{1,0:T(8,128)(2,1)} %q.7) | copy-start | bytes 3145732
  13.7 3.7 %copy-start = (bf16[128,4096]{1,0:T(8,128)(2,1)S(1)}, bf16[128,4096]{1,0:T(8,128)(2,1)}, u32[]{:S(2)}) copy-start(bf16[128,4096]{1,0:T(8,128)(2,1)} %k.15) | copy-start | bytes 3145732
  13.7 3.7 %copy-start.1 = (bf16[128,4096]{1,0:T(8,128)(2,1)S(1)}, bf16[128,4096]{1,0:T(8,128)(2,1)}, u32[]{:S(2)}) copy-start(bf16[128,4096]{1,0:T(8,128)(2,1)} %v.15) | copy-start | bytes 3145732
  13.9 28.0 %collective-permute-start.1 = (f16[1056,128]{1,0:T(8,128)(2,1)S(1)}, f16[1056,128]{1,0:T(8,128)(2,1)S(1)}, u32[]{:S(2)}, u32[]{:S(2)}) collective-permute-start(f16[1056,128]{1,0:T(8,128)(2,1)S(1)} %convert_element_type.347), channel_id=1, source_target_pairs={{0,1},{1,0},{2,3},{3,2},{4,5},{5,4},{6,7},{7,6},{8,9},{9,8},{10,11... | collective-permute-start | bytes 811016 | tf_op jit(solution)/shard_map/up/ppermute | solution.py:293
  15.9 26.1 %collective-permute-start.2 = (f16[1056,128]{1,0:T(8,128)(2,1)S(1)}, f16[1056,128]{1,0:T(8,128)(2,1)S(1)}, u32[]{:S(2)}, u32[]{:S(2)}) collective-permute-start(f16[1056,128]{1,0:T(8,128)(2,1)S(1)} %convert_element_type.348), channel_id=1, source_target_pairs={{0,4},{1,5},{2,6},{3,7},{4,0},{5,1},{6,2},{7,3},{8,12},{9,13},{10,... | collective-permute-start | bytes 811016 | tf_op jit(solution)/shard_map/up/ppermute | solution.py:293
  24.7 17.3 %collective-permute-start.3 = (f16[1056,128]{1,0:T(8,128)(2,1)S(1)}, f16[1056,128]{1,0:T(8,128)(2,1)S(1)}, u32[]{:S(2)}, u32[]{:S(2)}) collective-permute-start(f16[1056,128]{1,0:T(8,128)(2,1)S(1)} %convert_element_type.349), channel_id=1, source_target_pairs={{0,5},{1,4},{2,7},{3,6},{4,1},{5,0},{6,3},{7,2},{8,13},{9,12},{10,... | collective-permute-start | bytes 811016 | tf_op jit(solution)/shard_map/up/ppermute | solution.py:293
  26.7 5.2 %collective-permute-start.8 = (f16[528,128]{1,0:T(8,128)(2,1)S(1)}, f16[528,128]{1,0:T(8,128)(2,1)S(1)}, u32[]{:S(2)}, u32[]{:S(2)}) collective-permute-start(f16[528,128]{1,0:T(8,128)(2,1)S(1)} %pad_maximum_fusion.6), channel_id=1, source_target_pairs={{0,8},{1,9},{2,10},{3,11},{4,12},{5,13},{6,14},{7,15},{8,0},{9,1},... | collective-permute-start | bytes 405512 | tf_op jit(solution)/shard_map/outer/ppermute | solution.py:293
  32.2 5.4 %collective-permute-start.9 = (f16[272,128]{1,0:T(8,128)(2,1)S(1)}, f16[272,128]{1,0:T(8,128)(2,1)S(1)}, u32[]{:S(2)}, u32[]{:S(2)}) collective-permute-start(f16[272,128]{1,0:T(8,128)(2,1)S(1)} %pad_maximum_fusion.8), channel_id=1, source_target_pairs={{0,16},{1,17},{2,18},{3,19},{4,20},{5,21},{6,22},{7,23},{8,24},{9,... | collective-permute-start | bytes 208904 | tf_op jit(solution)/shard_map/outer/ppermute | solution.py:293
  38.4 19.6 %collective-permute-start.15 = (f16[1040,128]{1,0:T(8,128)(2,1)S(1)}, f16[1040,128]{1,0:T(8,128)(2,1)S(1)}, u32[]{:S(2)}, u32[]{:S(2)}) collective-permute-start(f16[1040,128]{1,0:T(8,128)(2,1)S(1)} %get-tuple-element.232), channel_id=1, source_target_pairs={{0,1},{1,0},{2,3},{3,2},{4,5},{5,4},{6,7},{7,6},{8,9},{9,8},{10,11... | collective-permute-start | bytes 798728 | tf_op jit(solution)/shard_map/down/ppermute | solution.py:293
  40.4 18.2 %collective-permute-start.16 = (f16[1040,128]{1,0:T(8,128)(2,1)S(1)}, f16[1040,128]{1,0:T(8,128)(2,1)S(1)}, u32[]{:S(2)}, u32[]{:S(2)}) collective-permute-start(f16[1040,128]{1,0:T(8,128)(2,1)S(1)} %get-tuple-element.231), channel_id=1, source_target_pairs={{0,4},{1,5},{2,6},{3,7},{4,0},{5,1},{6,2},{7,3},{8,12},{9,13},{10,... | collective-permute-start | bytes 798728 | tf_op jit(solution)/shard_map/down/ppermute | solution.py:293
  41.8 16.8 %collective-permute-start.17 = (f16[1040,128]{1,0:T(8,128)(2,1)S(1)}, f16[1040,128]{1,0:T(8,128)(2,1)S(1)}, u32[]{:S(2)}, u32[]{:S(2)}) collective-permute-start(f16[1040,128]{1,0:T(8,128)(2,1)S(1)} %get-tuple-element.230), channel_id=1, source_target_pairs={{0,5},{1,4},{2,7},{3,6},{4,1},{5,0},{6,3},{7,2},{8,13},{9,12},{10,... | collective-permute-start | bytes 798728 | tf_op jit(solution)/shard_map/down/ppermute | solution.py:293
  42.6 5.8 %collective-permute-start.10 = (f16[528,128]{1,0:T(8,128)(2,1)S(1)}, f16[528,128]{1,0:T(8,128)(2,1)S(1)}, u32[]{:S(2)}, u32[]{:S(2)}) collective-permute-start(f16[528,128]{1,0:T(8,128)(2,1)S(1)} %pad_maximum_fusion.7), channel_id=1, source_target_pairs={{0,8},{1,9},{2,10},{3,11},{4,12},{5,13},{6,14},{7,15},{8,0},{9,1},... | collective-permute-start | bytes 405512 | tf_op jit(solution)/shard_map/outer/ppermute | solution.py:293
  48.7 5.3 %collective-permute-start.11 = (f16[272,128]{1,0:T(8,128)(2,1)S(1)}, f16[272,128]{1,0:T(8,128)(2,1)S(1)}, u32[]{:S(2)}, u32[]{:S(2)}) collective-permute-start(f16[272,128]{1,0:T(8,128)(2,1)S(1)} %pad_maximum_fusion.9), channel_id=1, source_target_pairs={{0,16},{1,17},{2,18},{3,19},{4,20},{5,21},{6,22},{7,23},{8,24},{9,... | collective-permute-start | bytes 208904 | tf_op jit(solution)/shard_map/outer/ppermute | solution.py:293
  54.9 8.2 %collective-permute-start.12 = (f16[1040,128]{1,0:T(8,128)(2,1)S(1)}, f16[1040,128]{1,0:T(8,128)(2,1)S(1)}, u32[]{:S(2)}, u32[]{:S(2)}) collective-permute-start(f16[1040,128]{1,0:T(8,128)(2,1)S(1)} %get-tuple-element.229), channel_id=1, source_target_pairs={{0,1},{1,0},{2,3},{3,2},{4,5},{5,4},{6,7},{7,6},{8,9},{9,8},{10,11... | collective-permute-start | bytes 798728 | tf_op jit(solution)/shard_map/down/ppermute | solution.py:293
  56.5 6.6 %collective-permute-start.13 = (f16[1040,128]{1,0:T(8,128)(2,1)S(1)}, f16[1040,128]{1,0:T(8,128)(2,1)S(1)}, u32[]{:S(2)}, u32[]{:S(2)}) collective-permute-start(f16[1040,128]{1,0:T(8,128)(2,1)S(1)} %get-tuple-element.228), channel_id=1, source_target_pairs={{0,4},{1,5},{2,6},{3,7},{4,0},{5,1},{6,2},{7,3},{8,12},{9,13},{10,... | collective-permute-start | bytes 798728 | tf_op jit(solution)/shard_map/down/ppermute | solution.py:293
  58.0 7.7 %collective-permute-start.14 = (f16[1040,128]{1,0:T(8,128)(2,1)S(1)}, f16[1040,128]{1,0:T(8,128)(2,1)S(1)}, u32[]{:S(2)}, u32[]{:S(2)}) collective-permute-start(f16[1040,128]{1,0:T(8,128)(2,1)S(1)} %get-tuple-element.227), channel_id=1, source_target_pairs={{0,5},{1,4},{2,7},{3,6},{4,1},{5,0},{6,3},{7,2},{8,13},{9,12},{10,... | collective-permute-start | bytes 798728 | tf_op jit(solution)/shard_map/down/ppermute | solution.py:293
  58.9 2.0 %collective-permute-start.18 = (f16[2112,128]{1,0:T(8,128)(2,1)S(1)}, f16[2112,128]{1,0:T(8,128)(2,1)S(1)}, u32[]{:S(2)}, u32[]{:S(2)}) collective-permute-start(f16[2112,128]{1,0:T(8,128)(2,1)S(1)} %constant_dynamic-update-slice_fusion), channel_id=1, source_target_pairs={{0,2},{1,3},{2,0},{3,1},{4,6},{5,7},{6,4},{7,5},{8,10},{9,11},{10,... | collective-permute-start | bytes 1622024 | tf_op jit(solution)/shard_map/core_return/ppermute | solution.py:293
  66.2 2.0 %collective-permute-start.19 = (f16[2112,128]{1,0:T(8,128)(2,1)S(1)}, f16[2112,128]{1,0:T(8,128)(2,1)S(1)}, u32[]{:S(2)}, u32[]{:S(2)}) collective-permute-start(f16[2112,128]{1,0:T(8,128)(2,1)S(1)} %constant_dynamic-update-slice_fusion.8), channel_id=1, source_target_pairs={{0,2},{1,3},{2,0},{3,1},{4,6},{5,7},{6,4},{7,5},{8,10},{9,11},{10,... | collective-permute-start | bytes 1622024 | tf_op jit(solution)/shard_map/core_return/ppermute | solution.py:293
